TPU v7x, 32 devices: a whole 2x2x4 slice. The times are simulated.
32 devices in a mesh: dp: 8 (over z, x), seq: 4 (over y, core).
Axes of the slice: x: 2, y: 2, z: 4, core: 2. Of those that a mesh axis runs over, the one named last changes fastest.
Arguments:
- stream: bfloat16 [8, 3, 512, 1024], P('dp', None, 'seq'), may hold values from -9 to 9
- encoded: bfloat16 [8, 512, 1024], P('dp', 'seq'), may hold values from -6 to 6
- cotangent: bfloat16 [8, 3, 512, 1024], P('dp', None, 'seq'), may hold values from -6 to 6
- lengths: int32 [8], P('dp'), may hold values from 65 to 512, as said below
- bucket_table: int32 [512], replicated, may hold values from 0 to 31, as said below
- w_query: bfloat16 [1024, 1024], replicated, may hold values from -0.1875 to 0.1875
- w_key: bfloat16 [1024, 1024], replicated, may hold values from -0.1875 to 0.1875
- w_value: bfloat16 [1024, 1024], replicated, may hold values from -0.1875 to 0.1875
- w_out: bfloat16 [1024, 1024], replicated, may hold values from -0.75 to 0.75
- c_query: bfloat16 [1024, 1024], replicated, may hold values from -0.1875 to 0.1875
- c_key: bfloat16 [1024, 1024], replicated, may hold values from -0.1875 to 0.1875
- c_value: bfloat16 [1024, 1024], replicated, may hold values from -0.1875 to 0.1875
- c_out: bfloat16 [1024, 1024], replicated, may hold values from -0.75 to 0.75
- w_in: bfloat16 [1024, 4096], replicated, may hold values from -0.1875 to 0.1875
- w_back: bfloat16 [4096, 1024], replicated, may hold values from -0.09375 to 0.09375
- gain_one: float32 [1024], replicated, may hold values from 0.25 to 1.75
- shift_one: float32 [1024], replicated, may hold values from -1.2 to 1.2
- gain_two: float32 [1024], replicated, may hold values from 0.25 to 1.75
- shift_two: float32 [1024], replicated, may hold values from -1.2 to 1.2
- gain_three: float32 [1024], replicated, may hold values from 0.25 to 1.75
- shift_three: float32 [1024], replicated, may hold values from -1.2 to 1.2
- position_bias: float32 [32, 16], replicated, may hold values from -4 to 4
Outputs:
- layer_output: bfloat16 [8, 3, 512, 1024], P('dp', None, 'seq')
- stream_grad: bfloat16 [8, 3, 512, 1024], P('dp', None, 'seq')
- encoded_grad: bfloat16 [8, 512, 1024], P('dp', 'seq')
- w_query_grad: float32 [1024, 1024], P('dp', 'seq')
- w_key_grad: float32 [1024, 1024], P('dp', 'seq')
- w_value_grad: float32 [1024, 1024], P('dp', 'seq')
- w_out_grad: float32 [1024, 1024], P('dp', 'seq')
- c_query_grad: float32 [1024, 1024], P('dp', 'seq')
- c_key_grad: float32 [1024, 1024], P('dp', 'seq')
- c_value_grad: float32 [1024, 1024], P('dp', 'seq')
- c_out_grad: float32 [1024, 1024], P('dp', 'seq')
- w_in_grad: float32 [1024, 4096], P('dp', 'seq')
- w_back_grad: float32 [4096, 1024], P('dp', 'seq')
- gain_one_grad: float32 [1024], replicated
- shift_one_grad: float32 [1024], replicated
- gain_two_grad: float32 [1024], replicated
- shift_two_grad: float32 [1024], replicated
- gain_three_grad: float32 [1024], replicated
- shift_three_grad: float32 [1024], replicated
- position_bias_grad: float32 [32, 16], replicated
- rms: float32 [4], replicated
Inputs may be any that keep to these rules, and one draw needn't show every extreme that they name: `lengths`: each length lies in the upper half of one of the buckets 512 / 4, 256 and 512. In each aligned block of 1 row one row, drawn from the seed, is longer than 448; one row of all, drawn from the seed, has length 512. `bucket_table`: entry d is the bucket of distance d; it never falls as d grows, and entry 0 is 0.
All inputs are finite; a program needn't handle non-finite values.
Results may differ from a plain program's by a relative error of at most 0.025.
Values may be sent and summed in bfloat16 or wider, within the bound.
A program may use at most 256 MiB of HBM per device.

v0:
```python
import jax
import jax.numpy as jnp
from jax import lax
from jax.sharding import PartitionSpec as P

HEADS = 16
HEAD_DIM = 64
NBUCKET = 32


epsilon = 1e-05
masked_score = -1e30


def layer_norm(values, norm_gain, norm_shift):
    centre = jnp.mean(values, axis=-1, keepdims=True)
    centred = values - centre
    spread = jnp.mean(centred * centred, axis=-1, keepdims=True)
    return centred * lax.rsqrt(spread + epsilon) * norm_gain + norm_shift


def norm_back(values, norm_gain, norm_shift, incoming):
    result, pull_back = jax.vjp(layer_norm, values, norm_gain, norm_shift)
    return pull_back(incoming)


def exact_gelu(values):
    return jax.nn.gelu(values, approximate=False)


def project(left_rows, weight):
    return jnp.dot(left_rows, weight, preferred_element_type=jnp.float32)


def weight_grad(left_rows, right_rows):
    return jnp.einsum("nd,ne->de", left_rows, right_rows, preferred_element_type=jnp.float32)


def back_project(grad_rows, weight):
    return jnp.einsum("ne,de->nd", grad_rows, weight, preferred_element_type=jnp.float32)


def per_device(
    stream,
    encoded,
    cotangent,
    lengths,
    bucket_table,
    w_query,
    w_key,
    w_value,
    w_out,
    c_query,
    c_key,
    c_value,
    c_out,
    w_in,
    w_back,
    gain_one,
    shift_one,
    gain_two,
    shift_two,
    gain_three,
    shift_three,
    position_bias,
):
    num_rows, num_streams, local_len, model_width = stream.shape
    full_len = local_len * lax.axis_size("seq")
    first_pos = lax.axis_index("seq") * local_len
    query_pos = first_pos + jnp.arange(local_len, dtype=jnp.int32)
    key_pos = jnp.arange(full_len, dtype=jnp.int32)
    valid_query = (query_pos[None, :] < lengths[:, None]).astype(jnp.float32)
    valid_key = key_pos[None, :] < lengths[:, None]
    distance = query_pos[:, None] - key_pos[None, :]
    buckets = jnp.take(bucket_table, jnp.clip(distance, 0, full_len - 1))
    bucket_ids = jnp.arange(NBUCKET, dtype=jnp.int32)
    one_hot = (buckets[:, :, None] == bucket_ids).astype(jnp.float32)
    rel_bias = jnp.einsum("tjb,bh->htj", one_hot, position_bias, precision=lax.Precision.HIGHEST)
    own_hot = (bucket_ids == bucket_table[0]).astype(jnp.float32)
    own_bias = jnp.dot(own_hot, position_bias, precision=lax.Precision.HIGHEST)
    stream_ids = jnp.arange(num_streams)
    allowed = jnp.where(stream_ids[:, None, None] == 0, distance[None] >= 0, distance[None] > 0)
    allowed = (allowed[None] & valid_key[:, None, None, :])[:, :, None]
    predicting = (stream_ids > 0)[None, :, None, None]
    cross_allowed = valid_key[:, None, None, None, :]
    head_shape = (num_rows, num_streams, local_len, HEADS, HEAD_DIM)
    flat_rows = stream.reshape(-1, model_width)
    source_rows = encoded.reshape(-1, model_width)
    row_mask = jnp.broadcast_to(
        valid_query[:, None, :], (num_rows, num_streams, local_len)
    ).reshape(-1, 1)

    def heads_of(block):
        return block.reshape(num_rows, full_len, HEADS, HEAD_DIM)

    queries = project(flat_rows, w_query).astype(jnp.bfloat16).reshape(head_shape)
    keys_local = project(flat_rows, w_key).astype(jnp.bfloat16).reshape(head_shape)
    values_local = project(flat_rows, w_value).astype(jnp.bfloat16).reshape(head_shape)
    main_key = keys_local[:, 0].reshape(num_rows, local_len, model_width)
    main_value = values_local[:, 0].reshape(num_rows, local_len, model_width)
    kept_keys, kept_values = (
        lax.all_gather(main_key, "seq", axis=1, tiled=True),
        lax.all_gather(main_value, "seq", axis=1, tiled=True),
    )

    def self_scores(key_block):
        raw_scores = jnp.einsum(
            "rstha,rjha->rshtj", queries, heads_of(key_block), preferred_element_type=jnp.float32
        )
        scores = jnp.where(allowed, raw_scores * 0.125 + rel_bias, masked_score)
        own_raw = jnp.einsum(
            "rstha,rstha->rsht", queries, keys_local, preferred_element_type=jnp.float32
        )
        own_score = jnp.where(
            predicting, own_raw * 0.125 + own_bias[None, None, :, None], masked_score
        )
        return (scores, own_score)

    scores, own_score = self_scores(kept_keys)
    row_top = jnp.maximum(jnp.max(scores, axis=-1), own_score)
    expo_main = jnp.exp(scores - row_top[..., None])
    expo_own = jnp.exp(own_score - row_top)
    row_total = jnp.sum(expo_main, axis=-1) + expo_own
    self_lse = row_top + jnp.log(row_total)
    probs_main = (expo_main / row_total[..., None]).astype(jnp.bfloat16)
    probs_own = expo_own / row_total
    own_weight = jnp.transpose(probs_own, (0, 1, 3, 2))[..., None]
    context = jnp.einsum(
        "rshtj,rjha->rstha", probs_main, heads_of(kept_values), preferred_element_type=jnp.float32
    )
    context = context + own_weight * values_local.astype(jnp.float32)
    context_low = context.astype(jnp.bfloat16).reshape(-1, model_width)
    attended = project(context_low, w_out)
    resid_one = flat_rows.astype(jnp.float32) + attended
    first_norm = layer_norm(resid_one, gain_one, shift_one).astype(jnp.bfloat16)
    cross_queries = project(first_norm, c_query).astype(jnp.bfloat16).reshape(head_shape)
    cross_key_local = (
        project(source_rows, c_key).astype(jnp.bfloat16).reshape(num_rows, local_len, model_width)
    )
    cross_value_local = (
        project(source_rows, c_value).astype(jnp.bfloat16).reshape(num_rows, local_len, model_width)
    )
    kept_cross_keys, kept_cross_values = (
        lax.all_gather(cross_key_local, "seq", axis=1, tiled=True),
        lax.all_gather(cross_value_local, "seq", axis=1, tiled=True),
    )

    def cross_scores(key_block):
        raw_scores = jnp.einsum(
            "rstha,rjha->rshtj",
            cross_queries,
            heads_of(key_block),
            preferred_element_type=jnp.float32,
        )
        return jnp.where(cross_allowed, raw_scores * 0.125, masked_score)

    cross_raw = cross_scores(kept_cross_keys)
    cross_top = jnp.max(cross_raw, axis=-1, keepdims=True)
    cross_expo = jnp.exp(cross_raw - cross_top)
    cross_total = jnp.sum(cross_expo, axis=-1, keepdims=True)
    cross_lse = cross_top + jnp.log(cross_total)
    cross_probs = (cross_expo / cross_total).astype(jnp.bfloat16)
    cross_context = jnp.einsum(
        "rshtj,rjha->rstha",
        cross_probs,
        heads_of(kept_cross_values),
        preferred_element_type=jnp.float32,
    )
    cross_low = cross_context.astype(jnp.bfloat16).reshape(-1, model_width)
    crossed = project(cross_low, c_out)
    resid_two = first_norm.astype(jnp.float32) + crossed
    second_norm = layer_norm(resid_two, gain_two, shift_two).astype(jnp.bfloat16)
    ffn_inner = project(second_norm, w_in)
    activated = exact_gelu(ffn_inner).astype(jnp.bfloat16)
    ffn_out = project(activated, w_back)
    resid_three = second_norm.astype(jnp.float32) + ffn_out
    layer_output = (layer_norm(resid_three, gain_three, shift_three) * row_mask).astype(
        jnp.bfloat16
    )
    input_wide = flat_rows.astype(jnp.float32)
    totals = lax.psum(
        (
            jnp.sum(input_wide * input_wide * row_mask),
            jnp.sum(attended * attended * row_mask),
            jnp.sum(crossed * crossed * row_mask),
            jnp.sum(ffn_out * ffn_out * row_mask),
            jnp.sum(row_mask),
        ),
        ("dp", "seq"),
    )
    rms = jnp.sqrt(
        jnp.stack([totals[0], totals[1], totals[2], totals[3]]) / (totals[4] * model_width)
    )
    key_block, value_block = (kept_keys, kept_values)
    cross_key_block, cross_value_block = (kept_cross_keys, kept_cross_values)
    d_output = cotangent.reshape(-1, model_width).astype(jnp.float32) * row_mask
    d_resid_three, d_gain_three, d_shift_three = norm_back(
        resid_three, gain_three, shift_three, d_output
    )
    d_ffn_out = d_resid_three.astype(jnp.bfloat16)
    g_back = weight_grad(activated, d_ffn_out)
    gelu_value, gelu_pull = jax.vjp(exact_gelu, ffn_inner)
    d_inner = gelu_pull(back_project(d_ffn_out, w_back))[0].astype(jnp.bfloat16)
    g_in = weight_grad(second_norm, d_inner)
    d_second = d_resid_three + back_project(d_inner, w_in)
    d_resid_two, d_gain_two, d_shift_two = norm_back(resid_two, gain_two, shift_two, d_second)
    d_crossed = d_resid_two.astype(jnp.bfloat16)
    g_cout = weight_grad(cross_low, d_crossed)
    d_cross_ctx = back_project(d_crossed, c_out).astype(jnp.bfloat16).reshape(head_shape)
    cross_back = jnp.exp(cross_scores(cross_key_block) - cross_lse)
    d_cross_probs = jnp.einsum(
        "rstha,rjha->rshtj",
        d_cross_ctx,
        heads_of(cross_value_block),
        preferred_element_type=jnp.float32,
    )
    cross_delta = jnp.sum(cross_back * d_cross_probs, axis=-1, keepdims=True)
    d_cross_scores = (cross_back * (d_cross_probs - cross_delta)).astype(jnp.bfloat16)
    d_cross_query = (
        (
            jnp.einsum(
                "rshtj,rjha->rstha",
                d_cross_scores,
                heads_of(cross_key_block),
                preferred_element_type=jnp.float32,
            )
            * 0.125
        )
        .astype(jnp.bfloat16)
        .reshape(-1, model_width)
    )
    cross_key_part = (
        jnp.einsum(
            "rshtj,rstha->rjha", d_cross_scores, cross_queries, preferred_element_type=jnp.float32
        )
        * 0.125
    ).reshape(num_rows, full_len, model_width)
    cross_value_part = jnp.einsum(
        "rshtj,rstha->rjha", cross_probs, d_cross_ctx, preferred_element_type=jnp.float32
    ).reshape(num_rows, full_len, model_width)
    d_cross_key, d_cross_value = (
        lax.psum_scatter(
            cross_key_part.astype(jnp.bfloat16), "seq", scatter_dimension=1, tiled=True
        ).astype(jnp.float32),
        lax.psum_scatter(
            cross_value_part.astype(jnp.bfloat16), "seq", scatter_dimension=1, tiled=True
        ).astype(jnp.float32),
    )
    d_cross_key = d_cross_key.astype(jnp.bfloat16).reshape(-1, model_width)
    d_cross_value = d_cross_value.astype(jnp.bfloat16).reshape(-1, model_width)
    g_ckey = weight_grad(source_rows, d_cross_key)
    g_cvalue = weight_grad(source_rows, d_cross_value)
    encoded_grad = (
        (back_project(d_cross_key, c_key) + back_project(d_cross_value, c_value))
        .astype(jnp.bfloat16)
        .reshape(encoded.shape)
    )
    g_cquery = weight_grad(first_norm, d_cross_query)
    d_first = d_resid_two + back_project(d_cross_query, c_query)
    d_resid_one, d_gain_one, d_shift_one = norm_back(resid_one, gain_one, shift_one, d_first)
    d_attended = d_resid_one.astype(jnp.bfloat16)
    g_out = weight_grad(context_low, d_attended)
    d_context = back_project(d_attended, w_out).astype(jnp.bfloat16).reshape(head_shape)
    scores_back, own_back = self_scores(key_block)
    p_main = jnp.exp(scores_back - self_lse[..., None])
    p_own = jnp.exp(own_back - self_lse)
    d_probs = jnp.einsum(
        "rstha,rjha->rshtj", d_context, heads_of(value_block), preferred_element_type=jnp.float32
    )
    d_probs_own = jnp.einsum(
        "rstha,rstha->rsht", d_context, values_local, preferred_element_type=jnp.float32
    )
    row_delta = jnp.sum(p_main * d_probs, axis=-1) + p_own * d_probs_own
    d_scores = (p_main * (d_probs - row_delta[..., None])).astype(jnp.bfloat16)
    d_own = (p_own * (d_probs_own - row_delta)).astype(jnp.bfloat16)
    own_grad = jnp.transpose(d_own, (0, 1, 3, 2))[..., None].astype(jnp.float32) * 0.125
    d_queries = jnp.einsum(
        "rshtj,rjha->rstha", d_scores, heads_of(key_block), preferred_element_type=jnp.float32
    ) * 0.125 + own_grad * keys_local.astype(jnp.float32)
    key_part = (
        jnp.einsum("rshtj,rstha->rjha", d_scores, queries, preferred_element_type=jnp.float32)
        * 0.125
    ).reshape(num_rows, full_len, model_width)
    value_part = jnp.einsum(
        "rshtj,rstha->rjha", probs_main, d_context, preferred_element_type=jnp.float32
    ).reshape(num_rows, full_len, model_width)
    d_main_key, d_main_value = (
        lax.psum_scatter(
            key_part.astype(jnp.bfloat16), "seq", scatter_dimension=1, tiled=True
        ).astype(jnp.float32),
        lax.psum_scatter(
            value_part.astype(jnp.bfloat16), "seq", scatter_dimension=1, tiled=True
        ).astype(jnp.float32),
    )
    stream_shape = (num_rows, num_streams, local_len, model_width)
    own_key_grad = (own_grad * queries.astype(jnp.float32)).reshape(stream_shape)
    own_value_grad = (
        jnp.transpose(p_own, (0, 1, 3, 2))[..., None] * d_context.astype(jnp.float32)
    ).reshape(stream_shape)
    d_keys = (
        jnp.concatenate([d_main_key[:, None], own_key_grad[:, 1:]], axis=1)
        .astype(jnp.bfloat16)
        .reshape(-1, model_width)
    )
    d_values = (
        jnp.concatenate([d_main_value[:, None], own_value_grad[:, 1:]], axis=1)
        .astype(jnp.bfloat16)
        .reshape(-1, model_width)
    )
    d_query_low = d_queries.astype(jnp.bfloat16).reshape(-1, model_width)
    g_query = weight_grad(flat_rows, d_query_low)
    g_key = weight_grad(flat_rows, d_keys)
    g_value = weight_grad(flat_rows, d_values)
    stream_grad = (
        (
            d_resid_one
            + back_project(d_query_low, w_query)
            + back_project(d_keys, w_key)
            + back_project(d_values, w_value)
        )
        .astype(jnp.bfloat16)
        .reshape(stream.shape)
    )
    score_sum = jnp.sum(d_scores.astype(jnp.float32), axis=(0, 1))
    table_part = jnp.einsum("htj,tjb->bh", score_sum, one_hot, precision=lax.Precision.HIGHEST)
    table_part = (
        table_part + own_hot[:, None] * jnp.sum(d_own.astype(jnp.float32), axis=(0, 1, 3))[None, :]
    )
    small_sums = lax.psum(
        (table_part, d_gain_one, d_shift_one, d_gain_two, d_shift_two, d_gain_three, d_shift_three),
        ("dp", "seq"),
    )
    row_parts = (
        lax.psum_scatter(g_query, "dp", scatter_dimension=0, tiled=True),
        lax.psum_scatter(g_key, "dp", scatter_dimension=0, tiled=True),
        lax.psum_scatter(g_value, "dp", scatter_dimension=0, tiled=True),
        lax.psum_scatter(g_out, "dp", scatter_dimension=0, tiled=True),
        lax.psum_scatter(g_cquery, "dp", scatter_dimension=0, tiled=True),
        lax.psum_scatter(g_ckey, "dp", scatter_dimension=0, tiled=True),
        lax.psum_scatter(g_cvalue, "dp", scatter_dimension=0, tiled=True),
        lax.psum_scatter(g_cout, "dp", scatter_dimension=0, tiled=True),
        lax.psum_scatter(g_in, "dp", scatter_dimension=0, tiled=True),
        lax.psum_scatter(g_back, "dp", scatter_dimension=0, tiled=True),
    )
    shares = (
        lax.psum_scatter(
            row_parts[0].astype(jnp.bfloat16), "seq", scatter_dimension=1, tiled=True
        ).astype(jnp.float32),
        lax.psum_scatter(
            row_parts[1].astype(jnp.bfloat16), "seq", scatter_dimension=1, tiled=True
        ).astype(jnp.float32),
        lax.psum_scatter(
            row_parts[2].astype(jnp.bfloat16), "seq", scatter_dimension=1, tiled=True
        ).astype(jnp.float32),
        lax.psum_scatter(
            row_parts[3].astype(jnp.bfloat16), "seq", scatter_dimension=1, tiled=True
        ).astype(jnp.float32),
        lax.psum_scatter(
            row_parts[4].astype(jnp.bfloat16), "seq", scatter_dimension=1, tiled=True
        ).astype(jnp.float32),
        lax.psum_scatter(
            row_parts[5].astype(jnp.bfloat16), "seq", scatter_dimension=1, tiled=True
        ).astype(jnp.float32),
        lax.psum_scatter(
            row_parts[6].astype(jnp.bfloat16), "seq", scatter_dimension=1, tiled=True
        ).astype(jnp.float32),
        lax.psum_scatter(
            row_parts[7].astype(jnp.bfloat16), "seq", scatter_dimension=1, tiled=True
        ).astype(jnp.float32),
        lax.psum_scatter(
            row_parts[8].astype(jnp.bfloat16), "seq", scatter_dimension=1, tiled=True
        ).astype(jnp.float32),
        lax.psum_scatter(
            row_parts[9].astype(jnp.bfloat16), "seq", scatter_dimension=1, tiled=True
        ).astype(jnp.float32),
    )
    return (
        layer_output.reshape(stream.shape),
        stream_grad,
        encoded_grad,
        shares[0],
        shares[1],
        shares[2],
        shares[3],
        shares[4],
        shares[5],
        shares[6],
        shares[7],
        shares[8],
        shares[9],
        small_sums[1],
        small_sums[2],
        small_sums[3],
        small_sums[4],
        small_sums[5],
        small_sums[6],
        small_sums[0],
        rms,
    )


def solution(mesh):
    placed = (
        P("dp", None, "seq", None),
        P("dp", "seq", None),
        P("dp", None, "seq", None),
        P("dp"),
        P(),
        P(),
        P(),
        P(),
        P(),
        P(),
        P(),
        P(),
        P(),
        P(),
        P(),
        P(),
        P(),
        P(),
        P(),
        P(),
        P(),
        P(),
    )
    return jax.shard_map(
        per_device,
        mesh=mesh,
        in_specs=placed,
        out_specs=(
            P("dp", None, "seq", None),
            P("dp", None, "seq", None),
            P("dp", "seq", None),
            P("dp", "seq"),
            P("dp", "seq"),
            P("dp", "seq"),
            P("dp", "seq"),
            P("dp", "seq"),
            P("dp", "seq"),
            P("dp", "seq"),
            P("dp", "seq"),
            P("dp", "seq"),
            P("dp", "seq"),
            P(),
            P(),
            P(),
            P(),
            P(),
            P(),
            P(),
            P(),
        ),
        check_vma=False,
    )
```

profile of v0, /device:TPU:0, one launch (start us, length us, event | category | flops | bytes accessed | tf_op | source)
XLA Modules:
  0.0 2303.7 jit_solution(15259104879285489548)
XLA Ops:
  38.8 408.2 %gather_fusion = s32[65536]{0:T(1024)S(1)} fusion(s32[512]{0:T(512)S(1)} %copy-done.2, s32[65536]{0:T(1024)S(1)} %broadcast_clamp_fusion), kind=kCustom, calls=%fused_computation | custom fusion | bytes 786432 | tf_op jit(solution)/shard_map/jit(_take)/gather | solution.py:75
  458.6 37.3 %copy.182 = pred[128,512,32]{1,2,0:T(32,128)(4,1)S(1)} copy(pred[128,512,32]{0,2,1:T(32,128)(4,1)S(1)} %iota_compare_fusion) | data formatting | bytes 4194304 | tf_op jit(solution)/shard_map/eq | solution.py:77
  496.6 3.8 convolution_bitcast_fusion.5
  500.4 5.3 copy.183
  507.9 4.8 fusion.143
  517.3 4.1 divide_convert_fusion.1
  521.4 4.4 fusion.43
  539.5 4.4 bitcast_reduce_fusion
  550.8 8.3 fusion.53
  561.7 20.6 multiply_convert_fusion
  591.9 14.1 add_convert_fusion
  606.0 7.6 multiply_reduce_fusion.6
  621.6 9.4 bitcast_convert_fusion
  631.0 4.7 copy.260
  637.2 9.0 fusion.4
  646.2 7.5 fusion.12
  658.2 4.0 copy.258
  665.4 4.3 multiply_reduce_fusion.7
  675.7 5.1 bitcast_convert_fusion.1
  680.8 4.0 copy.256
  687.9 8.7 fusion.1
  697.8 12.7 convert_reduce_fusion
  716.6 4.7 fusion.72
  732.6 4.2 fusion.42
  769.5 10.2 fusion.144
  781.2 10.2 fusion.131
  791.5 52.5 %reduce-scatter.61.cloned.1.call-done = f32[128,1024]{1,0:T(8,128)} async-done(((f32[1024,1024]{1,0:T(8,128)}), f32[128,1024]{1,0:T(8,128)}) %reduce-scatter.61.cloned.1.call-update) | async-done | bytes 524304 | tf_op jit(solution)/shard_map/reduce_scatter | solution.py:341
  845.9 89.9 %reduce-scatter.49.cloned.1.call-done = f32[128,1024]{1,0:T(8,128)} async-done(((f32[1024,1024]{1,0:T(8,128)}), f32[128,1024]{1,0:T(8,128)}) %reduce-scatter.49.cloned.1.call-update) | async-done | bytes 524304 | tf_op jit(solution)/shard_map/reduce_scatter | solution.py:338
  937.7 89.7 %reduce-scatter.45.cloned.1.call-done = f32[128,1024]{1,0:T(8,128)} async-done(((f32[1024,1024]{1,0:T(8,128)}), f32[128,1024]{1,0:T(8,128)}) %reduce-scatter.45.cloned.1.call-update) | async-done | bytes 524304 | tf_op jit(solution)/shard_map/reduce_scatter | solution.py:337
  1029.2 90.3 %reduce-scatter.33.cloned.1.call-done = f32[128,1024]{0,1:T(8,128)} async-done(((f32[1024,1024]{0,1:T(8,128)}), f32[128,1024]{0,1:T(8,128)}) %reduce-scatter.33.cloned.1.call-update) | async-done | bytes 524304 | tf_op jit(solution)/shard_map/reduce_scatter | solution.py:334
  1121.3 90.0 %reduce-scatter.57.cloned.1.call-done = f32[128,1024]{0,1:T(8,128)} async-done(((f32[1024,1024]{0,1:T(8,128)}), f32[128,1024]{0,1:T(8,128)}) %reduce-scatter.57.cloned.1.call-update) | async-done | bytes 524304 | tf_op jit(solution)/shard_map/reduce_scatter | solution.py:340
  1213.2 90.3 %reduce-scatter.53.cloned.1.call-done = f32[128,1024]{0,1:T(8,128)} async-done(((f32[1024,1024]{0,1:T(8,128)}), f32[128,1024]{0,1:T(8,128)}) %reduce-scatter.53.cloned.1.call-update) | async-done | bytes 524304 | tf_op jit(solution)/shard_map/reduce_scatter | solution.py:339
  1305.4 89.9 %reduce-scatter.41.cloned.1.call-done = f32[128,1024]{0,1:T(8,128)} async-done(((f32[1024,1024]{0,1:T(8,128)}), f32[128,1024]{0,1:T(8,128)}) %reduce-scatter.41.cloned.1.call-update) | async-done | bytes 524304 | tf_op jit(solution)/shard_map/reduce_scatter | solution.py:336
  1397.1 90.2 %reduce-scatter.37.cloned.1.call-done = f32[128,1024]{0,1:T(8,128)} async-done(((f32[1024,1024]{0,1:T(8,128)}), f32[128,1024]{0,1:T(8,128)}) %reduce-scatter.37.cloned.1.call-update) | async-done | bytes 524304 | tf_op jit(solution)/shard_map/reduce_scatter | solution.py:335
  1489.1 284.3 %reduce-scatter.65.cloned.1.call-done = f32[128,4096]{1,0:T(8,128)} async-done(((f32[1024,4096]{1,0:T(8,128)}), f32[128,4096]{1,0:T(8,128)}) %reduce-scatter.65.cloned.1.call-update) | async-done | bytes 2097168 | tf_op jit(solution)/shard_map/reduce_scatter | solution.py:342
  1778.0 7.8 fusion.61
  1785.8 44.8 %all-reduce = (f32[1024]{0:T(1024)}, f32[1024]{0:T(1024)}, f32[1024]{0:T(1024)}, f32[1024]{0:T(1024)}, f32[1024]{0:T(1024)}, /*index=5*/f32[1024]{0:T(1024)}, f3...) all-reduce(f32[1024]{0:T(1024)S(1)} %get-tuple-element.107, ...), channel_id=1, replica_groups=mesh['dp'=8,'seq'=4] {'dp','seq'}, use_global_device_ids=true, to_apply=%region_43.44 | all-reduce | flops 6661 | bytes 53288 | tf_op jit(solution)/shard_map/psum | solution.py:329
  1831.3 229.0 %reduce-scatter.69.cloned.1.call-done = f32[512,1024]{1,0:T(8,128)} async-done(((f32[4096,1024]{1,0:T(8,128)}), f32[512,1024]{1,0:T(8,128)}) %reduce-scatter.69.cloned.1.call-update) | async-done | bytes 2097168 | tf_op jit(solution)/shard_map/reduce_scatter | solution.py:343
  2066.3 3.9 fusion.67
  2084.4 20.0 reduce-scatter.51.cloned.1.call-done
  2105.9 21.0 reduce-scatter.47.cloned.1.call-done
  2128.4 21.1 reduce-scatter.35.cloned.1.call-done
  2151.2 20.9 reduce-scatter.59.cloned.1.call-done
  2173.7 20.9 reduce-scatter.55.cloned.1.call-done
  2196.2 20.9 reduce-scatter.43.cloned.1.call-done
  2218.7 20.9 reduce-scatter.39.cloned.1.call-done
  2241.3 25.7 %reduce-scatter.67.cloned.1.call-done = bf16[128,1024]{1,0:T(8,128)(2,1)} async-done(((bf16[128,4096]{1,0:T(8,128)(2,1)}), bf16[128,1024]{1,0:T(8,128)(2,1)}) %reduce-scatter.67.cloned.1.call-update) | async-done | bytes 262160 | tf_op jit(solution)/shard_map/reduce_scatter | solution.py:370
  2268.7 25.8 %reduce-scatter.71.cloned.1.call-done = bf16[512,256]{1,0:T(8,128)(2,1)} async-done(((bf16[512,1024]{1,0:T(8,128)(2,1)}), bf16[512,256]{1,0:T(8,128)(2,1)}) %reduce-scatter.71.cloned.1.call-update) | async-done | bytes 262160 | tf_op jit(solution)/shard_map/reduce_scatter | solution.py:373
  (410 shorter events, 214.3 us)
Async XLA Ops:
  7.2 552.6 %copy-start = (bf16[1024,1024]{1,0:T(8,128)(2,1)S(1)}, bf16[1024,1024]{1,0:T(8,128)(2,1)}, u32[]{:S(2)}) copy-start(bf16[1024,1024]{1,0:T(8,128)(2,1)} %param.34) | copy-start | bytes 6291460
  7.2 500.7 %all-gather.9.cloned.1.call-start = ((), (), s32[]{:S(2)}) async-start(), calls=%async_computation.25 | async-start | bytes 1310720 | tf_op jit(solution)/shard_map/all_gather | solution.py:102
  14.9 506.5 %all-gather.7.cloned.1.call-start = ((), (), s32[]{:S(2)}) async-start(), calls=%async_computation.24 | async-start | bytes 1310720 | tf_op jit(solution)/shard_map/all_gather | solution.py:103
  24.6 512.9 %all-gather.13.cloned.1.call-start = ((), (), s32[]{:S(2)}) async-start(), calls=%async_computation.47 | async-start | bytes 1310720 | tf_op jit(solution)/shard_map/all_gather | solution.py:144
  27.6 520.9 %all-gather.11.cloned.1.call-start = ((), (), s32[]{:S(2)}) async-start(), calls=%async_computation.46 | async-start | bytes 1310720 | tf_op jit(solution)/shard_map/all_gather | solution.py:145
  30.5 710.9 %reduce-scatter.79.cloned.1.call-start = ((), (), s32[]{:S(2)}) async-start(), calls=%async_computation.51 | async-start | bytes 1310720
  30.7 486.5 %copy-start.87 = (pred[3]{0:T(512)(128)(4,1)}, pred[3]{0:T(512)(128)(4,1)S(1)}, u32[]{:S(2)}) copy-start(pred[3]{0:T(512)(128)(4,1)S(1)} %iota_compare_fusion.2) | copy-start | bytes 13
  38.8 410.3 %copy-start.26 = (bf16[1,3,128,1024]{3,2,1,0:T(8,128)(2,1)S(1)}, bf16[1,3,128,1024]{3,2,1,0:T(8,128)(2,1)}, u32[]{:S(2)}) copy-start(bf16[1,3,128,1024]{3,2,1,0:T(8,128)(2,1)} %param.22) | copy-start | bytes 2359300
  449.1 8.3 copy-start.54
  457.4 50.5 %copy-start.13 = (bf16[3,128,16,64]{1,0,3,2:T(4,128)(2,1)}, bf16[3,128,16,64]{1,0,3,2:T(4,128)(2,1)S(1)}, u32[]{:S(2)}) copy-start(bf16[3,128,16,64]{1,0,3,2:T(4,128)(2,1)S(1)} %reshape.805) | copy-start | bytes 2359300
  458.6 37.3 %copy-start.75 = (f32[32,16]{0,1:T(8,128)S(1)}, f32[32,16]{0,1:T(8,128)}, u32[]{:S(2)}) copy-start(f32[32,16]{0,1:T(8,128)} %param.43) | copy-start | bytes 6148
  496.6 20.6 copy-start.85
  507.7 9.6 copy-start.66
  560.2 22.1 slice-start
  561.3 52.3 %copy-start.6 = (f32[384,1024]{1,0:T(8,128)}, f32[384,1024]{1,0:T(8,128)S(1)}, u32[]{:S(2)}) copy-start(f32[384,1024]{1,0:T(8,128)S(1)} %get-tuple-element.150) | copy-start | bytes 4718596
  561.7 20.7 slice-start.1
  591.9 14.1 copy-start.36
  637.2 108.6 %reduce-scatter.77.cloned.1.call-start = ((), (), s32[]{:S(2)}) async-start(), calls=%async_computation.50 | async-start | bytes 1310720
  656.0 9.3 copy-start.52
  669.7 84.5 %reduce-scatter.75.cloned.1.call-start = ((), (), s32[]{:S(2)}) async-start(), calls=%async_computation.49 | async-start | bytes 1310720
  687.9 8.9 copy-start.49
  696.7 66.5 %reduce-scatter.73.cloned.1.call-start = ((), (), s32[]{:S(2)}) async-start(), calls=%async_computation.48 | async-start | bytes 1310720
  697.8 12.7 copy-start.14
  716.5 127.5 %reduce-scatter.61.cloned.1.call-start = ((), (), s32[]{:S(2)}) async-start(), calls=%async_computation.40 | async-start | bytes 4718592 | tf_op jit(solution)/shard_map/reduce_scatter | solution.py:341
  721.3 214.5 %reduce-scatter.49.cloned.1.call-start = ((), (), s32[]{:S(2)}) async-start(), calls=%async_computation.34 | async-start | bytes 4718592 | tf_op jit(solution)/shard_map/reduce_scatter | solution.py:338
  726.1 301.3 %reduce-scatter.45.cloned.1.call-start = ((), (), s32[]{:S(2)}) async-start(), calls=%async_computation.32 | async-start | bytes 4718592 | tf_op jit(solution)/shard_map/reduce_scatter | solution.py:337
  731.1 388.4 %reduce-scatter.33.cloned.1.call-start = ((), (), s32[]{:S(2)}) async-start(), calls=%async_computation.26 | async-start | bytes 4718592 | tf_op jit(solution)/shard_map/reduce_scatter | solution.py:334
  741.3 470.1 %reduce-scatter.57.cloned.1.call-start = ((), (), s32[]{:S(2)}) async-start(), calls=%async_computation.38 | async-start | bytes 4718592 | tf_op jit(solution)/shard_map/reduce_scatter | solution.py:340
  745.7 557.8 %reduce-scatter.53.cloned.1.call-start = ((), (), s32[]{:S(2)}) async-start(), calls=%async_computation.36 | async-start | bytes 4718592 | tf_op jit(solution)/shard_map/reduce_scatter | solution.py:339
  750.2 645.1 %reduce-scatter.41.cloned.1.call-start = ((), (), s32[]{:S(2)}) async-start(), calls=%async_computation.30 | async-start | bytes 4718592 | tf_op jit(solution)/shard_map/reduce_scatter | solution.py:336
  759.2 728.0 %reduce-scatter.37.cloned.1.call-start = ((), (), s32[]{:S(2)}) async-start(), calls=%async_computation.28 | async-start | bytes 4718592 | tf_op jit(solution)/shard_map/reduce_scatter | solution.py:335
  768.1 1005.3 %reduce-scatter.65.cloned.1.call-start = ((), (), s32[]{:S(2)}) async-start(), calls=%async_computation.42 | async-start | bytes 18874368 | tf_op jit(solution)/shard_map/reduce_scatter | solution.py:342
  779.8 1280.5 %reduce-scatter.69.cloned.1.call-start = ((), (), s32[]{:S(2)}) async-start(), calls=%async_computation.44 | async-start | bytes 18874368 | tf_op jit(solution)/shard_map/reduce_scatter | solution.py:343
  791.5 1291.4 %reduce-scatter.63.cloned.1.call-start = ((), (), s32[]{:S(2)}) async-start(), calls=%async_computation.41 | async-start | bytes 327680 | tf_op jit(solution)/shard_map/reduce_scatter | solution.py:367
  845.8 1258.6 %reduce-scatter.51.cloned.1.call-start = ((), (), s32[]{:S(2)}) async-start(), calls=%async_computation.35 | async-start | bytes 327680 | tf_op jit(solution)/shard_map/reduce_scatter | solution.py:358
  937.6 1189.3 %reduce-scatter.47.cloned.1.call-start = ((), (), s32[]{:S(2)}) async-start(), calls=%async_computation.33 | async-start | bytes 327680 | tf_op jit(solution)/shard_map/reduce_scatter | solution.py:355
  1029.1 1120.4 %reduce-scatter.35.cloned.1.call-start = ((), (), s32[]{:S(2)}) async-start(), calls=%async_computation.27 | async-start | bytes 327680 | tf_op jit(solution)/shard_map/reduce_scatter | solution.py:346
  1121.3 1050.8 %reduce-scatter.59.cloned.1.call-start = ((), (), s32[]{:S(2)}) async-start(), calls=%async_computation.39 | async-start | bytes 327680 | tf_op jit(solution)/shard_map/reduce_scatter | solution.py:364
  1213.2 981.4 %reduce-scatter.55.cloned.1.call-start = ((), (), s32[]{:S(2)}) async-start(), calls=%async_computation.37 | async-start | bytes 327680 | tf_op jit(solution)/shard_map/reduce_scatter | solution.py:361
  1305.3 911.8 %reduce-scatter.43.cloned.1.call-start = ((), (), s32[]{:S(2)}) async-start(), calls=%async_computation.31 | async-start | bytes 327680 | tf_op jit(solution)/shard_map/reduce_scatter | solution.py:352
  1397.0 842.6 %reduce-scatter.39.cloned.1.call-start = ((), (), s32[]{:S(2)}) async-start(), calls=%async_computation.29 | async-start | bytes 327680 | tf_op jit(solution)/shard_map/reduce_scatter | solution.py:349
  1489.1 287.8 %copy-start.30 = (bf16[1,3,128,1024]{3,2,1,0:T(8,128)(2,1)S(1)}, bf16[1,3,128,1024]{3,2,1,0:T(8,128)(2,1)}, u32[]{:S(2)}) copy-start(bf16[1,3,128,1024]{3,2,1,0:T(8,128)(2,1)} %param.24) | copy-start | bytes 2359300
  1489.1 287.8 %copy-start.92 = (f32[128]{0:T(128)S(1)}, f32[128]{0:T(128)}, u32[]{:S(2)}) copy-start(f32[128]{0:T(128)} %copy-done.91) | copy-start | bytes 1540
  1489.1 777.9 %reduce-scatter.67.cloned.1.call-start = ((), (), s32[]{:S(2)}) async-start(), calls=%async_computation.43 | async-start | bytes 1310720 | tf_op jit(solution)/shard_map/reduce_scatter | solution.py:370
  1776.1 518.4 %reduce-scatter.71.cloned.1.call-start = ((), (), s32[]{:S(2)}) async-start(), calls=%async_computation.45 | async-start | bytes 1310720 | tf_op jit(solution)/shard_map/reduce_scatter | solution.py:373
  1778.0 7.8 copy-start.81
  1831.3 235.0 %copy-start.43 = (bf16[1,3,128,16,64]{2,1,4,3,0:T(4,128)(2,1)S(1)}, bf16[1,3,128,16,64]{2,1,4,3,0:T(4,128)(2,1)}, u32[]{:S(2)}) copy-start(bf16[1,3,128,16,64]{2,1,4,3,0:T(4,128)(2,1)} %copy-done.42) | copy-start | bytes 2359300
  2080.9 215.5 %copy-start.1 = (bf16[1024,1024]{1,0:T(8,128)(2,1)S(1)}, bf16[1024,1024]{1,0:T(8,128)(2,1)}, u32[]{:S(2)}) copy-start(bf16[1024,1024]{1,0:T(8,128)(2,1)} %param.34) | copy-start | bytes 6291460
  (78 other events, 202.9 us)
Sparse Core Ops, SparseCore 0:
  15.1 19.5 all-gather.8
  36.8 16.8 all-gather.6
  55.2 16.7 all-gather.12
  73.4 16.7 all-gather.10
  637.3 27.5 reduce-scatter.78
  669.8 27.3 reduce-scatter.76
  699.7 24.8 reduce-scatter.74
  727.3 24.8 reduce-scatter.72
  755.9 88.1 reduce-scatter.60
  848.0 87.7 reduce-scatter.48
  939.4 87.8 reduce-scatter.44
  1031.2 88.1 reduce-scatter.32
  1123.1 88.2 reduce-scatter.56
  1215.3 88.2 reduce-scatter.52
  1307.0 88.2 reduce-scatter.40
  1399.2 88.0 reduce-scatter.36
  1490.9 282.4 reduce-scatter.64
  1777.5 282.7 reduce-scatter.68
  2062.8 19.1 reduce-scatter.62
  2084.4 19.9 reduce-scatter.50
  2106.9 20.0 reduce-scatter.46
  2129.5 20.0 reduce-scatter.34
  2152.0 20.0 reduce-scatter.58
  2174.6 19.9 reduce-scatter.54
  2197.1 20.0 reduce-scatter.42
  2219.6 20.0 reduce-scatter.38
  2242.0 24.8 reduce-scatter.66
  2269.6 24.8 reduce-scatter.70
where the time goes:
time: 2310 us; the launch traced here: 2300 us
  waiting for transfers between devices  1390 us (60%)
  local copies, waits for them, and re-layouts  556 us (24%)
  matrix products  207 us (9%)
  other arithmetic  81.9 us (4%)
  blocking collectives  44.8 us (2%)
    gather x2, local copies, waits for them, and re-layouts, per_device(): buckets = jnp.take(bucket_table, jnp.clip(distance, 0, full_len - 1))  408 us
    reduce_scatter x1, waiting for transfers between devices, per_device(): lax.psum_scatter(g_in, 'dp', scatter_dimension=0, tiled=True)  284 us
    reduce_scatter x1, waiting for transfers between devices, per_device(): lax.psum_scatter(g_back, 'dp', scatter_dimension=0, tiled=True)  229 us
    reduce_scatter x1, waiting for transfers between devices, per_device(): lax.psum_scatter(g_ckey, 'dp', scatter_dimension=0, tiled=True)  90.3 us
    reduce_scatter x1, waiting for transfers between devices, per_device(): lax.psum_scatter(g_query, 'dp', scatter_dimension=0, tiled=True)  90.3 us
    reduce_scatter x1, waiting for transfers between devices, per_device(): lax.psum_scatter(g_key, 'dp', scatter_dimension=0, tiled=True)  90.2 us
    reduce_scatter x1, waiting for transfers between devices, per_device(): lax.psum_scatter(g_cvalue, 'dp', scatter_dimension=0, tiled=True)  90 us
    reduce_scatter x1, waiting for transfers between devices, per_device(): lax.psum_scatter(g_cquery, 'dp', scatter_dimension=0, tiled=True)  89.9 us
  transfers between devices with their start and end apart: 28, of which 19 were waited for; matrix products, arithmetic and copies ran while one was open for 32% of the time, Pallas kernels for 0%

commit v1 on v0

--- a/solution.py
+++ b/solution.py
@@ -72,7 +72,13 @@
     valid_query = (query_pos[None, :] < lengths[:, None]).astype(jnp.float32)
     valid_key = key_pos[None, :] < lengths[:, None]
     distance = query_pos[:, None] - key_pos[None, :]
-    buckets = jnp.take(bucket_table, jnp.clip(distance, 0, full_len - 1))
+    starts = jnp.sum(
+        (bucket_table[:, None] < jnp.arange(1, NBUCKET, dtype=jnp.int32)[None, :]).astype(jnp.int32),
+        axis=0,
+    )
+    buckets = jnp.zeros_like(distance)
+    for step in range(NBUCKET - 1):
+        buckets = buckets + (distance >= starts[step]).astype(jnp.int32)
     bucket_ids = jnp.arange(NBUCKET, dtype=jnp.int32)
     one_hot = (buckets[:, :, None] == bucket_ids).astype(jnp.float32)
     rel_bias = jnp.einsum("tjb,bh->htj", one_hot, position_bias, precision=lax.Precision.HIGHEST)
@@ -330,50 +336,16 @@
         (table_part, d_gain_one, d_shift_one, d_gain_two, d_shift_two, d_gain_three, d_shift_three),
         ("dp", "seq"),
     )
-    row_parts = (
-        lax.psum_scatter(g_query, "dp", scatter_dimension=0, tiled=True),
-        lax.psum_scatter(g_key, "dp", scatter_dimension=0, tiled=True),
-        lax.psum_scatter(g_value, "dp", scatter_dimension=0, tiled=True),
-        lax.psum_scatter(g_out, "dp", scatter_dimension=0, tiled=True),
-        lax.psum_scatter(g_cquery, "dp", scatter_dimension=0, tiled=True),
-        lax.psum_scatter(g_ckey, "dp", scatter_dimension=0, tiled=True),
-        lax.psum_scatter(g_cvalue, "dp", scatter_dimension=0, tiled=True),
-        lax.psum_scatter(g_cout, "dp", scatter_dimension=0, tiled=True),
-        lax.psum_scatter(g_in, "dp", scatter_dimension=0, tiled=True),
-        lax.psum_scatter(g_back, "dp", scatter_dimension=0, tiled=True),
-    )
-    shares = (
-        lax.psum_scatter(
-            row_parts[0].astype(jnp.bfloat16), "seq", scatter_dimension=1, tiled=True
-        ).astype(jnp.float32),
-        lax.psum_scatter(
-            row_parts[1].astype(jnp.bfloat16), "seq", scatter_dimension=1, tiled=True
-        ).astype(jnp.float32),
-        lax.psum_scatter(
-            row_parts[2].astype(jnp.bfloat16), "seq", scatter_dimension=1, tiled=True
-        ).astype(jnp.float32),
-        lax.psum_scatter(
-            row_parts[3].astype(jnp.bfloat16), "seq", scatter_dimension=1, tiled=True
-        ).astype(jnp.float32),
-        lax.psum_scatter(
-            row_parts[4].astype(jnp.bfloat16), "seq", scatter_dimension=1, tiled=True
-        ).astype(jnp.float32),
-        lax.psum_scatter(
-            row_parts[5].astype(jnp.bfloat16), "seq", scatter_dimension=1, tiled=True
-        ).astype(jnp.float32),
-        lax.psum_scatter(
-            row_parts[6].astype(jnp.bfloat16), "seq", scatter_dimension=1, tiled=True
-        ).astype(jnp.float32),
-        lax.psum_scatter(
-            row_parts[7].astype(jnp.bfloat16), "seq", scatter_dimension=1, tiled=True
-        ).astype(jnp.float32),
-        lax.psum_scatter(
-            row_parts[8].astype(jnp.bfloat16), "seq", scatter_dimension=1, tiled=True
-        ).astype(jnp.float32),
-        lax.psum_scatter(
-            row_parts[9].astype(jnp.bfloat16), "seq", scatter_dimension=1, tiled=True
-        ).astype(jnp.float32),
-    )
+    def share_of(grads, rows_dim):
+        low = grads.astype(jnp.bfloat16)
+        low = lax.psum_scatter(low, "seq", scatter_dimension=rows_dim + 1, tiled=True)
+        low = lax.psum_scatter(low, "dp", scatter_dimension=rows_dim, tiled=True)
+        return low.astype(jnp.float32)
+
+    square = share_of(
+        jnp.stack([g_query, g_key, g_value, g_out, g_cquery, g_ckey, g_cvalue, g_cout]), 1
+    )
+    shares = tuple(square[i] for i in range(8)) + (share_of(g_in, 0), share_of(g_back, 0))
     return (
         layer_output.reshape(stream.shape),
         stream_grad,

time: 2310 us -> 894 us (0.39)
  waiting for transfers between devices: 1390 us -> 394 us
  local copies, waits for them, and re-layouts: 556 us -> 158 us
    reduce_scatter x20 -> x5, waiting for transfers between devices: 1390 us -> 304 us  [the longest x3 249 us: share_of(): lax.psum_scatter(low, 'seq', scatter_dimension=rows_dim + 1, tiled=True)]
    gather x2 -> x0, local copies, waits for them, and re-layouts: 408 us -> none  [per_device(): buckets = jnp.take(bucket_table, jnp.clip(distance, 0, full_len - 1))]
    unnamed x32 -> x19, waiting for transfers between devices: 0.54 us -> 89.5 us
    convert_element_type x15 -> x3, other arithmetic: 27.8 us -> 3.64 us  [share_of(): return low.astype(jnp.float32)]
    unnamed x222 -> x214, local copies, waits for them, and re-layouts: 65.2 us -> 75.3 us
  transfers between devices with their start and end apart: 28 -> 14, of which waited for: 19 -> 5; matrix products, arithmetic and copies ran while one was open for 32% -> 36% of each run, Pallas kernels for 0% -> 0%
where the time goes in v1:
time: 894 us; the launch traced here: 888 us
  waiting for transfers between devices  394 us (44%)
  matrix products  198 us (22%)
  local copies, waits for them, and re-layouts  158 us (18%)
  other arithmetic  79.4 us (9%)
  blocking collectives  41.4 us (5%)
  between operations  16.8 us (2%)
    reduce_scatter x3, waiting for transfers between devices, share_of(): lax.psum_scatter(low, 'seq', scatter_dimension=rows_dim + 1, tiled=True)  249 us
    unnamed x19, waiting for transfers between devices  89.5 us
    unnamed x214, local copies, waits for them, and re-layouts  75.3 us
    reduce_scatter x2, waiting for transfers between devices, share_of(): low = lax.psum_scatter(low, 'dp', scatter_dimension=rows_dim, tiled=True)  54.8 us
    dot_general x10, matrix products, project(): return jnp.dot(left_rows, weight, preferred_element_type=jnp.float32)  44 us
    psum x1, blocking collectives, per_device(): lax.psum((table_part, d_gain_one, d_shift_one, d_gain_two, d_shift_two, d...  41.4 us
    dot_general x10, matrix products, back_project(): jnp.einsum('ne,de->nd', grad_rows, weight, preferred_element_type=jnp.flo...  40.2 us
    dot_general x10, matrix products, weight_grad(): jnp.einsum('nd,ne->de', left_rows, right_rows, preferred_element_type=jnp...  38.2 us
  transfers between devices with their start and end apart: 14, of which 5 were waited for; matrix products, arithmetic and copies ran while one was open for 36% of the time, Pallas kernels for 0%

profile of v1, /device:TPU:0, one launch (start us, length us, event | category | flops | bytes accessed | tf_op | source)
XLA Modules:
  0.0 887.7 jit_solution(17295676532620560727)
XLA Ops:
  7.3 2.9 convolution_convert_fusion.6
  15.0 3.7 convolution_convert_fusion.7
  24.7 2.9 convolution_convert_fusion.8
  33.0 3.2 reshape.861
  38.8 2.8 convolution_convert_fusion.5
  46.2 20.5 %convert_add_fusion.3 = s32[128,512]{0,1:T(8,128)S(1)} fusion(s32[]{:T(128)} %bitcast.44, s32[]{:T(128)} %bitcast.43, s32[]{:T(128)} %bitcast.42, s32[]{:T(128)} %bitcast.41, s32[]{:T(128)} %bitcast.40, s32[]{:T(128)} %bitcast.39, s32[]{:T(128)} %bitcast.38, s32[]{:T(128)} %bitcast.37, s32[]{:T(128)} %bitcast.36, s32[]{:T(128)} %bitcast.35, s32[]{:T(128)} %bitcast.34, ...), kind=kLoop, calls=%fused_computation.190 | loop fusion | flops 6094848 | bytes 262780 | tf_op jit(solution)/shard_map/add | solution.py:81
  68.6 37.3 %copy.191 = pred[128,512,32]{1,2,0:T(32,128)(4,1)S(1)} copy(pred[128,512,32]{0,2,1:T(32,128)(4,1)S(1)} %iota_compare_fusion) | data formatting | bytes 4194304 | tf_op jit(solution)/shard_map/eq | solution.py:83
  106.6 3.7 convolution_bitcast_fusion
  110.4 5.3 copy.192
  117.8 5.2 fusion.167
  123.1 2.9 fusion.9
  127.6 4.2 divide_convert_fusion.1
  131.8 4.4 fusion.43
  149.5 4.4 bitcast_reduce_fusion
  153.9 3.2 fusion.10
  160.7 8.3 fusion.53
  171.6 20.9 %multiply_convert_fusion = (bf16[384,4096]{1,0:T(8,128)(2,1)S(1)}, f32[384,4096]{1,0:T(8,128)}, f32[384,4096]{1,0:T(8,128)}) fusion(bf16[1024,4096]{1,0:T(8,128)(2,1)} %param.35, f32[384,1024]{1,0:T(8,128)S(1)} %get-tuple-element.150, f32[1024]{0:T(1024)S(1)} %copy-done.87, f32[1024]{0:T(1024)S(1)} %copy-done.81, f32[384]{0:T(512)S(1)} %fusion.145, ...), kind=kOutput, calls=%fused_computation.44 | convolution fusion | flops 3325427712 | bytes 25701376 | tf_op jit(solution)/shard_map/dot_general | solution.py:32
  192.6 3.7 fusion.161
  202.1 14.1 %add_convert_fusion = bf16[384,4096]{1,0:T(8,128)(2,1)} fusion(f32[384,4096]{1,0:T(8,128)} %get-tuple-element.148, f32[384,4096]{1,0:T(8,128)} %get-tuple-element.204, bf16[4096,1024]{1,0:T(8,128)(2,1)} %param.36, f32[384,1024]{1,0:T(8,128)} %get-tuple-element.144, f32[384]{0:T(512)S(1)} %negate_multiply_fusion.3), kind=kOutput, calls=%fused_computation.43 | convolution fusion | flops 3244032000 | bytes 25691648 | tf_op jit(solution)/shard_map/ne,de->nd/dot_general | solution.py:40
  216.2 7.5 multiply_reduce_fusion.6
  231.8 9.4 %bitcast_convert_fusion.2 = bf16[16,64,512]{2,1,0:T(8,128)(2,1)} fusion(bf16[3,128,16,64]{1,3,0,2:T(8,128)(2,1)} %copy.204, f32[16,512,3,128]{3,1,2,0:T(8,128)} %copy-done.3, f32[3,16,128]{2,0,1:T(4,128)S(1)} %fusion.10, f32[3,16,128]{2,0,1:T(4,128)S(1)} %get-tuple-element.201, pred[512]{0:T(512)(128)(4,1)S(1)} %iota_compare_fusion.1), kind=kOutput, calls=%fused_computation.74 | convolution fusion | flops 418906112 | bytes 14467584 | tf_op jit(solution)/shard_map/rshtj,rstha->rjha/dot_general | solution.py:244
  241.2 4.7 copy.278
  247.4 8.6 fusion.4
  256.0 7.5 fusion.12
  268.0 4.0 copy.276
  272.0 3.1 copy.363
  275.2 4.3 multiply_reduce_fusion.7
  284.7 4.9 bitcast_convert_fusion.3
  289.5 4.0 copy.274
  293.6 3.1 copy.364
  296.6 8.7 fusion.1
  307.7 12.7 %convert_reduce_fusion = (f32[16,128,512]{1,2,0:T(8,128)}, bf16[1,3,16,128,512]{3,4,1,2,0:T(8,128)(2,1)S(1)}) fusion(f32[3,16,128]{2,0,1:T(4,128)S(1)} %get-tuple-element.162, f32[16,512,3,128]{3,1,2,0:T(8,128)} %get-tuple-element.211, f32[1,3,16,128,512]{3,4,1,2,0:T(8,128)} %copy-done.2, f32[3,16,128]{2,0,1:T(4,128)S(1)} %copy-done.62), kind=kLoop, calls=%fused_computation.18 | loop fusion | flops 17825792 | bytes 35700736 | tf_op jit(solution)/shard_map/reduce_sum | solution.py:330
  323.1 3.9 copy.272
  327.0 3.1 copy.365
  330.2 8.9 %convolution_convert_fusion.1 = bf16[1024,4096]{1,0:T(8,128)(2,1)} fusion(bf16[384,4096]{1,0:T(8,128)(2,1)} %add_convert_fusion, f32[384,1024]{1,0:T(8,128)S(1)} %copy-done.8, f32[1024]{0:T(1024)S(1)} %copy-done.87, f32[1024]{0:T(1024)S(1)} %copy-done.81, f32[384]{0:T(512)S(1)} %fusion.145, f32[384]{0:T(512)S(1)} %broadcast_multiply_fusion.1), kind=kOutput, calls=%fused_computation.28 | convolution fusion | flops 3227385856 | bytes 13118464 | tf_op jit(solution)/shard_map/nd,ne->de/dot_general | solution.py:36
  340.5 9.4 %convolution_convert_fusion = bf16[4096,1024]{1,0:T(8,128)(2,1)} fusion(bf16[384,4096]{1,0:T(8,128)(2,1)} %copy-done.88, f32[384,1024]{1,0:T(8,128)S(1)} %copy-done.52, f32[384]{0:T(512)S(1)} %negate_multiply_fusion.3), kind=kOutput, calls=%fused_computation.27 | convolution fusion | flops 3226206208 | bytes 13108736 | tf_op jit(solution)/shard_map/nd,ne->de/dot_general | solution.py:36
  355.2 3.9 fusion.42
  390.0 46.4 %reduce-scatter.23.cloned.1.call-done = bf16[1024,1024]{1,0:T(8,128)(2,1)} async-done(((bf16[1024,4096]{1,0:T(8,128)(2,1)}), bf16[1024,1024]{1,0:T(8,128)(2,1)}) %reduce-scatter.23.cloned.1.call-update) | async-done | bytes 2097168 | tf_op jit(solution)/shard_map/reduce_scatter | solution.py:341
  436.4 74.3 %reduce-scatter.27.cloned.1.call-done = bf16[4096,256]{1,0:T(8,128)(2,1)} async-done(((bf16[4096,1024]{1,0:T(8,128)(2,1)}), bf16[4096,256]{1,0:T(8,128)(2,1)}) %reduce-scatter.27.cloned.1.call-update) | async-done | bytes 2097168 | tf_op jit(solution)/shard_map/reduce_scatter | solution.py:341
  510.8 128.7 %reduce-scatter.21.cloned.1.call-done = bf16[8,1024,256]{1,2,0:T(8,128)(2,1)} async-done(((bf16[8,1024,1024]{1,2,0:T(8,128)(2,1)}), bf16[8,1024,256]{1,2,0:T(8,128)(2,1)}) %reduce-scatter.21.cloned.1.call-update) | async-done | bytes 4194320 | tf_op jit(solution)/shard_map/reduce_scatter | solution.py:341
  639.5 7.2 copy.280
  646.7 5.6 copy.298
  654.5 7.8 fusion.61
  662.4 41.4 %all-reduce = (f32[1024]{0:T(1024)}, f32[1024]{0:T(1024)}, f32[1024]{0:T(1024)}, f32[1024]{0:T(1024)}, f32[1024]{0:T(1024)}, /*index=5*/f32[1024]{0:T(1024)}, f3...) all-reduce(f32[1024]{0:T(1024)S(1)} %get-tuple-element.107, ...), channel_id=1, replica_groups=mesh['dp'=8,'seq'=4] {'dp','seq'}, use_global_device_ids=true, to_apply=%region_30.31 | all-reduce | flops 6661 | bytes 53288 | tf_op jit(solution)/shard_map/psum | solution.py:335
  704.5 3.2 fusion.149
  707.7 4.2 fusion.67
  727.3 54.8 %reduce-scatter.29.cloned.1.call-done = bf16[512,256]{1,0:T(8,128)(2,1)} async-done(((bf16[4096,256]{1,0:T(8,128)(2,1)}), bf16[512,256]{1,0:T(8,128)(2,1)}) %reduce-scatter.29.cloned.1.call-update) | async-done | bytes 262160 | tf_op jit(solution)/shard_map/reduce_scatter | solution.py:342
  783.9 89.2 %reduce-scatter.39.cloned.1.call-done = bf16[128,2048]{1,0:T(8,128)(2,1)} async-done(((bf16[1024,2048]{1,0:T(8,128)(2,1)}), bf16[128,2048]{1,0:T(8,128)(2,1)}) %reduce-scatter.39.cloned.1.call-update) | async-done | bytes 524304
  (346 shorter events, 142.8 us)
Async XLA Ops:
  7.2 162.5 %copy-start = (bf16[1024,1024]{1,0:T(8,128)(2,1)S(1)}, bf16[1024,1024]{1,0:T(8,128)(2,1)}, u32[]{:S(2)}) copy-start(bf16[1024,1024]{1,0:T(8,128)(2,1)} %param.34) | copy-start | bytes 6291460
  7.2 110.6 %all-gather.9.cloned.1.call-start = ((), (), s32[]{:S(2)}) async-start(), calls=%async_computation.11 | async-start | bytes 1310720 | tf_op jit(solution)/shard_map/all_gather | solution.py:108
  13.8 4.9 copy-start.11
  14.9 116.8 %all-gather.7.cloned.1.call-start = ((), (), s32[]{:S(2)}) async-start(), calls=%async_computation.10 | async-start | bytes 1310720 | tf_op jit(solution)/shard_map/all_gather | solution.py:109
  21.0 3.7 copy-start.28
  23.4 4.1 copy-start.13
  24.6 123.2 %all-gather.13.cloned.1.call-start = ((), (), s32[]{:S(2)}) async-start(), calls=%async_computation.18 | async-start | bytes 1310720 | tf_op jit(solution)/shard_map/all_gather | solution.py:150
  27.6 8.7 copy-start.18
  27.6 130.8 %all-gather.11.cloned.1.call-start = ((), (), s32[]{:S(2)}) async-start(), calls=%async_computation.17 | async-start | bytes 1310720 | tf_op jit(solution)/shard_map/all_gather | solution.py:151
  30.5 334.5 %reduce-scatter.37.cloned.1.call-start = ((), (), s32[]{:S(2)}) async-start(), calls=%async_computation.22 | async-start | bytes 1310720
  30.9 96.6 %copy-start.77 = (pred[3]{0:T(512)(128)(4,1)}, pred[3]{0:T(512)(128)(4,1)S(1)}, u32[]{:S(2)}) copy-start(pred[3]{0:T(512)(128)(4,1)S(1)} %iota_compare_fusion.2) | copy-start | bytes 13
  46.2 71.6 %copy-start.9 = (bf16[3,128,16,64]{1,0,3,2:T(4,128)(2,1)}, bf16[3,128,16,64]{1,0,3,2:T(4,128)(2,1)S(1)}, u32[]{:S(2)}) copy-start(bf16[3,128,16,64]{1,0,3,2:T(4,128)(2,1)S(1)} %reshape.844) | copy-start | bytes 2359300
  68.6 37.3 %copy-start.66 = (f32[32,16]{0,1:T(8,128)S(1)}, f32[32,16]{0,1:T(8,128)}, u32[]{:S(2)}) copy-start(f32[32,16]{0,1:T(8,128)} %param.43) | copy-start | bytes 6148
  106.6 20.8 %copy-start.75 = (f32[16]{0:T(128)}, f32[16]{0:T(128)S(1)}, u32[]{:S(2)}) copy-start(f32[16]{0:T(128)S(1)} %convolution_bitcast_fusion.1) | copy-start | bytes 196
  117.6 9.9 %copy-start.59 = (f32[3,16,128]{2,0,1:T(4,128)}, f32[3,16,128]{2,0,1:T(4,128)S(1)}, u32[]{:S(2)}) copy-start(f32[3,16,128]{2,0,1:T(4,128)S(1)} %fusion.35) | copy-start | bytes 73732
  123.0 4.6 copy-start.2
  127.6 4.2 copy-start.14
  131.8 5.1 copy-start.45
  153.9 4.5 copy-start.3
  170.2 22.4 %slice-start = ((s8[8388608]{0:T(1024)(128)(4,1)}), s8[4194304]{0:T(1024)(128)(4,1)S(1)}, s32[]{:S(2)}) async-start(s8[8388608]{0:T(1024)(128)(4,1)} %bitcast.557), calls=%async_computation.24 | async-start | bytes 8388608
  171.3 52.5 %copy-start.7 = (f32[384,1024]{1,0:T(8,128)}, f32[384,1024]{1,0:T(8,128)S(1)}, u32[]{:S(2)}) copy-start(f32[384,1024]{1,0:T(8,128)S(1)} %get-tuple-element.150) | copy-start | bytes 4718596
  171.6 20.9 %slice-start.1 = ((s8[8388608]{0:T(1024)(128)(4,1)}), s8[4194304]{0:T(1024)(128)(4,1)S(1)}, s32[]{:S(2)}) async-start(s8[8388608]{0:T(1024)(128)(4,1)} %bitcast.557), calls=%async_computation.25 | async-start | bytes 8388608
  192.5 3.7 copy-start.88
  192.6 4.0 copy-start.25
  192.6 4.0 copy-start.72
  202.1 14.1 %copy-start.51 = (f32[384,1024]{1,0:T(8,128)S(1)}, f32[384,1024]{1,0:T(8,128)}, u32[]{:S(2)}) copy-start(f32[384,1024]{1,0:T(8,128)} %get-tuple-element.144) | copy-start | bytes 4718596
  247.4 119.5 %reduce-scatter.35.cloned.1.call-start = ((), (), s32[]{:S(2)}) async-start(), calls=%async_computation.21 | async-start | bytes 1310720
  265.8 9.3 %copy-start.53 = (bf16[1,3,128,16,64]{2,1,4,3,0:T(4,128)(2,1)}, bf16[1,3,128,16,64]{2,1,4,3,0:T(4,128)(2,1)S(1)}, u32[]{:S(2)}) copy-start(bf16[1,3,128,16,64]{2,1,4,3,0:T(4,128)(2,1)S(1)} %copy.206) | copy-start | bytes 2359300
  268.0 7.1 copy-start.68
  268.0 7.1 copy-start.74
  275.2 4.3 copy-start.70
  279.5 89.1 %reduce-scatter.33.cloned.1.call-start = ((), (), s32[]{:S(2)}) async-start(), calls=%async_computation.20 | async-start | bytes 1310720
  305.4 65.5 %reduce-scatter.31.cloned.1.call-start = ((), (), s32[]{:S(2)}) async-start(), calls=%async_computation.19 | async-start | bytes 1310720
  307.7 12.7 %copy-start.10 = (bf16[3,128,16,64]{1,0,3,2:T(4,128)(2,1)S(1)}, bf16[3,128,16,64]{1,0,3,2:T(4,128)(2,1)}, u32[]{:S(2)}) copy-start(bf16[3,128,16,64]{1,0,3,2:T(4,128)(2,1)} %copy-done.9) | copy-start | bytes 2359300
  330.1 106.2 %reduce-scatter.23.cloned.1.call-start = ((), (), s32[]{:S(2)}) async-start(), calls=%async_computation.13 | async-start | bytes 10485760 | tf_op jit(solution)/shard_map/reduce_scatter | solution.py:341
  339.1 171.6 %reduce-scatter.27.cloned.1.call-start = ((), (), s32[]{:S(2)}) async-start(), calls=%async_computation.15 | async-start | bytes 10485760 | tf_op jit(solution)/shard_map/reduce_scatter | solution.py:341
  350.0 289.5 %reduce-scatter.21.cloned.1.call-start = ((), (), s32[]{:S(2)}) async-start(), calls=%async_computation.12 | async-start | bytes 20971520 | tf_op jit(solution)/shard_map/reduce_scatter | solution.py:341
  368.1 4.5 copy-start.43
  383.2 4.1 copy-start.34
  383.2 4.1 copy-start.50
  389.9 335.6 %reduce-scatter.25.cloned.1.call-start = ((), (), s32[]{:S(2)}) async-start(), calls=%async_computation.14 | async-start | bytes 2359296 | tf_op jit(solution)/shard_map/reduce_scatter | solution.py:342
  436.4 345.7 %reduce-scatter.29.cloned.1.call-start = ((), (), s32[]{:S(2)}) async-start(), calls=%async_computation.16 | async-start | bytes 2359296 | tf_op jit(solution)/shard_map/reduce_scatter | solution.py:342
  510.7 362.4 %reduce-scatter.39.cloned.1.call-start = ((), (), s32[]{:S(2)}) async-start(), calls=%async_computation.23 | async-start | bytes 4718592
  654.5 7.9 copy-start.71
  707.7 4.2 copy-start.57
  714.8 5.0 copy-start.17
  717.2 4.1 copy-start.86
  874.7 6.2 copy-start.1
  (57 other events, 114.8 us)
Sparse Core Ops, SparseCore 0:
  15.1 19.5 all-gather.8
  36.8 16.9 all-gather.6
  55.4 16.7 all-gather.12
  74.1 16.7 all-gather.10
  247.5 27.4 reduce-scatter.36
  279.6 27.3 reduce-scatter.34
  309.5 24.8 reduce-scatter.32
  337.1 24.8 reduce-scatter.30
  364.6 71.6 reduce-scatter.22
  439.0 71.6 reduce-scatter.26
  513.3 126.1 reduce-scatter.20
  643.3 68.4 reduce-scatter.24
  715.7 66.3 reduce-scatter.28
  786.0 87.0 reduce-scatter.38

commit v2 on v1

--- a/solution.py
+++ b/solution.py
@@ -1,11 +1,17 @@
+import functools
+
 import jax
 import jax.numpy as jnp
 from jax import lax
+from jax.experimental import pallas as pl
+from jax.experimental.pallas import tpu as pltpu
 from jax.sharding import PartitionSpec as P
 
 HEADS = 16
 HEAD_DIM = 64
 NBUCKET = 32
+COLS = 256
+SLOTS = 4
 
 
 epsilon = 1e-05
@@ -38,6 +44,297 @@
 
 def back_project(grad_rows, weight):
     return jnp.einsum("ne,de->nd", grad_rows, weight, preferred_element_type=jnp.float32)
+
+
+MESH_ID = pl.DeviceIdType.MESH
+
+
+def tile_dot(x_ref, x_start, y_ref, y_start, rows):
+    left = x_ref[:, pl.ds(x_start, rows)]
+    right = y_ref[:, pl.ds(y_start, COLS)]
+    return lax.dot_general(
+        left, right, (((0,), (0,)), ((), ())), preferred_element_type=jnp.float32
+    )
+
+
+def reduce_kernel(units, num_in, num_out, dp_size, *refs):
+    ins, small_ref = refs[:num_in], refs[num_in]
+    outs, small_out = refs[num_in + 1 : num_in + 1 + num_out], refs[num_in + 1 + num_out]
+    sent, core_in, first_y, first_x, second, third, small_in = refs[num_in + num_out + 2 : -10]
+    sems = refs[-10:]
+    core_s, core_r, one_s, one_r, two_s, two_r, three_s, three_r, small_s, small_r = sems
+    dp, sq = lax.axis_index("dp"), lax.axis_index("seq")
+    core, ypos = sq % 2, sq // 2
+    xpos, zpos = dp % 2, dp // 2
+    depth = dp_size // 2
+    chunk = 1024 // dp_size
+    core_peer = (dp, sq + 1 - 2 * core)
+    y_peer = (dp, sq + 2 - 4 * ypos)
+    x_peer = (dp + 1 - 2 * xpos, sq)
+
+    def z_peer(step):
+        return ((zpos + step) % depth * 2 + xpos, sq)
+
+    barrier = pltpu.get_barrier_semaphore()
+    for peer in [core_peer, y_peer, x_peer] + [z_peer(step) for step in range(1, depth)]:
+        pl.semaphore_signal(barrier, inc=1, device_id=peer, device_id_type=MESH_ID)
+    pl.semaphore_wait(barrier, 2 + depth)
+
+    def remote(src, dst, send_sem, recv_sem, peer):
+        return pltpu.make_async_remote_copy(
+            src_ref=src,
+            dst_ref=dst,
+            send_sem=send_sem,
+            recv_sem=recv_sem,
+            device_id=peer,
+            device_id_type=MESH_ID,
+        )
+
+    def half_dots(unit, half, write):
+        x_id, y_id, kind, part = units[unit]
+        x_ref, y_ref = ins[x_id], ins[y_id]
+        rows = chunk if kind == "back" else 256
+
+        def body(step, carry):
+            tile, side = step // 2, step % 2
+            block = side * 2 + half
+            x_start = tile * 256
+            y_start = block * COLS
+            if kind == "in":
+                y_start = block * 1024 + part * COLS
+            if kind == "back":
+                x_start = tile * (4 * chunk) + part * chunk
+            write(
+                side,
+                pl.ds(pl.multiple_of(tile * rows, rows), rows),
+                tile_dot(
+                    x_ref,
+                    pl.multiple_of(x_start, 128),
+                    y_ref,
+                    pl.multiple_of(y_start, COLS),
+                    rows,
+                ),
+            )
+            return carry
+
+        lax.fori_loop(0, 2 * (1024 // rows), body, 0)
+
+    def core_copy(unit):
+        return remote(
+            sent.at[unit % SLOTS], core_in.at[unit], core_s.at[unit], core_r.at[unit], core_peer
+        )
+
+    def one_copy(unit):
+        half = unit // 2
+        if unit % 2 == 0:
+            return remote(
+                core_in.at[unit, 1 - ypos], first_y.at[half], one_s.at[unit], one_r.at[unit], y_peer
+            )
+        source = core_in.at[unit].reshape(2, depth, 2, chunk, COLS)
+        return remote(
+            source.at[:, :, 1 - xpos], first_x.at[half], one_s.at[unit], one_r.at[unit], x_peer
+        )
+
+    def two_copy(unit):
+        half = unit // 2
+        if unit % 2 == 0:
+            source = first_y.at[half].reshape(depth, 2, chunk, COLS)
+            return remote(
+                source.at[:, 1 - xpos], second.at[unit], two_s.at[unit], two_r.at[unit], x_peer
+            )
+        return remote(
+            first_x.at[half, 1 - ypos], second.at[unit], two_s.at[unit], two_r.at[unit], y_peer
+        )
+
+    def three_copy(unit, step):
+        return remote(
+            second.at[unit, (zpos + step) % depth],
+            third.at[unit, step - 1],
+            three_s.at[unit, step - 1],
+            three_r.at[unit, step - 1],
+            z_peer(step),
+        )
+
+    def products(unit):
+        slot = unit % SLOTS
+        if unit >= SLOTS:
+            core_copy(unit - SLOTS).wait_send()
+
+        def write(side, rows, value):
+            sent[slot, side, rows, :] = value.astype(jnp.bfloat16)
+
+        half_dots(unit, 1 - core, write)
+        core_copy(unit).start()
+
+    def core_sum(unit):
+        core_copy(unit).wait_recv()
+
+        def write(side, rows, value):
+            old = core_in[unit, side, rows, :].astype(jnp.float32)
+            core_in[unit, side, rows, :] = (value + old).astype(jnp.bfloat16)
+
+        half_dots(unit, core, write)
+        one_copy(unit).start()
+
+    def plus(left, right):
+        return (left.astype(jnp.float32) + right.astype(jnp.float32)).astype(jnp.bfloat16)
+
+    def one_sum(unit):
+        one_copy(unit).wait_recv()
+        half = unit // 2
+        if unit % 2 == 0:
+
+            def body(step, carry):
+                rows = pl.ds(pl.multiple_of(step * 128, 128), 128)
+                first_y[half, rows, :] = plus(first_y[half, rows, :], core_in[unit, ypos, rows, :])
+                return carry
+
+            lax.fori_loop(0, 8, body, 0)
+        else:
+            def body(step, carry):
+                side, layer = step // depth, step % depth
+                rows = pl.ds(pl.multiple_of((layer * 2 + xpos) * chunk, chunk), chunk)
+                first_x[half, side, layer] = plus(
+                    first_x[half, side, layer], core_in[unit, side, rows, :]
+                )
+                return carry
+
+            lax.fori_loop(0, 2 * depth, body, 0)
+        two_copy(unit).start()
+
+    def two_sum(unit):
+        two_copy(unit).wait_recv()
+        half = unit // 2
+
+        def body(layer, carry):
+            if unit % 2 == 0:
+                rows = pl.ds(pl.multiple_of((layer * 2 + xpos) * chunk, chunk), chunk)
+                old = first_y[half, rows, :]
+            else:
+                old = first_x[half, ypos, layer]
+            second[unit, layer] = plus(second[unit, layer], old)
+            return carry
+
+        lax.fori_loop(0, depth, body, 0)
+
+        def send(step, carry):
+            three_copy(unit, step).start()
+            return carry
+
+        lax.fori_loop(1, depth, send, 0)
+
+    def last_sum(unit):
+        def body(step, total):
+            three_copy(unit, step).wait_recv()
+            return total + third[unit, step - 1].astype(jnp.float32)
+
+        total = lax.fori_loop(1, depth, body, second[unit, zpos].astype(jnp.float32))
+        x_id, y_id, kind, part = units[unit]
+        if kind == "in":
+            outs[8][:, part * COLS : (part + 1) * COLS] = total
+        elif kind in ("back", "parted"):
+            outs[9][part * chunk : (part + 1) * chunk, :] = total
+        else:
+            outs[part][...] = total
+
+    bits = 0
+    while (1 << bits) < dp_size:
+        bits += 1
+    small_out[...] = small_ref[...]
+
+    def small_copy(step):
+        if step == 0:
+            peer = core_peer
+        elif step == 1:
+            peer = y_peer
+        else:
+            flip = 1 << (step - 2)
+            peer = (dp + flip - 2 * flip * (dp // flip % 2), sq)
+        return remote(small_out, small_in.at[step], small_s.at[step], small_r.at[step], peer)
+
+    def small_step(step):
+        small_copy(step).wait()
+        small_out[...] = small_out[...] + small_in[step]
+
+    count = len(units)
+    pairs = count // 2
+    small_copy(0).start()
+    for turn in range(pairs + 5):
+        for unit in (2 * turn, 2 * turn + 1):
+            if unit < count:
+                products(unit)
+        for unit in (2 * turn - 2, 2 * turn - 1):
+            if 0 <= unit < count:
+                core_sum(unit)
+        for unit in (2 * turn - 4, 2 * turn - 3):
+            if 0 <= unit < count:
+                one_sum(unit)
+        for unit in (2 * turn - 6, 2 * turn - 5):
+            if 0 <= unit < count:
+                two_sum(unit)
+        for unit in (2 * turn - 8, 2 * turn - 7):
+            if 0 <= unit < count:
+                last_sum(unit)
+        if turn < bits + 2:
+            small_step(turn)
+            if turn + 1 < bits + 2:
+                small_copy(turn + 1).start()
+    for step in range(pairs + 5, bits + 2):
+        small_step(step)
+        if step + 1 < bits + 2:
+            small_copy(step + 1).start()
+    for unit in range(count):
+        if unit >= count - SLOTS:
+            core_copy(unit).wait_send()
+        one_copy(unit).wait_send()
+        two_copy(unit).wait_send()
+
+        def drain(step, carry):
+            three_copy(unit, step).wait_send()
+            return carry
+
+        lax.fori_loop(1, depth, drain, 0)
+
+
+def reduce_grads(units, operands, small, dp_size):
+    count = len(units)
+    depth, chunk = dp_size // 2, 1024 // dp_size
+    bits = dp_size.bit_length() - 1
+    low = jnp.bfloat16
+    out_shapes = [jax.ShapeDtypeStruct((chunk, COLS), jnp.float32)] * 8
+    out_shapes.append(jax.ShapeDtypeStruct((chunk, 4 * COLS), jnp.float32))
+    out_shapes.append(jax.ShapeDtypeStruct((4 * chunk, COLS), jnp.float32))
+    out_shapes.append(jax.ShapeDtypeStruct(small.shape, jnp.float32))
+    sem = pltpu.SemaphoreType.DMA
+    vmem = pl.BlockSpec(memory_space=pltpu.VMEM)
+    return pl.pallas_call(
+        functools.partial(reduce_kernel, units, len(operands), 10, dp_size),
+        out_shape=out_shapes,
+        in_specs=[vmem] * (len(operands) + 1),
+        out_specs=[vmem] * 11,
+        scratch_shapes=[
+            pltpu.VMEM((SLOTS, 2, 1024, COLS), low),
+            pltpu.VMEM((count, 2, 1024, COLS), low),
+            pltpu.VMEM((count // 2, 1024, COLS), low),
+            pltpu.VMEM((count // 2, 2, depth, chunk, COLS), low),
+            pltpu.VMEM((count, depth, chunk, COLS), low),
+            pltpu.VMEM((count, depth - 1, chunk, COLS), low),
+            pltpu.VMEM((bits + 2,) + small.shape, jnp.float32),
+            sem((count,)),
+            sem((count,)),
+            sem((count,)),
+            sem((count,)),
+            sem((count,)),
+            sem((count,)),
+            sem((count, depth - 1)),
+            sem((count, depth - 1)),
+            sem((bits + 2,)),
+            sem((bits + 2,)),
+        ],
+        compiler_params=pltpu.CompilerParams(
+            collective_id=0, has_side_effects=True, vmem_limit_bytes=60 << 20
+        ),
+    )(*operands, small)
 
 
 def per_device(
@@ -184,18 +481,12 @@
         jnp.bfloat16
     )
     input_wide = flat_rows.astype(jnp.float32)
-    totals = lax.psum(
-        (
-            jnp.sum(input_wide * input_wide * row_mask),
-            jnp.sum(attended * attended * row_mask),
-            jnp.sum(crossed * crossed * row_mask),
-            jnp.sum(ffn_out * ffn_out * row_mask),
-            jnp.sum(row_mask),
-        ),
-        ("dp", "seq"),
-    )
-    rms = jnp.sqrt(
-        jnp.stack([totals[0], totals[1], totals[2], totals[3]]) / (totals[4] * model_width)
+    local_totals = (
+        jnp.sum(input_wide * input_wide * row_mask),
+        jnp.sum(attended * attended * row_mask),
+        jnp.sum(crossed * crossed * row_mask),
+        jnp.sum(ffn_out * ffn_out * row_mask),
+        jnp.sum(row_mask),
     )
     key_block, value_block = (kept_keys, kept_values)
     cross_key_block, cross_value_block = (kept_cross_keys, kept_cross_values)
@@ -204,14 +495,11 @@
         resid_three, gain_three, shift_three, d_output
     )
     d_ffn_out = d_resid_three.astype(jnp.bfloat16)
-    g_back = weight_grad(activated, d_ffn_out)
     gelu_value, gelu_pull = jax.vjp(exact_gelu, ffn_inner)
     d_inner = gelu_pull(back_project(d_ffn_out, w_back))[0].astype(jnp.bfloat16)
-    g_in = weight_grad(second_norm, d_inner)
     d_second = d_resid_three + back_project(d_inner, w_in)
     d_resid_two, d_gain_two, d_shift_two = norm_back(resid_two, gain_two, shift_two, d_second)
     d_crossed = d_resid_two.astype(jnp.bfloat16)
-    g_cout = weight_grad(cross_low, d_crossed)
     d_cross_ctx = back_project(d_crossed, c_out).astype(jnp.bfloat16).reshape(head_shape)
     cross_back = jnp.exp(cross_scores(cross_key_block) - cross_lse)
     d_cross_probs = jnp.einsum(
@@ -254,18 +542,14 @@
     )
     d_cross_key = d_cross_key.astype(jnp.bfloat16).reshape(-1, model_width)
     d_cross_value = d_cross_value.astype(jnp.bfloat16).reshape(-1, model_width)
-    g_ckey = weight_grad(source_rows, d_cross_key)
-    g_cvalue = weight_grad(source_rows, d_cross_value)
     encoded_grad = (
         (back_project(d_cross_key, c_key) + back_project(d_cross_value, c_value))
         .astype(jnp.bfloat16)
         .reshape(encoded.shape)
     )
-    g_cquery = weight_grad(first_norm, d_cross_query)
     d_first = d_resid_two + back_project(d_cross_query, c_query)
     d_resid_one, d_gain_one, d_shift_one = norm_back(resid_one, gain_one, shift_one, d_first)
     d_attended = d_resid_one.astype(jnp.bfloat16)
-    g_out = weight_grad(context_low, d_attended)
     d_context = back_project(d_attended, w_out).astype(jnp.bfloat16).reshape(head_shape)
     scores_back, own_back = self_scores(key_block)
     p_main = jnp.exp(scores_back - self_lse[..., None])
@@ -314,9 +598,6 @@
         .reshape(-1, model_width)
     )
     d_query_low = d_queries.astype(jnp.bfloat16).reshape(-1, model_width)
-    g_query = weight_grad(flat_rows, d_query_low)
-    g_key = weight_grad(flat_rows, d_keys)
-    g_value = weight_grad(flat_rows, d_values)
     stream_grad = (
         (
             d_resid_one
@@ -332,20 +613,36 @@
     table_part = (
         table_part + own_hot[:, None] * jnp.sum(d_own.astype(jnp.float32), axis=(0, 1, 3))[None, :]
     )
-    small_sums = lax.psum(
-        (table_part, d_gain_one, d_shift_one, d_gain_two, d_shift_two, d_gain_three, d_shift_three),
-        ("dp", "seq"),
-    )
-    def share_of(grads, rows_dim):
-        low = grads.astype(jnp.bfloat16)
-        low = lax.psum_scatter(low, "seq", scatter_dimension=rows_dim + 1, tiled=True)
-        low = lax.psum_scatter(low, "dp", scatter_dimension=rows_dim, tiled=True)
-        return low.astype(jnp.float32)
-
-    square = share_of(
-        jnp.stack([g_query, g_key, g_value, g_out, g_cquery, g_ckey, g_cvalue, g_cout]), 1
-    )
-    shares = tuple(square[i] for i in range(8)) + (share_of(g_in, 0), share_of(g_back, 0))
+    tail = jnp.concatenate(
+        [table_part.reshape(-1), jnp.stack(local_totals), jnp.zeros((507,), jnp.float32)]
+    )
+    small = jnp.stack(
+        [d_gain_one, d_shift_one, d_gain_two, d_shift_two, d_gain_three, d_shift_three, tail]
+        + [jnp.zeros_like(tail)]
+    )
+    dp_size = lax.axis_size("dp")
+    chunk = model_width // dp_size
+    units = []
+    operands = [d_ffn_out, second_norm, d_inner, cross_low, d_crossed, first_norm, d_cross_query]
+    operands += [source_rows, d_cross_key, d_cross_value, context_low, d_attended]
+    operands += [flat_rows, d_query_low, d_keys, d_values]
+    if chunk % 128 == 0:
+        operands.append(activated)
+        for part in range(4):
+            units.append((16, 0, "back", part))
+    else:
+        parted = jnp.transpose(activated.reshape(-1, dp_size, 4, chunk), (2, 0, 1, 3))
+        parted = parted.reshape(4, -1, model_width)
+        for part in range(4):
+            operands.append(parted[part])
+            units.append((16 + part, 0, "parted", part))
+    for part in range(4):
+        units.append((1, 2, "in", part))
+    units += [(3, 4, "", 7), (5, 6, "", 4), (7, 8, "", 5), (7, 9, "", 6), (10, 11, "", 3)]
+    units += [(12, 13, "", 0), (12, 14, "", 1), (12, 15, "", 2)]
+    reduced = reduce_grads(tuple(units), operands, small, dp_size)
+    shares, sums = reduced[:10], reduced[10]
+    rms = jnp.sqrt(sums[6, 512:516] / (sums[6, 516] * model_width))
     return (
         layer_output.reshape(stream.shape),
         stream_grad,
@@ -360,13 +657,13 @@
         shares[7],
         shares[8],
         shares[9],
-        small_sums[1],
-        small_sums[2],
-        small_sums[3],
-        small_sums[4],
-        small_sums[5],
-        small_sums[6],
-        small_sums[0],
+        sums[0],
+        sums[1],
+        sums[2],
+        sums[3],
+        sums[4],
+        sums[5],
+        sums[6, :512].reshape(NBUCKET, HEADS),
         rms,
     )
 

time: 894 us -> 616 us (0.69)
  waiting for transfers between devices: 394 us -> 27.1 us
  Pallas kernels: 0 us -> 189 us
  blocking collectives: 41.4 us -> 0 us
  matrix products: 198 us -> 162 us
  local copies, waits for them, and re-layouts: 158 us -> 146 us
  other arithmetic: 79.4 us -> 67.5 us
    reduce_scatter x5 -> x2, waiting for transfers between devices: 304 us -> 26.9 us  [the longest x1 26.9 us: per_device(): lax.psum_scatter(cross_key_part.astype(jnp.bfloat16), 'seq', scatter_dime...]
    pallas_call x0 -> x1, Pallas kernels: none -> 189 us  [reduce_grads(): pl.pallas_call(functools.partial(reduce_kernel, units, len(operands), 10,...]
    unnamed x19 -> x10, waiting for transfers between devices: 89.5 us -> 0.14 us
    psum x1 -> x0, blocking collectives: 41.4 us -> none  [per_device(): lax.psum((table_part, d_gain_one, d_shift_one, d_gain_two, d_shift_two, d...]
    dot_general x10 -> x0, matrix products: 38.2 us -> none  [weight_grad(): jnp.einsum('nd,ne->de', left_rows, right_rows, preferred_element_type=jnp...]
    unnamed x214 -> x217, local copies, waits for them, and re-layouts: 75.3 us -> 44.8 us
    another operation x8 -> x11, local copies, waits for them, and re-layouts: 16.2 us -> 19.2 us
  transfers between devices with their start and end apart: 14 -> 8, of which waited for: 5 -> 1; matrix products, arithmetic and copies ran while one was open for 36% -> 36% of each run, Pallas kernels for 0% -> 0%
where the time goes in v2:
time: 616 us; the launch traced here: 610 us
  Pallas kernels  189 us (31%)
  matrix products  162 us (26%)
  local copies, waits for them, and re-layouts  146 us (24%)
  other arithmetic  67.5 us (11%)
  waiting for transfers between devices  27.1 us (4%)
  between operations  17.2 us (3%)
    pallas_call x1, Pallas kernels, reduce_grads(): pl.pallas_call(functools.partial(reduce_kernel, units, len(operands), 10,...  189 us
    unnamed x217, local copies, waits for them, and re-layouts  44.8 us
    dot_general x10, matrix products, project(): return jnp.dot(left_rows, weight, preferred_element_type=jnp.float32)  43.5 us
    dot_general x10, matrix products, back_project(): jnp.einsum('ne,de->nd', grad_rows, weight, preferred_element_type=jnp.flo...  39.4 us
    eq x1, local copies, waits for them, and re-layouts, per_device(): one_hot = (buckets[:, :, None] == bucket_ids).astype(jnp.float32)  37.3 us
    reduce_scatter x1, waiting for transfers between devices, per_device(): lax.psum_scatter(cross_key_part.astype(jnp.bfloat16), 'seq', scatter_dime...  26.9 us
    add x1, other arithmetic, per_device(): buckets = buckets + (distance >= starts[step]).astype(jnp.int32)  20.7 us
    another operation x8, local copies, waits for them, and re-layouts  18.5 us
  transfers between devices with their start and end apart: 8, of which 1 were waited for; matrix products, arithmetic and copies ran while one was open for 36% of the time, Pallas kernels for 0%

profile of v2, /device:TPU:0, one launch (start us, length us, event | category | flops | bytes accessed | tf_op | source)
XLA Modules:
  0.0 609.9 jit_solution(1191916831840020169)
XLA Ops:
  7.3 2.9 convolution_convert_fusion.4
  11.4 2.4 reshape.830
  15.0 3.7 convolution_convert_fusion.5
  18.7 2.3 copy.177
  21.0 2.4 reshape.828
  24.7 2.9 convolution_convert_fusion.6
  27.7 2.7 convolution_convert_fusion.7
  32.9 3.2 reshape.849
  36.1 3.3 reshape.833
  40.9 3.5 convolution_convert_fusion.3
  44.3 2.3 copy.179
  46.6 2.4 reshape.832
  49.0 20.7 %convert_add_fusion.3 = s32[128,512]{0,1:T(8,128)S(1)} fusion(s32[]{:T(128)} %bitcast.44, s32[]{:T(128)} %bitcast.43, s32[]{:T(128)} %bitcast.42, s32[]{:T(128)} %bitcast.41, s32[]{:T(128)} %bitcast.40, s32[]{:T(128)} %bitcast.39, s32[]{:T(128)} %bitcast.38, s32[]{:T(128)} %bitcast.37, s32[]{:T(128)} %bitcast.36, s32[]{:T(128)} %bitcast.35, s32[]{:T(128)} %bitcast.34, ...), kind=kLoop, calls=%fused_computation.142 | loop fusion | flops 6094848 | bytes 262780 | tf_op jit(solution)/shard_map/add | solution.py:378
  71.6 37.3 %copy.181 = pred[128,512,32]{1,2,0:T(32,128)(4,1)S(1)} copy(pred[128,512,32]{0,2,1:T(32,128)(4,1)S(1)} %iota_compare_fusion) | data formatting | bytes 4194304 | tf_op jit(solution)/shard_map/eq | solution.py:380
  109.7 3.8 convolution_bitcast_fusion
  113.5 5.3 copy.182
  120.9 4.9 fusion.133
  125.9 2.9 fusion.9
  130.4 4.1 divide_convert_fusion.1
  134.5 4.3 fusion.43
  148.2 2.7 copy.190
  152.8 4.4 bitcast_reduce_fusion
  157.2 3.2 fusion.10
  161.8 2.4 copy.187
  164.2 8.3 %fusion.53 = bf16[1,3,128,16,64]{2,4,1,3,0:T(8,128)(2,1)S(1)} fusion(bf16[512,16,64,1]{0,2,3,1:T(8,128)(2,1)} %bitcast.453, f32[16,512,3,128]{3,1,2,0:T(8,128)} %copy-done.3, f32[3,16,128]{2,0,1:T(4,128)S(1)} %fusion.10, f32[3,16,128]{2,0,1:T(4,128)S(1)} %get-tuple-element.209, pred[512]{0:T(512)(128)(4,1)S(1)} %iota_compare_fusion.1), kind=kOutput, calls=%fused_computation.113 | convolution fusion | flops 418775040 | bytes 14467584 | tf_op jit(solution)/shard_map/rshtj,rjha->rstha/dot_general | solution.py:466
  175.5 20.0 %multiply_convert_fusion = (bf16[384,4096]{1,0:T(8,128)(2,1)S(1)}, f32[384,4096]{1,0:T(8,128)}, f32[384,4096]{1,0:T(8,128)}) fusion(bf16[384,1024]{1,0:T(8,128)(2,1)S(1)} %add_convert_fusion.2.refs_1_, bf16[1024,4096]{1,0:T(8,128)(2,1)} %param.35), kind=kOutput, calls=%fused_computation.42 | convolution fusion | flops 3323461632 | bytes 24903680 | tf_op jit(solution)/shard_map/dot_general | solution.py:38
  195.6 3.5 fusion.126
  200.2 2.3 multiply_reduce_fusion
  205.5 14.1 %add_convert_fusion.refs_2_ = bf16[384,4096]{1,0:T(8,128)(2,1)} fusion(f32[384,4096]{1,0:T(8,128)} %get-tuple-element.158, f32[384,4096]{1,0:T(8,128)} %get-tuple-element.212, bf16[384,1024]{1,0:T(8,128)(2,1)S(1)} %add_convert_fusion.6.refs_0_, bf16[4096,1024]{1,0:T(8,128)(2,1)} %param.36), kind=kOutput, calls=%fused_computation.41 | convolution fusion | flops 3243245568 | bytes 24903680 | tf_op jit(solution)/shard_map/ne,de->nd/dot_general | solution.py:46
  219.7 7.4 %multiply_reduce_fusion.6 = (f32[1024]{0:T(1024)S(1)}, f32[384]{0:T(512)S(1)}, f32[1024]{0:T(1024)S(1)}, f32[384,1024]{1,0:T(8,128)S(1)}) fusion(f32[384,1024]{1,0:T(8,128)S(1)} %get-tuple-element.160, f32[384]{0:T(512)S(1)} %fusion.109, f32[384]{0:T(512)S(1)} %broadcast_multiply_fusion.1, f32[1024]{0:T(1024)S(1)} %copy-done.75, ...), kind=kOutput, calls=%fused_computation.83 | convolution fusion | flops 3225155072 | bytes 16271360 | tf_op jit(solution)/shard_map/ne,de->nd/dot_general | solution.py:46
  231.6 2.9 reshape.893
  236.4 8.5 %fusion.4 = (f32[3,16,128]{2,0,1:T(4,128)S(1)}, f32[16,512,3,128]{3,1,2,0:T(8,128)S(1)}) fusion(f32[16,512,3,128]{3,1,2,0:T(8,128)} %copy-done.3, f32[3,16,128]{2,0,1:T(4,128)S(1)} %log_add_fusion.1, pred[512]{0:T(512)(128)(4,1)S(1)} %iota_compare_fusion.1, bf16[512,16,64,1]{0,2,3,1:T(8,128)(2,1)} %bitcast.454, bf16[3,128,16,64]{1,3,0,2:T(8,128)(2,1)} %copy.194), kind=kOutput, calls=%fused_computation.9 | convolution fusion | flops 418375680 | bytes 27050496 | tf_op jit(solution)/shard_map/rstha,rjha->rshtj/dot_general | solution.py:505
  244.9 7.3 %fusion.12 = bf16[3,16,128,512]{2,3,0,1:T(8,128)(2,1)S(1)} fusion(f32[16,512,3,128]{3,1,2,0:T(8,128)S(1)} %get-tuple-element.216, f32[16,512,3,128]{3,1,2,0:T(8,128)} %copy-done.3, f32[3,16,128]{2,0,1:T(4,128)S(1)} %get-tuple-element.215, f32[3,16,128]{2,0,1:T(4,128)S(1)} %log_add_fusion.1, pred[512]{0:T(512)(128)(4,1)S(1)} %iota_compare_fusion.1), kind=kLoop, calls=%fused_computation.28 | loop fusion | flops 18874368 | bytes 31506944 | tf_op jit(solution)/shard_map/reshape.39
  264.1 4.9 bitcast_convert_fusion.1
  269.0 4.0 copy.258
  273.0 3.0 copy.300
  276.2 10.8 %fusion.1 = (f32[3,16,128]{2,0,1:T(4,128)S(1)}, f32[16,512,3,128]{3,1,2,0:T(8,128)}) fusion(f32[1,3,16,128,512]{3,4,1,2,0:T(8,128)} %copy-done.2, f32[3,16,128]{2,0,1:T(4,128)S(1)} %copy-done.63, bf16[512,16,64,1]{0,2,3,1:T(8,128)(2,1)S(1)} %bitcast.434, bf16[3,128,16,64]{1,0,3,2:T(4,128)(2,1)S(1)} %reshape.848), kind=kOutput, calls=%fused_computation.4 | convolution fusion | flops 412084224 | bytes 27049984 | tf_op jit(solution)/shard_map/rstha,rjha->rshtj/dot_general | solution.py:557
  289.3 10.1 %convert_reduce_fusion = (f32[16,128,512]{1,2,0:T(8,128)}, bf16[1,3,16,128,512]{3,4,1,2,0:T(8,128)(2,1)S(1)}) fusion(f32[3,16,128]{2,0,1:T(4,128)S(1)} %get-tuple-element.164, f32[16,512,3,128]{3,1,2,0:T(8,128)} %get-tuple-element.219, f32[1,3,16,128,512]{3,4,1,2,0:T(8,128)S(1)} %bitcast.428, f32[3,16,128]{2,0,1:T(4,128)S(1)} %copy-done.63), kind=kLoop, calls=%fused_computation.18 | loop fusion | flops 17825792 | bytes 35700736 | tf_op jit(solution)/shard_map/reduce_sum | solution.py:611
  305.4 8.1 %bitcast_convert_fusion = bf16[16,64,512]{2,1,0:T(8,128)(2,1)S(1)} fusion(bf16[3,128,16,64]{1,3,0,2:T(8,128)(2,1)S(1)} %copy-done.46, f32[16,512,3,128]{3,1,2,0:T(8,128)} %copy-done.3, f32[3,16,128]{2,0,1:T(4,128)S(1)} %fusion.10, f32[3,16,128]{2,0,1:T(4,128)S(1)} %get-tuple-element.209, pred[512]{0:T(512)(128)(4,1)S(1)} %iota_compare_fusion.1), kind=kOutput, calls=%fused_computation.62 | convolution fusion | flops 418906112 | bytes 14467584 | tf_op jit(solution)/shard_map/rshtj,rstha->rjha/dot_general | solution.py:532
  321.8 2.3 copy.222.refs_6_
  324.2 4.9 fusion.32
  331.6 8.0 %fusion.61 = f32[32,16]{0,1:T(8,128)S(1)} fusion(f32[16,128,512]{1,2,0:T(8,128)} %get-tuple-element.144, f32[16]{0:T(128)S(1)} %get-tuple-element.142, f32[32]{0:T(128)S(1)} %compare_convert_fusion.1, s32[128,512]{0,1:T(8,128)S(1)} %copy-done.53), kind=kOutput, calls=%fused_computation.120 | convolution fusion | flops 404751360 | bytes 4458688 | tf_op jit(solution)/shard_map/htj,tjb->bh/dot_general | solution.py:612
  339.8 4.2 fusion.42
  346.0 3.3 concatenate.23
  361.2 26.9 %reduce-scatter.9.cloned.1.call-done = bf16[1,128,1024]{2,1,0:T(8,128)(2,1)} async-done(((bf16[1,512,1024]{2,1,0:T(8,128)(2,1)}), bf16[1,128,1024]{2,1,0:T(8,128)(2,1)}) %reduce-scatter.9.cloned.1.call-update) | async-done | bytes 262160 | tf_op jit(solution)/shard_map/reduce_scatter | solution.py:536
  388.0 189.5 %shard_map.373 = (f32[128,256]{1,0:T(8,128)}, f32[128,256]{1,0:T(8,128)}, f32[128,256]{1,0:T(8,128)}, f32[128,256]{1,0:T(8,128)}, f32[128,256]{1,0:T(8,128)}, /*...) custom-call(bf16[384,1024]{1,0:T(8,128)(2,1)} %copy-done.43, ...), custom_call_target="tpu_custom_call" | custom-call | tf_op jit(solution)/shard_map/pallas_call | solution.py:310
  581.1 4.1 fusion.135
  587.9 4.6 add_convert_fusion.1
  (338 shorter events, 99.7 us)
Async XLA Ops:
  7.2 166.2 %copy-start = (bf16[1024,1024]{1,0:T(8,128)(2,1)S(1)}, bf16[1024,1024]{1,0:T(8,128)(2,1)}, u32[]{:S(2)}) copy-start(bf16[1024,1024]{1,0:T(8,128)(2,1)} %param.34) | copy-start | bytes 6291460
  7.2 113.7 %all-gather.9.cloned.1.call-start = ((), (), s32[]{:S(2)}) async-start(), calls=%async_computation.5 | async-start | bytes 1310720 | tf_op jit(solution)/shard_map/all_gather | solution.py:405
  13.8 4.9 copy-start.12
  15.0 119.5 %all-gather.7.cloned.1.call-start = ((), (), s32[]{:S(2)}) async-start(), calls=%async_computation.4 | async-start | bytes 1310720 | tf_op jit(solution)/shard_map/all_gather | solution.py:406
  23.5 4.1 copy-start.14
  24.7 126.2 %all-gather.13.cloned.1.call-start = ((), (), s32[]{:S(2)}) async-start(), calls=%async_computation.9 | async-start | bytes 1310720 | tf_op jit(solution)/shard_map/all_gather | solution.py:447
  27.6 134.2 %all-gather.11.cloned.1.call-start = ((), (), s32[]{:S(2)}) async-start(), calls=%async_computation.8 | async-start | bytes 1310720 | tf_op jit(solution)/shard_map/all_gather | solution.py:448
  30.4 10.4 %copy-start.20 = (bf16[1,3,128,1024]{3,2,1,0:T(8,128)(2,1)S(1)}, bf16[1,3,128,1024]{3,2,1,0:T(8,128)(2,1)}, u32[]{:S(2)}) copy-start(bf16[1,3,128,1024]{3,2,1,0:T(8,128)(2,1)} %param.22) | copy-start | bytes 2359300
  30.4 324.8 %reduce-scatter.15.cloned.1.call-start = ((), (), s32[]{:S(2)}) async-start(), calls=%async_computation.11 | async-start | bytes 1310720
  30.7 99.6 %copy-start.79 = (pred[3]{0:T(512)(128)(4,1)}, pred[3]{0:T(512)(128)(4,1)S(1)}, u32[]{:S(2)}) copy-start(pred[3]{0:T(512)(128)(4,1)S(1)} %iota_compare_fusion.2) | copy-start | bytes 13
  40.1 4.2 copy-start.84
  49.0 71.9 %copy-start.10 = (bf16[3,128,16,64]{1,0,3,2:T(4,128)(2,1)}, bf16[3,128,16,64]{1,0,3,2:T(4,128)(2,1)S(1)}, u32[]{:S(2)}) copy-start(bf16[3,128,16,64]{1,0,3,2:T(4,128)(2,1)S(1)} %reshape.832) | copy-start | bytes 2359300
  71.6 37.3 %copy-start.73 = (f32[32,16]{0,1:T(8,128)S(1)}, f32[32,16]{0,1:T(8,128)}, u32[]{:S(2)}) copy-start(f32[32,16]{0,1:T(8,128)} %param.43) | copy-start | bytes 6148
  109.7 20.6 %copy-start.77 = (f32[16]{0:T(128)}, f32[16]{0:T(128)S(1)}, u32[]{:S(2)}) copy-start(f32[16]{0:T(128)S(1)} %convolution_bitcast_fusion.1) | copy-start | bytes 196
  120.7 9.6 %copy-start.59 = (f32[3,16,128]{2,0,1:T(4,128)}, f32[3,16,128]{2,0,1:T(4,128)S(1)}, u32[]{:S(2)}) copy-start(f32[3,16,128]{2,0,1:T(4,128)S(1)} %fusion.35) | copy-start | bytes 73732
  125.8 4.6 copy-start.2
  157.2 4.5 copy-start.3
  173.7 21.9 %slice-start.3 = ((s8[8388608]{0:T(1024)(128)(4,1)}), s8[4194304]{0:T(1024)(128)(4,1)S(1)}, s32[]{:S(2)}) async-start(s8[8388608]{0:T(1024)(128)(4,1)} %bitcast.491), calls=%async_computation.15 | async-start | bytes 8388608
  175.5 20.1 %copy-start.42 = (bf16[384,1024]{1,0:T(8,128)(2,1)}, bf16[384,1024]{1,0:T(8,128)(2,1)S(1)}, u32[]{:S(2)}) copy-start(bf16[384,1024]{1,0:T(8,128)(2,1)S(1)} %add_convert_fusion.2.refs_1_) | copy-start | bytes 2359300
  175.5 20.1 %slice-start.4 = ((s8[8388608]{0:T(1024)(128)(4,1)}), s8[4194304]{0:T(1024)(128)(4,1)S(1)}, s32[]{:S(2)}) async-start(s8[8388608]{0:T(1024)(128)(4,1)} %bitcast.491), calls=%async_computation.16 | async-start | bytes 8388608
  205.5 14.2 %copy-start.43 = (bf16[384,1024]{1,0:T(8,128)(2,1)}, bf16[384,1024]{1,0:T(8,128)(2,1)S(1)}, u32[]{:S(2)}) copy-start(bf16[384,1024]{1,0:T(8,128)(2,1)S(1)} %add_convert_fusion.6.refs_0_) | copy-start | bytes 2359300
  205.5 14.2 %copy-start.35 = (f32[384,1024]{1,0:T(8,128)S(1)}, f32[384,1024]{1,0:T(8,128)}, u32[]{:S(2)}) copy-start(f32[384,1024]{1,0:T(8,128)} %copy-done.34) | copy-start | bytes 4718596
  276.1 82.2 %reduce-scatter.13.cloned.1.call-start = ((), (), s32[]{:S(2)}) async-start(), calls=%async_computation.10 | async-start | bytes 1310720
  276.1 12.8 %slice-start = ((s8[12582912]{0:T(1024)(128)(4,1)}), s8[4194304]{0:T(1024)(128)(4,1)S(1)}, s32[]{:S(2)}) async-start(s8[12582912]{0:T(1024)(128)(4,1)} %bitcast.427), calls=%async_computation.12 | async-start | bytes 8388608
  276.2 10.8 %copy-start.40 = (bf16[3,128,16,64]{1,0,3,2:T(4,128)(2,1)S(1)}, bf16[3,128,16,64]{1,0,3,2:T(4,128)(2,1)}, u32[]{:S(2)}) copy-start(bf16[3,128,16,64]{1,0,3,2:T(4,128)(2,1)} %reshape.849) | copy-start | bytes 2359300
  276.2 12.8 %slice-start.1 = ((s8[12582912]{0:T(1024)(128)(4,1)}), s8[4194304]{0:T(1024)(128)(4,1)S(1)}, s32[]{:S(2)}) async-start(s8[12582912]{0:T(1024)(128)(4,1)} %bitcast.427), calls=%async_computation.13 | async-start | bytes 8388608
  276.2 13.1 %slice-start.2 = ((s8[12582912]{0:T(1024)(128)(4,1)}), s8[4194304]{0:T(1024)(128)(4,1)S(1)}, s32[]{:S(2)}) async-start(s8[12582912]{0:T(1024)(128)(4,1)} %bitcast.427), calls=%async_computation.14 | async-start | bytes 8388608
  289.3 10.1 %copy-start.11 = (bf16[3,128,16,64]{1,0,3,2:T(4,128)(2,1)S(1)}, bf16[3,128,16,64]{1,0,3,2:T(4,128)(2,1)}, u32[]{:S(2)}) copy-start(bf16[3,128,16,64]{1,0,3,2:T(4,128)(2,1)} %copy-done.10) | copy-start | bytes 2359300
  305.4 55.8 %reduce-scatter.11.cloned.1.call-start = ((), (), s32[]{:S(2)}) async-start(), calls=%async_computation.7 | async-start | bytes 1310720 | tf_op jit(solution)/shard_map/reduce_scatter | solution.py:539
  315.0 73.1 %reduce-scatter.9.cloned.1.call-start = ((), (), s32[]{:S(2)}) async-start(), calls=%async_computation.6 | async-start | bytes 1310720 | tf_op jit(solution)/shard_map/reduce_scatter | solution.py:536
  315.2 4.3 copy-start.27
  316.5 4.2 copy-start.29
  319.5 4.7 copy-start.72
  319.5 4.7 copy-start.31
  331.6 8.2 %copy-start.13 = (bf16[1,3,128,16,64]{2,1,4,3,0:T(4,128)(2,1)S(1)}, bf16[1,3,128,16,64]{2,1,4,3,0:T(4,128)(2,1)}, u32[]{:S(2)}) copy-start(bf16[1,3,128,16,64]{2,1,4,3,0:T(4,128)(2,1)} %copy-done.12) | copy-start | bytes 2359300
  331.6 8.2 %copy-start.16 = (bf16[1,512,1024]{1,2,0:T(8,128)(2,1)S(1)}, bf16[1,512,1024]{1,2,0:T(8,128)(2,1)}, u32[]{:S(2)}) copy-start(bf16[1,512,1024]{1,2,0:T(8,128)(2,1)} %all-gather.9.cloned.1.call-done) | copy-start | bytes 3145732
  344.8 4.5 copy-start.48
  581.1 6.8 %copy-start.9 = (f32[384,1024]{1,0:T(8,128)S(1)}, f32[384,1024]{1,0:T(8,128)}, u32[]{:S(2)}) copy-start(f32[384,1024]{1,0:T(8,128)} %copy-done.8) | copy-start | bytes 4718596
  581.1 6.8 %copy-start.25 = (bf16[1,3,128,1024]{3,2,1,0:T(8,128)(2,1)S(1)}, bf16[1,3,128,1024]{3,2,1,0:T(8,128)(2,1)}, u32[]{:S(2)}) copy-start(bf16[1,3,128,1024]{3,2,1,0:T(8,128)(2,1)} %copy.212) | copy-start | bytes 2359300
  587.9 4.6 copy-start.19
  587.9 4.6 copy-start.58
  594.1 4.2 copy-start.67
  594.1 4.9 copy-start.66
  594.1 5.5 copy-start.65
  594.1 6.2 %copy-start.64 = (f32[128,256]{1,0:T(8,128)S(1)}, f32[128,256]{1,0:T(8,128)}, u32[]{:S(2)}) copy-start(f32[128,256]{1,0:T(8,128)} %get-tuple-element.251) | copy-start | bytes 393220
  594.2 6.8 %copy-start.62 = (f32[128,1024]{1,0:T(8,128)S(1)}, f32[128,1024]{1,0:T(8,128)}, u32[]{:S(2)}) copy-start(f32[128,1024]{1,0:T(8,128)} %get-tuple-element.252) | copy-start | bytes 1572868
  595.7 6.1 copy-start.61
  595.7 6.9 %copy-start.1 = (bf16[1024,1024]{1,0:T(8,128)(2,1)S(1)}, bf16[1024,1024]{1,0:T(8,128)(2,1)}, u32[]{:S(2)}) copy-start(bf16[1024,1024]{1,0:T(8,128)(2,1)} %param.34) | copy-start | bytes 6291460
  (55 other events, 116.8 us)
Sparse Core Ops, SparseCore 0:
  15.1 19.5 all-gather.8
  36.8 16.8 all-gather.6
  55.3 16.6 all-gather.12
  74.0 16.7 all-gather.10
  276.2 27.5 reduce-scatter.14
  306.3 26.5 reduce-scatter.12
  335.4 24.9 reduce-scatter.10
  363.1 24.8 reduce-scatter.8

commit v3 on v2

v3 whole, which is shorter than its diff:
```python
import functools

import jax
import jax.numpy as jnp
from jax import lax
from jax.experimental import pallas as pl
from jax.experimental.pallas import tpu as pltpu
from jax.sharding import PartitionSpec as P

HEADS = 16
HEAD_DIM = 64
NBUCKET = 32
COLS = 256
SLOTS = 4
epsilon = 1e-05
masked_score = -1e30


LOW = jnp.bfloat16
WIDE = jnp.float32
NN = (((1,), (0,)), ((), ()))
NT = (((1,), (1,)), ((), ()))


def dot(left, right, dims=NN):
    return lax.dot_general(left, right, dims, preferred_element_type=WIDE)


def flip(block):
    return jnp.transpose(block.astype(WIDE))


def places():
    dp, sq = lax.axis_index("dp"), lax.axis_index("seq")
    core, ypos = sq % 2, sq // 2
    return dp, sq, core, ypos, (dp, sq + 1 - 2 * core), (dp, sq + 2 - 4 * ypos)


def remote_copy(src, dst, send_sem, recv_sem, peer):
    return pltpu.make_async_remote_copy(
        src_ref=src,
        dst_ref=dst,
        send_sem=send_sem,
        recv_sem=recv_sem,
        device_id=peer,
        device_id_type=MESH_ID,
    )


def greet(peers):
    barrier = pltpu.get_barrier_semaphore()
    for peer in peers:
        pl.semaphore_signal(barrier, inc=1, device_id=peer, device_id_type=MESH_ID)
    pl.semaphore_wait(barrier, len(peers))


def tiles(count, size, body):
    def step(index, carry):
        body(pl.ds(pl.multiple_of(index * size, size), size))
        return carry

    lax.fori_loop(0, count, step, 0)


def project_to(dst, left, weight, scale=None):
    def body(cols):
        product = dot(left[...], weight[:, cols])
        if scale is not None:
            product = product * scale
        dst[:, cols] = product.astype(dst.dtype)

    tiles(dst.shape[1] // 256, 256, body)


def norm_stats(rows):
    centre = jnp.mean(rows, axis=-1, keepdims=True)
    centred = rows - centre
    spread = jnp.mean(centred * centred, axis=-1, keepdims=True)
    return centred, lax.rsqrt(spread + epsilon)


def norm_backward(rows, gain, incoming):
    centred, scale = norm_stats(rows)
    unit = centred * scale
    scaled = incoming * gain
    first = jnp.mean(scaled, axis=-1, keepdims=True)
    second = jnp.mean(scaled * unit, axis=-1, keepdims=True)
    grads = scale * (scaled - first - unit * second)
    d_gain = jnp.sum(incoming * unit, axis=0, keepdims=True)
    return grads, d_gain, jnp.sum(incoming, axis=0, keepdims=True)


def valid_rows(sq, length, count):
    position = sq * count + lax.broadcasted_iota(jnp.int32, (count, 1), 0)
    return (position < length).astype(WIDE)


def sum_squares(rows, mask):
    return jnp.sum(rows * rows * mask, axis=0, keepdims=True)


def half_rows(block, side):
    row = lax.broadcasted_iota(jnp.int32, block.shape, 0)
    return jnp.where(row // HEAD_DIM == side, block, 0.0).astype(LOW)


def half_lanes(block, side):
    lane = lax.broadcasted_iota(jnp.int32, block.shape, 1)
    return jnp.where(lane // HEAD_DIM == side, block.astype(WIDE), 0.0).astype(LOW)


def front_kernel(*refs):
    stream, encoded, length_ref, bias_table = refs[:4]
    gain_one, shift_one, gain_two, shift_two = refs[4:8]
    hbm_weights = refs[8:16]
    (query, own_key, own_value, main_key, main_value, context, resid_one, first_norm) = refs[16:24]
    (cross_query, cross_key, cross_value, cross_context, resid_two, second_norm) = refs[24:30]
    own_probs, stats, probs_out, cross_probs_out = refs[30:34]
    weights = refs[34:42]
    main_all, source_all, kept, bias, masks = refs[42:47]
    weight_sem, kept_sem, send_sem, recv_sem = refs[47:]
    w_query, w_key, w_value, w_out, c_query, c_key, c_value, c_out = weights
    dp, sq, core, ypos, core_peer, y_peer = places()
    length = length_ref[0]
    rows = stream.shape[1]
    full = main_all.shape[0] * rows
    loads = [
        pltpu.make_async_copy(src, dst, weight_sem.at[index])
        for index, (src, dst) in enumerate(zip(hbm_weights, weights))
    ]
    for load in loads:
        load.start()
    greet([core_peer, y_peer])
    sources = (stream.at[0], encoded)
    gathered = (main_all, source_all)
    firsts = []
    for index in range(2):
        for lane, peer in enumerate((y_peer, core_peer)):
            slot = index * 3 + lane
            firsts.append(
                remote_copy(
                    sources[index],
                    gathered[index].at[sq],
                    send_sem.at[slot],
                    recv_sem.at[slot],
                    peer,
                )
            )
            firsts[-1].start()
    main_all[sq] = stream[0]
    source_all[sq] = encoded[...]

    def passed_on(index):
        other = gathered[index].at[sq + 2 - 4 * ypos]
        slot = index * 3 + 2
        return remote_copy(other, other, send_sem.at[slot], recv_sem.at[slot], core_peer)

    flat = stream.reshape(3 * rows, stream.shape[2])
    loads[0].wait()
    project_to(query, flat, w_query, 0.125)
    firsts[0].wait_recv()
    passed_on(0).start()
    predicting = flat.at[rows:, :]
    loads[1].wait()
    project_to(own_key, predicting, w_key)
    loads[2].wait()
    project_to(own_value, predicting, w_value)
    firsts[1].wait_recv()
    passed_on(0).wait_recv()
    firsts[2].wait_recv()
    passed_on(1).start()
    wide_main = main_all.reshape(full, main_all.shape[2])
    project_to(main_key, wide_main, w_key)
    project_to(main_value, wide_main, w_value)

    key_row = lax.broadcasted_iota(jnp.int32, (full, rows), 0)
    distance = sq * rows + lax.broadcasted_iota(jnp.int32, (full, rows), 1) - key_row
    in_range = key_row < length
    masks[0] = jnp.where((distance >= 0) & in_range, 0.0, masked_score)
    masks[1] = jnp.where((distance > 0) & in_range, 0.0, masked_score)
    masks[2] = jnp.where(in_range, 0.0, masked_score)

    def kept_copy(pair, out):
        slot = pair % 2
        return pltpu.make_async_copy(kept.at[slot], out.at[pair], kept_sem.at[slot])

    def self_pair(pair, carry):
        @pl.when(pair >= 2)
        def _():
            kept_copy(pair - 2, probs_out).wait()

        slot = pair % 2
        cols = pl.ds(pl.multiple_of(pair * 128, 128), 128)
        keys = main_key[:, cols]
        query_t = flip(query[:, cols])
        value_t = flip(main_value[:, cols]).astype(LOW)
        own_key_t, own_value_t = flip(own_key[:, cols]), flip(own_value[:, cols])
        own_product = query_t[:, rows:] * own_key_t
        sides = []
        for side in range(2):
            head = 2 * pair + side
            span = slice(side * HEAD_DIM, (side + 1) * HEAD_DIM)
            scores = dot(keys, half_rows(query_t, side))
            own_bias = bias_table[head, :, full : full + 128][:, 0:1]
            own_score = jnp.sum(own_product[span], axis=0, keepdims=True) + own_bias
            for block in range(full // rows):
                start = pl.multiple_of((sq - block + full // rows - 1) * rows, 128)
                line = bias_table[head, :, pl.ds(start, 2 * rows)]
                wide = jnp.broadcast_to(line, (rows, 2 * rows))
                near = pltpu.roll(wide, 0, 1, stride=1, stride_axis=0)[:, rows:]
                part = slice(block * rows, (block + 1) * rows)
                for kind in range(2):
                    bias[kind, part, :] = near + masks[kind, part, :]
            owns = []
            for stream_id in range(3):
                lanes = slice(stream_id * rows, (stream_id + 1) * rows)
                score = scores[:, lanes] + bias[min(stream_id, 1)]
                top = jnp.max(score, axis=0, keepdims=True)
                if stream_id > 0:
                    own = own_score[:, (stream_id - 1) * rows : stream_id * rows]
                    top = jnp.maximum(top, own)
                expo = jnp.exp(score - top)
                total = jnp.sum(expo, axis=0, keepdims=True)
                if stream_id > 0:
                    expo_own = jnp.exp(own - top)
                    total = total + expo_own
                share = 1.0 / total
                kept[slot, side, :, lanes] = (expo * share).astype(LOW)
                owns.append(expo_own * share if stream_id > 0 else jnp.zeros_like(total))
            own_probs[head] = jnp.concatenate(owns, axis=1)
            mixed = dot(value_t[span], kept[slot, side])
            mixed_own = jnp.concatenate(owns[1:], axis=1) * own_value_t[span]
            sides.append(
                jnp.concatenate([mixed[:, :rows], mixed[:, rows:] + mixed_own], axis=1)
            )
        context[:, cols] = jnp.transpose(jnp.concatenate(sides, axis=0)).astype(LOW)
        kept_copy(pair, probs_out).start()
        return carry

    lax.fori_loop(0, HEADS // 2, self_pair, 0)
    for pair in range(HEADS // 2 - 2, HEADS // 2):
        kept_copy(pair, probs_out).wait()

    mask = valid_rows(sq, length, rows)
    loads[3].wait()
    project_to(resid_one, context, w_out)
    seen = jnp.zeros((1, stream.shape[2]), WIDE)
    branch = jnp.zeros((1, stream.shape[2]), WIDE)
    for stream_id in range(3):
        part = slice(stream_id * rows, (stream_id + 1) * rows)
        source, attended = stream[stream_id].astype(WIDE), resid_one[part, :]
        seen = seen + sum_squares(source, mask)
        branch = branch + sum_squares(attended, mask)
        total = source + attended
        resid_one[part, :] = total
        centred, scale = norm_stats(total)
        first_norm[part, :] = (centred * scale * gain_one[...] + shift_one[...]).astype(LOW)
    stats[0:1, :] = seen
    stats[1:2, :] = branch
    loads[4].wait()
    project_to(cross_query, first_norm, c_query, 0.125)
    firsts[3].wait_recv()
    passed_on(1).wait_recv()
    wide_source = source_all.reshape(full, source_all.shape[2])
    loads[5].wait()
    project_to(cross_key, wide_source, c_key)
    loads[6].wait()
    project_to(cross_value, wide_source, c_value)

    def cross_pair(pair, carry):
        @pl.when(pair >= 2)
        def _():
            kept_copy(pair - 2, cross_probs_out).wait()

        slot = pair % 2
        cols = pl.ds(pl.multiple_of(pair * 128, 128), 128)
        keys = cross_key[:, cols]
        query_t = flip(cross_query[:, cols])
        value_t = flip(cross_value[:, cols]).astype(LOW)
        sides = []
        for side in range(2):
            span = slice(side * HEAD_DIM, (side + 1) * HEAD_DIM)
            scores = dot(keys, half_rows(query_t, side))
            for stream_id in range(3):
                lanes = slice(stream_id * rows, (stream_id + 1) * rows)
                score = scores[:, lanes] + masks[2]
                expo = jnp.exp(score - jnp.max(score, axis=0, keepdims=True))
                share = 1.0 / jnp.sum(expo, axis=0, keepdims=True)
                kept[slot, side, :, lanes] = (expo * share).astype(LOW)
            sides.append(dot(value_t[span], kept[slot, side]))
        cross_context[:, cols] = jnp.transpose(jnp.concatenate(sides, axis=0)).astype(LOW)
        kept_copy(pair, cross_probs_out).start()
        return carry

    lax.fori_loop(0, HEADS // 2, cross_pair, 0)
    for pair in range(HEADS // 2 - 2, HEADS // 2):
        kept_copy(pair, cross_probs_out).wait()
    loads[7].wait()
    project_to(resid_two, cross_context, c_out)
    branch = jnp.zeros((1, stream.shape[2]), WIDE)
    for stream_id in range(3):
        part = slice(stream_id * rows, (stream_id + 1) * rows)
        crossed = resid_two[part, :]
        branch = branch + sum_squares(crossed, mask)
        total = first_norm[part, :].astype(WIDE) + crossed
        resid_two[part, :] = total
        centred, scale = norm_stats(total)
        second_norm[part, :] = (centred * scale * gain_two[...] + shift_two[...]).astype(LOW)
    stats[2:3, :] = branch
    for copy in firsts:
        copy.wait_send()
    for index in range(2):
        passed_on(index).wait_send()


def front(stream, encoded, length, bias_table, norms, weights):
    streams, rows, width = stream.shape
    seq = lax.axis_size("seq")
    full, tokens = seq * rows, streams * rows
    own = tokens - rows
    shape = jax.ShapeDtypeStruct
    pairs = HEADS // 2
    outs = [
        shape((tokens, width), LOW),
        shape((own, width), LOW),
        shape((own, width), LOW),
        shape((full, width), LOW),
        shape((full, width), LOW),
        shape((tokens, width), LOW),
        shape((tokens, width), WIDE),
        shape((tokens, width), LOW),
        shape((tokens, width), LOW),
        shape((full, width), LOW),
        shape((full, width), LOW),
        shape((tokens, width), LOW),
        shape((tokens, width), WIDE),
        shape((tokens, width), LOW),
        shape((HEADS, 1, tokens), WIDE),
        shape((3, width), WIDE),
        shape((pairs, 2, full, tokens), LOW),
        shape((pairs, 2, full, tokens), LOW),
    ]
    vmem = pl.BlockSpec(memory_space=pltpu.VMEM)
    smem = pl.BlockSpec(memory_space=pltpu.SMEM)
    hbm = pl.BlockSpec(memory_space=pl.ANY)
    sem = pltpu.SemaphoreType.DMA
    return pl.pallas_call(
        front_kernel,
        out_shape=outs,
        in_specs=[vmem, vmem, smem] + [vmem] * 5 + [hbm] * 8,
        out_specs=[vmem] * 16 + [hbm] * 2,
        scratch_shapes=[pltpu.VMEM(w.shape, LOW) for w in weights]
        + [
            pltpu.VMEM((seq, rows, width), LOW),
            pltpu.VMEM((seq, rows, width), LOW),
            pltpu.VMEM((2, 2, full, tokens), LOW),
            pltpu.VMEM((2, full, rows), WIDE),
            pltpu.VMEM((3, full, rows), WIDE),
            sem((8,)),
            sem((2,)),
            sem((6,)),
            sem((6,)),
        ],
        compiler_params=pltpu.CompilerParams(
            collective_id=1, has_side_effects=True, vmem_limit_bytes=60 << 20
        ),
    )(stream, encoded, length, bias_table, *norms, *weights)


def middle_kernel(*refs):
    second_norm, resid_two, cotangent, length_ref, gain_two, gain_three, shift_three = refs[:7]
    hbm_in, hbm_back = refs[7:9]
    output, activated, d_ffn, d_inner, d_resid, d_crossed, grads, stats = refs[9:17]
    w_in, w_back, slope, total, load_sem = refs[17:]
    sq = lax.axis_index("seq")
    length = length_ref[0]
    tokens, width = second_norm.shape
    rows = tokens // 3
    hidden = w_in.shape[1]
    size = 512
    steps = hidden // size

    def load_in(step):
        cols = pl.ds(pl.multiple_of(step * size, size), size)
        return pltpu.make_async_copy(hbm_in.at[:, cols], w_in.at[:, cols], load_sem.at[0, step])

    def load_back(step):
        cols = pl.ds(pl.multiple_of(step * size, size), size)
        return pltpu.make_async_copy(hbm_back.at[cols], w_back.at[cols], load_sem.at[1, step])

    for step in range(steps):
        load_in(step).start()
        load_back(step).start()
    total[...] = jnp.zeros_like(total)

    def forward(step, carry):
        cols = pl.ds(pl.multiple_of(step * size, size), size)
        load_in(step).wait()
        inner = dot(second_norm[...], w_in[:, cols])
        phi = 0.5 + 0.5 * lax.erf(inner * (0.5**0.5))
        bell = jnp.exp(inner * inner * -0.5) * (0.5 / jnp.pi) ** 0.5
        value = (inner * phi).astype(LOW)
        activated[:, cols] = value
        slope[:, cols] = (phi + inner * bell).astype(LOW)
        load_back(step).wait()
        total[...] += dot(value, w_back[cols, :])
        return carry

    lax.fori_loop(0, steps, forward, 0)
    mask = valid_rows(sq, length, rows)
    branch = jnp.zeros((1, width), WIDE)
    d_gain = jnp.zeros((1, width), WIDE)
    d_shift = jnp.zeros((1, width), WIDE)
    for stream_id in range(3):
        part = slice(stream_id * rows, (stream_id + 1) * rows)
        ffn = total[part, :]
        branch = branch + sum_squares(ffn, mask)
        resid = second_norm[part, :].astype(WIDE) + ffn
        centred, scale = norm_stats(resid)
        normed = centred * scale * gain_three[...] + shift_three[...]
        output[part, :] = (normed * mask).astype(LOW)
        incoming = cotangent[part, :].astype(WIDE) * mask
        back, gain_part, shift_part = norm_backward(resid, gain_three[...], incoming)
        d_gain, d_shift = d_gain + gain_part, d_shift + shift_part
        total[part, :] = back
        d_ffn[part, :] = back.astype(LOW)
    stats[...] = branch
    grads[2:3, :] = d_gain
    grads[3:4, :] = d_shift

    def backward(step, carry):
        cols = pl.ds(pl.multiple_of(step * size, size), size)
        d_act = dot(d_ffn[...], w_back[cols, :], NT)
        d_in = (d_act * slope[:, cols].astype(WIDE)).astype(LOW)
        d_inner[:, cols] = d_in
        total[...] += dot(d_in, w_in[:, cols], NT)
        return carry

    lax.fori_loop(0, steps, backward, 0)
    d_gain = jnp.zeros((1, width), WIDE)
    d_shift = jnp.zeros((1, width), WIDE)
    for stream_id in range(3):
        part = slice(stream_id * rows, (stream_id + 1) * rows)
        back, gain_part, shift_part = norm_backward(
            resid_two[part, :], gain_two[...], total[part, :]
        )
        d_gain, d_shift = d_gain + gain_part, d_shift + shift_part
        d_resid[part, :] = back
        d_crossed[part, :] = back.astype(LOW)
    grads[0:1, :] = d_gain
    grads[1:2, :] = d_shift


def middle(second_norm, resid_two, cotangent, length, gain_two, gain_three, shift_three, w_in, w_back):
    tokens, width = second_norm.shape
    hidden = w_in.shape[1]
    shape = jax.ShapeDtypeStruct
    vmem = pl.BlockSpec(memory_space=pltpu.VMEM)
    smem = pl.BlockSpec(memory_space=pltpu.SMEM)
    hbm = pl.BlockSpec(memory_space=pl.ANY)
    return pl.pallas_call(
        middle_kernel,
        out_shape=[
            shape((tokens, width), LOW),
            shape((tokens, hidden), LOW),
            shape((tokens, width), LOW),
            shape((tokens, hidden), LOW),
            shape((tokens, width), WIDE),
            shape((tokens, width), LOW),
            shape((4, width), WIDE),
            shape((1, width), WIDE),
        ],
        in_specs=[vmem] * 3 + [smem] + [vmem] * 3 + [hbm] * 2,
        out_specs=[vmem] * 8,
        scratch_shapes=[
            pltpu.VMEM(w_in.shape, LOW),
            pltpu.VMEM(w_back.shape, LOW),
            pltpu.VMEM((tokens, hidden), LOW),
            pltpu.VMEM((tokens, width), WIDE),
            pltpu.SemaphoreType.DMA((2, hidden // 512)),
        ],
        compiler_params=pltpu.CompilerParams(vmem_limit_bytes=60 << 20),
    )(second_norm, resid_two, cotangent, length, gain_two, gain_three, shift_three, w_in, w_back)


def rear_kernel(*refs):
    d_crossed, d_resid_two, cross_key, cross_value, cross_query, resid_one = refs[:6]
    main_key, main_value, query, own_key, own_value, own_probs, gain_one = refs[6:13]
    hbm_weights = refs[13:21]
    cross_probs, probs = refs[21:23]
    (d_cross_query, d_cross_key, d_cross_value, encoded_grad, d_attended) = refs[23:28]
    (d_query, d_key, d_value, stream_grad, grads, bias_sums, own_sums) = refs[28:35]
    weights = refs[35:43]
    kept, d_context, d_resid, parts, near_in, far_in = refs[43:49]
    weight_sem, kept_sem, core_s, core_r, far_s, far_r = refs[49:]
    c_out, c_query, w_out, w_query, w_key, w_value, c_key, c_value = weights
    dp, sq, core, ypos, core_peer, y_peer = places()
    tokens, width = query.shape
    rows = tokens // 3
    full = main_key.shape[0]
    pairs = HEADS // 2
    loads = [
        pltpu.make_async_copy(src, dst, weight_sem.at[index])
        for index, (src, dst) in enumerate(zip(hbm_weights, weights))
    ]

    def fetch(pair, source, base):
        slot = (pair + base) % 2
        return pltpu.make_async_copy(source.at[pair], kept.at[slot], kept_sem.at[slot])

    loads[0].start()
    fetch(0, cross_probs, 0).start()
    for load in loads[1:]:
        load.start()
    greet([core_peer, y_peer])
    loads[0].wait()

    def back_to(dst, left, weight, scale=None):
        def body(cols):
            dst[:, cols] = dot(left[...], weight[cols, :], NT).astype(dst.dtype)

        tiles(width // 256, 256, body)

    back_to(d_context, d_crossed, c_out)

    def core_copy(index):
        view = parts.at[index].reshape(2, 2, rows, width)
        return remote_copy(
            view.at[:, 1 - core], near_in.at[index], core_s.at[index], core_r.at[index], core_peer
        )

    def far_copy(index):
        return remote_copy(
            near_in.at[index, 1 - ypos], far_in.at[index], far_s.at[index], far_r.at[index], y_peer
        )

    def near_sum(index):
        core_copy(index).wait_recv()
        for side in range(2):
            mine = parts[index, side * 2 + core].astype(WIDE)
            near_in[index, side] = (near_in[index, side].astype(WIDE) + mine).astype(LOW)
        far_copy(index).start()

    def far_sum(index):
        far_copy(index).wait_recv()
        return (near_in[index, ypos].astype(WIDE) + far_in[index].astype(WIDE)).astype(LOW)

    def store_part(index, cols, block):
        for part in range(full // rows):
            parts[index, part, :, cols] = block[part * rows : (part + 1) * rows].astype(LOW)

    def cross_pair(pair, carry):
        fetch(pair, cross_probs, 0).wait()

        @pl.when(pair + 1 < pairs)
        def _():
            fetch(pair + 1, cross_probs, 0).start()

        slot = pair % 2
        cols = pl.ds(pl.multiple_of(pair * 128, 128), 128)
        values = cross_value[:, cols]
        key_t = flip(cross_key[:, cols]).astype(LOW)
        queries, d_ctx = cross_query[:, cols], d_context[:, cols]
        d_ctx_t = flip(d_ctx)
        d_query_t, d_scores = [], []
        for side in range(2):
            span = slice(side * HEAD_DIM, (side + 1) * HEAD_DIM)
            d_prob = dot(values, half_rows(d_ctx_t, side))
            prob = kept[slot, side].astype(WIDE)
            delta = jnp.sum(prob * d_prob, axis=0, keepdims=True)
            d_score = (prob * (d_prob - delta)).astype(LOW)
            d_query_t.append(dot(key_t[span], d_score))
            d_scores.append(d_score)
        d_cross_query[:, cols] = (
            jnp.transpose(jnp.concatenate(d_query_t, axis=0)) * 0.125
        ).astype(LOW)
        both = jnp.concatenate(d_scores, axis=1)
        split = jnp.concatenate([half_lanes(queries, 0), half_lanes(queries, 1)], axis=0)
        store_part(0, cols, dot(both, split))
        both = jnp.concatenate([kept[slot, 0], kept[slot, 1]], axis=1)
        split = jnp.concatenate([half_lanes(d_ctx, 0), half_lanes(d_ctx, 1)], axis=0)
        store_part(1, cols, dot(both, split))
        return carry

    lax.fori_loop(0, pairs, cross_pair, 0)
    fetch(0, probs, 0).start()
    core_copy(0).start()
    core_copy(1).start()
    loads[1].wait()
    back_to(d_resid, d_cross_query, c_query)
    d_gain = jnp.zeros((1, width), WIDE)
    d_shift = jnp.zeros((1, width), WIDE)
    for stream_id in range(3):
        part = slice(stream_id * rows, (stream_id + 1) * rows)
        back, gain_part, shift_part = norm_backward(
            resid_one[part, :], gain_one[...], d_resid[part, :] + d_resid_two[part, :]
        )
        d_gain, d_shift = d_gain + gain_part, d_shift + shift_part
        d_resid[part, :] = back
        d_attended[part, :] = back.astype(LOW)
    grads[0:1, :] = d_gain
    grads[1:2, :] = d_shift
    near_sum(0)
    near_sum(1)
    loads[2].wait()
    back_to(d_context, d_attended, w_out)
    line = lax.broadcasted_iota(jnp.int32, (rows, rows), 0)
    turned = (line + lax.broadcasted_iota(jnp.int32, (rows, rows), 1) == rows - 1).astype(LOW)

    def self_pair(pair, carry):
        fetch(pair, probs, 0).wait()

        @pl.when(pair + 1 < pairs)
        def _():
            fetch(pair + 1, probs, 0).start()

        slot = pair % 2
        cols = pl.ds(pl.multiple_of(pair * 128, 128), 128)
        values = main_value[:, cols]
        key_t = flip(main_key[:, cols]).astype(LOW)
        queries, d_ctx = query[:, cols], d_context[:, cols]
        d_ctx_t, query_t = flip(d_ctx), flip(queries)
        own_key_t, own_value_t = flip(own_key[:, cols]), flip(own_value[:, cols])
        own_product = d_ctx_t[:, rows:] * own_value_t
        d_query_t, d_scores, d_own_key, d_own_value = [], [], [], []
        for side in range(2):
            head = 2 * pair + side
            span = slice(side * HEAD_DIM, (side + 1) * HEAD_DIM)
            d_prob = dot(values, half_rows(d_ctx_t, side))
            prob = kept[slot, side].astype(WIDE)
            prob_own = own_probs[head][:, rows:]
            d_prob_own = jnp.sum(own_product[span], axis=0, keepdims=True)
            delta = jnp.sum(prob * d_prob, axis=0, keepdims=True)
            delta = jnp.concatenate(
                [delta[:, :rows], delta[:, rows:] + prob_own * d_prob_own], axis=1
            )
            d_score = (prob * (d_prob - delta)).astype(LOW)
            d_own = (prob_own * (d_prob_own - delta[:, rows:])).astype(LOW).astype(WIDE)
            own_sums[head] = d_own
            mixed = dot(key_t[span], d_score)
            d_query_t.append(
                jnp.concatenate(
                    [mixed[:, :rows], mixed[:, rows:] + d_own * own_key_t[span]], axis=1
                )
            )
            d_scores.append(d_score)
            d_own_key.append(d_own * query_t[span, rows:])
            d_own_value.append(prob_own * d_ctx_t[span, rows:])
            wide = d_score.astype(WIDE)
            summed = wide[:, :rows] + wide[:, rows : 2 * rows] + wide[:, 2 * rows :]
            mirrored = dot(summed.astype(LOW), turned)
            for block in range(full // rows):
                piece = mirrored[block * rows : (block + 1) * rows]
                piece = jnp.concatenate([piece, jnp.zeros_like(piece)], axis=1)
                aligned = pltpu.roll(piece, 0, 1, stride=1, stride_axis=0)
                bias_sums[head, block : block + 1, :] = jnp.sum(aligned, axis=0, keepdims=True)
        d_query[:, cols] = (jnp.transpose(jnp.concatenate(d_query_t, axis=0)) * 0.125).astype(LOW)
        d_key[rows:, cols] = jnp.transpose(jnp.concatenate(d_own_key, axis=0)).astype(LOW)
        d_value[rows:, cols] = jnp.transpose(jnp.concatenate(d_own_value, axis=0)).astype(LOW)
        both = jnp.concatenate(d_scores, axis=1)
        split = jnp.concatenate([half_lanes(queries, 0), half_lanes(queries, 1)], axis=0)
        store_part(2, cols, dot(both, split))
        both = jnp.concatenate([kept[slot, 0], kept[slot, 1]], axis=1)
        split = jnp.concatenate([half_lanes(d_ctx, 0), half_lanes(d_ctx, 1)], axis=0)
        store_part(3, cols, dot(both, split))
        return carry

    lax.fori_loop(0, pairs, self_pair, 0)
    core_copy(2).start()
    core_copy(3).start()
    d_cross_key[...] = far_sum(0)
    d_cross_value[...] = far_sum(1)
    loads[6].wait()
    loads[7].wait()

    def source_body(cols):
        grad = dot(d_cross_key[...], c_key[cols, :], NT)
        grad = grad + dot(d_cross_value[...], c_value[cols, :], NT)
        encoded_grad[:, cols] = grad.astype(LOW)

    tiles(width // 256, 256, source_body)
    near_sum(2)
    near_sum(3)
    loads[3].wait()

    def query_body(cols):
        d_resid[:, cols] += dot(d_query[...], w_query[cols, :], NT)

    tiles(width // 256, 256, query_body)
    d_key[:rows, :] = far_sum(2)
    d_value[:rows, :] = far_sum(3)
    loads[4].wait()
    loads[5].wait()

    def last_body(cols):
        grad = d_resid[:, cols] + dot(d_key[...], w_key[cols, :], NT)
        grad = grad + dot(d_value[...], w_value[cols, :], NT)
        stream_grad[:, cols] = grad.astype(LOW)

    tiles(width // 256, 256, last_body)
    for index in range(4):
        core_copy(index).wait_send()
        far_copy(index).wait_send()


def rear(acts, gain_one, weights, cross_probs, probs):
    d_crossed, d_resid_two, cross_key = acts[:3]
    tokens, width = d_crossed.shape
    full = cross_key.shape[0]
    rows = tokens // 3
    shape = jax.ShapeDtypeStruct
    vmem = pl.BlockSpec(memory_space=pltpu.VMEM)
    hbm = pl.BlockSpec(memory_space=pl.ANY)
    sem = pltpu.SemaphoreType.DMA
    blocks = full // rows
    return pl.pallas_call(
        rear_kernel,
        out_shape=[
            shape((tokens, width), LOW),
            shape((rows, width), LOW),
            shape((rows, width), LOW),
            shape((rows, width), LOW),
            shape((tokens, width), LOW),
            shape((tokens, width), LOW),
            shape((tokens, width), LOW),
            shape((tokens, width), LOW),
            shape((tokens, width), LOW),
            shape((2, width), WIDE),
            shape((HEADS, blocks, 2 * rows), WIDE),
            shape((HEADS, 1, tokens - rows), WIDE),
        ],
        in_specs=[vmem] * 13 + [hbm] * 10,
        out_specs=[vmem] * 12,
        scratch_shapes=[pltpu.VMEM(w.shape, LOW) for w in weights]
        + [
            pltpu.VMEM((2, 2, full, tokens), LOW),
            pltpu.VMEM((tokens, width), LOW),
            pltpu.VMEM((tokens, width), WIDE),
            pltpu.VMEM((4, blocks, rows, width), LOW),
            pltpu.VMEM((4, 2, rows, width), LOW),
            pltpu.VMEM((4, rows, width), LOW),
            sem((8,)),
            sem((2,)),
            sem((4,)),
            sem((4,)),
            sem((4,)),
            sem((4,)),
        ],
        compiler_params=pltpu.CompilerParams(
            collective_id=2, has_side_effects=True, vmem_limit_bytes=60 << 20
        ),
    )(*acts, gain_one, *weights, cross_probs, probs)


MESH_ID = pl.DeviceIdType.MESH


def tile_dot(x_ref, x_start, y_ref, y_start, rows):
    left = x_ref[:, pl.ds(x_start, rows)]
    right = y_ref[:, pl.ds(y_start, COLS)]
    return lax.dot_general(
        left, right, (((0,), (0,)), ((), ())), preferred_element_type=jnp.float32
    )


def reduce_kernel(units, num_in, num_out, dp_size, *refs):
    ins, small_ref = refs[:num_in], refs[num_in]
    outs, small_out = refs[num_in + 1 : num_in + 1 + num_out], refs[num_in + 1 + num_out]
    sent, core_in, first_y, first_x, second, third, small_in = refs[num_in + num_out + 2 : -10]
    sems = refs[-10:]
    core_s, core_r, one_s, one_r, two_s, two_r, three_s, three_r, small_s, small_r = sems
    dp, sq = lax.axis_index("dp"), lax.axis_index("seq")
    core, ypos = sq % 2, sq // 2
    xpos, zpos = dp % 2, dp // 2
    depth = dp_size // 2
    chunk = 1024 // dp_size
    core_peer = (dp, sq + 1 - 2 * core)
    y_peer = (dp, sq + 2 - 4 * ypos)
    x_peer = (dp + 1 - 2 * xpos, sq)

    def z_peer(step):
        return ((zpos + step) % depth * 2 + xpos, sq)

    barrier = pltpu.get_barrier_semaphore()
    for peer in [core_peer, y_peer, x_peer] + [z_peer(step) for step in range(1, depth)]:
        pl.semaphore_signal(barrier, inc=1, device_id=peer, device_id_type=MESH_ID)
    pl.semaphore_wait(barrier, 2 + depth)

    def remote(src, dst, send_sem, recv_sem, peer):
        return pltpu.make_async_remote_copy(
            src_ref=src,
            dst_ref=dst,
            send_sem=send_sem,
            recv_sem=recv_sem,
            device_id=peer,
            device_id_type=MESH_ID,
        )

    def half_dots(unit, half, write):
        x_id, y_id, kind, part = units[unit]
        x_ref, y_ref = ins[x_id], ins[y_id]
        rows = chunk if kind == "back" else 256

        def body(step, carry):
            tile, side = step // 2, step % 2
            block = side * 2 + half
            x_start = tile * 256
            y_start = block * COLS
            if kind == "in":
                y_start = block * 1024 + part * COLS
            if kind == "back":
                x_start = tile * (4 * chunk) + part * chunk
            write(
                side,
                pl.ds(pl.multiple_of(tile * rows, rows), rows),
                tile_dot(
                    x_ref,
                    pl.multiple_of(x_start, 128),
                    y_ref,
                    pl.multiple_of(y_start, COLS),
                    rows,
                ),
            )
            return carry

        lax.fori_loop(0, 2 * (1024 // rows), body, 0)

    def core_copy(unit):
        return remote(
            sent.at[unit % SLOTS], core_in.at[unit], core_s.at[unit], core_r.at[unit], core_peer
        )

    def one_copy(unit):
        half = unit // 2
        if unit % 2 == 0:
            return remote(
                core_in.at[unit, 1 - ypos], first_y.at[half], one_s.at[unit], one_r.at[unit], y_peer
            )
        source = core_in.at[unit].reshape(2, depth, 2, chunk, COLS)
        return remote(
            source.at[:, :, 1 - xpos], first_x.at[half], one_s.at[unit], one_r.at[unit], x_peer
        )

    def two_copy(unit):
        half = unit // 2
        if unit % 2 == 0:
            source = first_y.at[half].reshape(depth, 2, chunk, COLS)
            return remote(
                source.at[:, 1 - xpos], second.at[unit], two_s.at[unit], two_r.at[unit], x_peer
            )
        return remote(
            first_x.at[half, 1 - ypos], second.at[unit], two_s.at[unit], two_r.at[unit], y_peer
        )

    def three_copy(unit, step):
        return remote(
            second.at[unit, (zpos + step) % depth],
            third.at[unit, step - 1],
            three_s.at[unit, step - 1],
            three_r.at[unit, step - 1],
            z_peer(step),
        )

    def products(unit):
        slot = unit % SLOTS
        if unit >= SLOTS:
            core_copy(unit - SLOTS).wait_send()

        def write(side, rows, value):
            sent[slot, side, rows, :] = value.astype(jnp.bfloat16)

        half_dots(unit, 1 - core, write)
        core_copy(unit).start()

    def core_sum(unit):
        core_copy(unit).wait_recv()

        def write(side, rows, value):
            old = core_in[unit, side, rows, :].astype(jnp.float32)
            core_in[unit, side, rows, :] = (value + old).astype(jnp.bfloat16)

        half_dots(unit, core, write)
        one_copy(unit).start()

    def plus(left, right):
        return (left.astype(jnp.float32) + right.astype(jnp.float32)).astype(jnp.bfloat16)

    def one_sum(unit):
        one_copy(unit).wait_recv()
        half = unit // 2
        if unit % 2 == 0:

            def body(step, carry):
                rows = pl.ds(pl.multiple_of(step * 128, 128), 128)
                first_y[half, rows, :] = plus(first_y[half, rows, :], core_in[unit, ypos, rows, :])
                return carry

            lax.fori_loop(0, 8, body, 0)
        else:
            def body(step, carry):
                side, layer = step // depth, step % depth
                rows = pl.ds(pl.multiple_of((layer * 2 + xpos) * chunk, chunk), chunk)
                first_x[half, side, layer] = plus(
                    first_x[half, side, layer], core_in[unit, side, rows, :]
                )
                return carry

            lax.fori_loop(0, 2 * depth, body, 0)
        two_copy(unit).start()

    def two_sum(unit):
        two_copy(unit).wait_recv()
        half = unit // 2

        def body(layer, carry):
            if unit % 2 == 0:
                rows = pl.ds(pl.multiple_of((layer * 2 + xpos) * chunk, chunk), chunk)
                old = first_y[half, rows, :]
            else:
                old = first_x[half, ypos, layer]
            second[unit, layer] = plus(second[unit, layer], old)
            return carry

        lax.fori_loop(0, depth, body, 0)

        def send(step, carry):
            three_copy(unit, step).start()
            return carry

        lax.fori_loop(1, depth, send, 0)

    def last_sum(unit):
        def body(step, total):
            three_copy(unit, step).wait_recv()
            return total + third[unit, step - 1].astype(jnp.float32)

        total = lax.fori_loop(1, depth, body, second[unit, zpos].astype(jnp.float32))
        x_id, y_id, kind, part = units[unit]
        if kind == "in":
            outs[8][:, part * COLS : (part + 1) * COLS] = total
        elif kind in ("back", "parted"):
            outs[9][part * chunk : (part + 1) * chunk, :] = total
        else:
            outs[part][...] = total

    bits = 0
    while (1 << bits) < dp_size:
        bits += 1
    small_out[...] = small_ref[...]

    def small_copy(step):
        if step == 0:
            peer = core_peer
        elif step == 1:
            peer = y_peer
        else:
            flip = 1 << (step - 2)
            peer = (dp + flip - 2 * flip * (dp // flip % 2), sq)
        return remote(small_out, small_in.at[step], small_s.at[step], small_r.at[step], peer)

    def small_step(step):
        small_copy(step).wait()
        small_out[...] = small_out[...] + small_in[step]

    count = len(units)
    pairs = count // 2
    small_copy(0).start()
    for turn in range(pairs + 5):
        for unit in (2 * turn, 2 * turn + 1):
            if unit < count:
                products(unit)
        for unit in (2 * turn - 2, 2 * turn - 1):
            if 0 <= unit < count:
                core_sum(unit)
        for unit in (2 * turn - 4, 2 * turn - 3):
            if 0 <= unit < count:
                one_sum(unit)
        for unit in (2 * turn - 6, 2 * turn - 5):
            if 0 <= unit < count:
                two_sum(unit)
        for unit in (2 * turn - 8, 2 * turn - 7):
            if 0 <= unit < count:
                last_sum(unit)
        if turn < bits + 2:
            small_step(turn)
            if turn + 1 < bits + 2:
                small_copy(turn + 1).start()
    for step in range(pairs + 5, bits + 2):
        small_step(step)
        if step + 1 < bits + 2:
            small_copy(step + 1).start()
    for unit in range(count):
        if unit >= count - SLOTS:
            core_copy(unit).wait_send()
        one_copy(unit).wait_send()
        two_copy(unit).wait_send()

        def drain(step, carry):
            three_copy(unit, step).wait_send()
            return carry

        lax.fori_loop(1, depth, drain, 0)


def reduce_grads(units, operands, small, dp_size):
    count = len(units)
    depth, chunk = dp_size // 2, 1024 // dp_size
    bits = dp_size.bit_length() - 1
    low = jnp.bfloat16
    out_shapes = [jax.ShapeDtypeStruct((chunk, COLS), jnp.float32)] * 8
    out_shapes.append(jax.ShapeDtypeStruct((chunk, 4 * COLS), jnp.float32))
    out_shapes.append(jax.ShapeDtypeStruct((4 * chunk, COLS), jnp.float32))
    out_shapes.append(jax.ShapeDtypeStruct(small.shape, jnp.float32))
    sem = pltpu.SemaphoreType.DMA
    vmem = pl.BlockSpec(memory_space=pltpu.VMEM)
    return pl.pallas_call(
        functools.partial(reduce_kernel, units, len(operands), 10, dp_size),
        out_shape=out_shapes,
        in_specs=[vmem] * (len(operands) + 1),
        out_specs=[vmem] * 11,
        scratch_shapes=[
            pltpu.VMEM((SLOTS, 2, 1024, COLS), low),
            pltpu.VMEM((count, 2, 1024, COLS), low),
            pltpu.VMEM((count // 2, 1024, COLS), low),
            pltpu.VMEM((count // 2, 2, depth, chunk, COLS), low),
            pltpu.VMEM((count, depth, chunk, COLS), low),
            pltpu.VMEM((count, depth - 1, chunk, COLS), low),
            pltpu.VMEM((bits + 2,) + small.shape, jnp.float32),
            sem((count,)),
            sem((count,)),
            sem((count,)),
            sem((count,)),
            sem((count,)),
            sem((count,)),
            sem((count, depth - 1)),
            sem((count, depth - 1)),
            sem((bits + 2,)),
            sem((bits + 2,)),
        ],
        compiler_params=pltpu.CompilerParams(
            collective_id=0, has_side_effects=True, vmem_limit_bytes=60 << 20
        ),
    )(*operands, small)


def per_device(
    stream,
    encoded,
    cotangent,
    lengths,
    bucket_table,
    w_query,
    w_key,
    w_value,
    w_out,
    c_query,
    c_key,
    c_value,
    c_out,
    w_in,
    w_back,
    gain_one,
    shift_one,
    gain_two,
    shift_two,
    gain_three,
    shift_three,
    position_bias,
):
    num_rows, num_streams, local_len, model_width = stream.shape
    full_len = local_len * lax.axis_size("seq")
    sq = lax.axis_index("seq")
    dp_size = lax.axis_size("dp")
    chunk = model_width // dp_size
    bucket_ids = jnp.arange(NBUCKET, dtype=jnp.int32)
    exact = lax.Precision.HIGHEST
    table_hot = (bucket_table[:, None] == bucket_ids[None, :]).astype(jnp.float32)
    by_distance = jnp.einsum("db,bh->hd", table_hot, position_bias, precision=exact)
    bias_table = jnp.concatenate([jnp.zeros_like(by_distance), by_distance], axis=1)[:, None, :]
    flat_rows = stream.reshape(-1, model_width)
    source_rows = encoded.reshape(-1, model_width)
    flat_cotangent = cotangent.reshape(-1, model_width)

    def line(values):
        return values.reshape(1, model_width)

    fronts = front(
        stream.reshape(num_streams, local_len, model_width),
        source_rows,
        lengths,
        bias_table,
        (line(gain_one), line(shift_one), line(gain_two), line(shift_two)),
        (w_query, w_key, w_value, w_out, c_query, c_key, c_value, c_out),
    )
    query, own_key, own_value, main_key, main_value, context_low, resid_one, first_norm = fronts[:8]
    cross_query, cross_key, cross_value, cross_low, resid_two, second_norm = fronts[8:14]
    own_probs, front_stats, probs, cross_probs = fronts[14:]
    layer_output, activated, d_ffn_out, d_inner, d_resid_two, d_crossed, mid_grads, ffn_stat = middle(
        second_norm,
        resid_two,
        flat_cotangent,
        lengths,
        line(gain_two),
        line(gain_three),
        line(shift_three),
        w_in,
        w_back,
    )
    rears = rear(
        (
            d_crossed,
            d_resid_two,
            cross_key,
            cross_value,
            cross_query,
            resid_one,
            main_key,
            main_value,
            query,
            own_key,
            own_value,
            own_probs,
        ),
        line(gain_one),
        (c_out, c_query, w_out, w_query, w_key, w_value, c_key, c_value),
        cross_probs,
        probs,
    )
    d_cross_query, d_cross_key, d_cross_value, encoded_grad, d_attended = rears[:5]
    d_query_low, d_keys, d_values, stream_grad, rear_grads, bias_sums, own_sums = rears[5:]

    blocks = full_len // local_len
    place = jnp.arange(2 * local_len, dtype=jnp.int32)
    reach = (sq - jnp.arange(blocks, dtype=jnp.int32))[:, None] * local_len + (
        local_len - 1 - place[None, :]
    )
    first_of = jnp.sum((bucket_table[:, None] < bucket_ids[None, :]).astype(jnp.int32), axis=0)
    next_of = jnp.sum((bucket_table[:, None] <= bucket_ids[None, :]).astype(jnp.int32), axis=0)
    window_hot = (reach[..., None] >= first_of) & (reach[..., None] < next_of)
    table_part = jnp.einsum(
        "hkv,kvb->bh", bias_sums, window_hot.astype(jnp.float32), precision=exact
    )
    own_hot = (bucket_ids == bucket_table[0]).astype(jnp.float32)
    table_part = table_part + own_hot[:, None] * jnp.sum(own_sums, axis=(1, 2))[None, :]
    position = sq * local_len + jnp.arange(local_len)
    count = num_streams * jnp.sum((position < lengths[0]).astype(jnp.float32))
    stats = jnp.concatenate([jnp.sum(front_stats, axis=1), jnp.sum(ffn_stat, axis=1), count[None]])
    tail = jnp.concatenate([table_part.reshape(-1), stats, jnp.zeros((507,), jnp.float32)])
    small = jnp.concatenate([rear_grads, mid_grads, tail[None], jnp.zeros_like(tail)[None]])
    units = []
    operands = [d_ffn_out, second_norm, d_inner, cross_low, d_crossed, first_norm, d_cross_query]
    operands += [source_rows, d_cross_key, d_cross_value, context_low, d_attended]
    operands += [flat_rows, d_query_low, d_keys, d_values]
    if chunk % 128 == 0:
        operands.append(activated)
        for part in range(4):
            units.append((16, 0, "back", part))
    else:
        parted = jnp.transpose(activated.reshape(-1, dp_size, 4, chunk), (2, 0, 1, 3))
        parted = parted.reshape(4, -1, model_width)
        for part in range(4):
            operands.append(parted[part])
            units.append((16 + part, 0, "parted", part))
    for part in range(4):
        units.append((1, 2, "in", part))
    units += [(3, 4, "", 7), (5, 6, "", 4), (7, 8, "", 5), (7, 9, "", 6), (10, 11, "", 3)]
    units += [(12, 13, "", 0), (12, 14, "", 1), (12, 15, "", 2)]
    reduced = reduce_grads(tuple(units), operands, small, dp_size)
    shares, sums = reduced[:10], reduced[10]
    rms = jnp.sqrt(sums[6, 512:516] / (sums[6, 516] * model_width))
    return (
        layer_output.reshape(stream.shape),
        stream_grad.reshape(stream.shape),
        encoded_grad.reshape(encoded.shape),
        shares[0],
        shares[1],
        shares[2],
        shares[3],
        shares[4],
        shares[5],
        shares[6],
        shares[7],
        shares[8],
        shares[9],
        sums[0],
        sums[1],
        sums[2],
        sums[3],
        sums[4],
        sums[5],
        sums[6, :512].reshape(NBUCKET, HEADS),
        rms,
    )


def solution(mesh):
    placed = (
        P("dp", None, "seq", None),
        P("dp", "seq", None),
        P("dp", None, "seq", None),
        P("dp"),
        P(),
        P(),
        P(),
        P(),
        P(),
        P(),
        P(),
        P(),
        P(),
        P(),
        P(),
        P(),
        P(),
        P(),
        P(),
        P(),
        P(),
        P(),
    )
    return jax.shard_map(
        per_device,
        mesh=mesh,
        in_specs=placed,
        out_specs=(
            P("dp", None, "seq", None),
            P("dp", None, "seq", None),
            P("dp", "seq", None),
            P("dp", "seq"),
            P("dp", "seq"),
            P("dp", "seq"),
            P("dp", "seq"),
            P("dp", "seq"),
            P("dp", "seq"),
            P("dp", "seq"),
            P("dp", "seq"),
            P("dp", "seq"),
            P("dp", "seq"),
            P(),
            P(),
            P(),
            P(),
            P(),
            P(),
            P(),
            P(),
        ),
        check_vma=False,
    )
```

time: 616 us -> 363 us (0.59)
  matrix products: 162 us -> 1.91 us
  Pallas kernels: 189 us -> 334 us
  local copies, waits for them, and re-layouts: 146 us -> 15.9 us
  other arithmetic: 67.5 us -> 7.79 us
  waiting for transfers between devices: 27.1 us -> 0 us
  between operations: 17.2 us -> 2.78 us
    dot_general x35 -> x2, matrix products: 162 us -> 1.91 us  [the longest x1 1.08 us: per_device(): jnp.einsum('hkv,kvb->bh', bias_sums, window_hot.astype(jnp.float32), prec...]
    pallas_call x0 -> x3, Pallas kernels: none -> 145 us  [the longest x1 59.2 us: front(): pl.pallas_call(front_kernel, out_shape=outs, in_specs=[vmem, vmem, smem]...]
    eq x1 -> x0, local copies, waits for them, and re-layouts: 37.3 us -> none  [per_device(): one_hot = (buckets[:, :, None] == bucket_ids).astype(jnp.float32)]
    unnamed x217 -> x43, local copies, waits for them, and re-layouts: 44.8 us -> 9.15 us
    reduce_scatter x2 -> x0, waiting for transfers between devices: 26.9 us -> none  [the longest x1 26.9 us: per_device(): lax.psum_scatter(cross_key_part.astype(jnp.bfloat16), 'seq', scatter_dime...]
    reduce_sum x14 -> x5, other arithmetic: 25.5 us -> 4.47 us  [the longest x1 1.3 us: per_device(): jnp.sum(ffn_stat, axis=1)]
    add x4 -> x1, other arithmetic: 20.7 us -> 0.07 us  [per_device(): (sq - jnp.arange(blocks, dtype=jnp.int32))[:, None] * local_len]
    another operation x10 -> x0, local copies, waits for them, and re-layouts: 19.2 us -> none
  transfers between devices with their start and end apart: 8 -> 0, of which waited for: 1 -> 0; matrix products, arithmetic and copies ran while one was open for 36% -> 0% of each run, Pallas kernels for 0% -> 0%
where the time goes in v3:
time: 363 us; the launch traced here: 362 us
  Pallas kernels  334 us (92%)
  local copies, waits for them, and re-layouts  15.9 us (4%)
  other arithmetic  7.79 us (2%)
    pallas_call x1, Pallas kernels, reduce_grads(): pl.pallas_call(functools.partial(reduce_kernel, units, len(operands), 10,...  189 us
    pallas_call x1, Pallas kernels, front(): pl.pallas_call(front_kernel, out_shape=outs, in_specs=[vmem, vmem, smem]...  59.2 us
    pallas_call x1, Pallas kernels, rear(): pl.pallas_call(rear_kernel, out_shape=[shape((tokens, width), LOW), shape...  58.1 us
    pallas_call x1, Pallas kernels, middle(): pl.pallas_call(middle_kernel, out_shape=[shape((tokens, width), LOW), sha...  27.6 us
    unnamed x43, local copies, waits for them, and re-layouts  9.15 us

profile of v3, /device:TPU:0, one launch (start us, length us, event | category | flops | bytes accessed | tf_op | source)
XLA Modules:
  0.0 361.9 jit_solution(12904574633193058617)
XLA Ops:
  0.7 0.0 copy-start
  1.3 0.6 fusion.9
  2.6 1.2 slice.30
  3.8 0.6 compare_convert_fusion.1
  4.4 0.1 pad.4.clone
  4.5 0.8 convert_reduce_fusion.1
  5.3 0.1 broadcast_add_fusion
  5.4 0.0 copy-done
  5.4 0.8 convolution_bitcast_fusion
  6.2 0.7 broadcast_in_dim.8.refs_3_
  6.9 59.2 %shard_map.373 = (bf16[384,1024]{1,0:T(8,128)(2,1)}, bf16[256,1024]{1,0:T(8,128)(2,1)}, bf16[256,1024]{1,0:T(8,128)(2,1)}, bf16[512,1024]{1,0:T(8,128)(2,1)}, bf...) custom-call(bf16[3,128,1024]{2,1,0:T(8,128)(2,1)} %bitcast.36, ...), custom_call_target="tpu_custom_call" | custom-call | tf_op jit(solution)/shard_map/pallas_call | solution.py:347
  66.1 0.8 reduce_sum.59
  67.0 27.6 %shard_map.374 = (bf16[384,1024]{1,0:T(8,128)(2,1)}, bf16[384,4096]{1,0:T(8,128)(2,1)}, bf16[384,1024]{1,0:T(8,128)(2,1)}, bf16[384,4096]{1,0:T(8,128)(2,1)}, f3...) custom-call(bf16[384,1024]{1,0:T(8,128)(2,1)} %get-tuple-element.70.refs_0_.refs_1_, ...), custom_call_target="tpu_custom_call" | custom-call | tf_op jit(solution)/shard_map/pallas_call | solution.py:461
  94.5 1.3 reduce_sum.60
  95.8 58.1 %shard_map.375 = (bf16[384,1024]{1,0:T(8,128)(2,1)}, bf16[128,1024]{1,0:T(8,128)(2,1)}, bf16[128,1024]{1,0:T(8,128)(2,1)}, bf16[128,1024]{1,0:T(8,128)(2,1)}, bf...) custom-call(bf16[384,1024]{1,0:T(8,128)(2,1)} %get-tuple-element.73., ...), custom_call_target="tpu_custom_call" | custom-call | tf_op jit(solution)/shard_map/pallas_call | solution.py:716
  154.0 0.9 reduce_sum.58
  154.9 1.1 fusion
  156.0 0.1 copy.49
  156.1 0.1 reshape.152
  156.1 0.7 concatenate.10
  156.9 0.0 copy-done.14
  156.9 1.4 maximum_maximum_fusion.refs_17_
  158.3 188.7 %shard_map.376 = (f32[128,256]{1,0:T(8,128)}, f32[128,256]{1,0:T(8,128)}, f32[128,256]{1,0:T(8,128)}, f32[128,256]{1,0:T(8,128)}, f32[128,256]{1,0:T(8,128)}, /*...) custom-call(bf16[384,1024]{1,0:T(8,128)(2,1)} %get-tuple-element.89., ...), custom_call_target="tpu_custom_call" | custom-call | tf_op jit(solution)/shard_map/pallas_call | solution.py:1016
  347.0 0.0 copy-start.13
  347.0 0.0 copy-start.12
  347.0 0.0 copy-start.11
  347.0 0.0 copy-start.10
  347.0 0.0 copy-start.9
  347.0 1.4 slice.39
  349.1 1.2 sqrt_bitcast_fusion
  350.3 0.7 slice_reduce_fusion
  351.0 1.7 fusion.10
  352.7 0.1 reshape_squeeze.3
  352.8 0.7 copy.50
  353.5 0.9 copy.66
  354.4 0.7 copy.67
  355.1 0.7 copy.68
  355.7 0.7 copy.69
  356.4 0.7 copy.70
  357.0 0.7 copy.71
  357.7 0.7 copy.72
  358.4 0.7 copy.73
  359.0 0.7 copy.74
  359.7 0.0 copy-done.6
  359.7 0.7 copy.75
  360.3 0.0 copy-done.4
  360.3 0.8 copy.76
  361.1 0.8 copy.77
  (24 shorter events, 0.1 us)
Async XLA Ops:
  0.7 4.7 %copy-start = (f32[32,16]{0,1:T(8,128)S(1)}, f32[32,16]{0,1:T(8,128)}, u32[]{:S(2)}) copy-start(f32[32,16]{0,1:T(8,128)} %param.43) | copy-start | bytes 6148
  95.8 61.0 %copy-start.14 = (f32[4,1024]{1,0:T(4,128)S(1)}, f32[4,1024]{1,0:T(4,128)}, u32[]{:S(2)}) copy-start(f32[4,1024]{1,0:T(4,128)} %get-tuple-element.103) | copy-start | bytes 49156
  158.3 195.2 %copy-start.2 = (bf16[384,1024]{1,0:T(8,128)(2,1)S(1)}, bf16[384,1024]{1,0:T(8,128)(2,1)}, u32[]{:S(2)}) copy-start(bf16[384,1024]{1,0:T(8,128)(2,1)} %get-tuple-element.87) | copy-start | bytes 2359300
  158.3 196.1 %copy-start.5 = (bf16[128,1024]{1,0:T(8,128)(2,1)S(1)}, bf16[128,1024]{1,0:T(8,128)(2,1)}, u32[]{:S(2)}) copy-start(bf16[128,1024]{1,0:T(8,128)(2,1)} %get-tuple-element.88) | copy-start | bytes 786436
  347.0 8.1 %copy-start.13 = (f32[128,256]{1,0:T(8,128)S(1)}, f32[128,256]{1,0:T(8,128)}, u32[]{:S(2)}) copy-start(f32[128,256]{1,0:T(8,128)} %get-tuple-element.214) | copy-start | bytes 393220
  347.0 8.8 %copy-start.12 = (f32[128,256]{1,0:T(8,128)S(1)}, f32[128,256]{1,0:T(8,128)}, u32[]{:S(2)}) copy-start(f32[128,256]{1,0:T(8,128)} %get-tuple-element.215) | copy-start | bytes 393220
  347.0 9.4 %copy-start.11 = (f32[128,256]{1,0:T(8,128)S(1)}, f32[128,256]{1,0:T(8,128)}, u32[]{:S(2)}) copy-start(f32[128,256]{1,0:T(8,128)} %get-tuple-element.216) | copy-start | bytes 393220
  347.0 10.1 %copy-start.10 = (f32[128,256]{1,0:T(8,128)S(1)}, f32[128,256]{1,0:T(8,128)}, u32[]{:S(2)}) copy-start(f32[128,256]{1,0:T(8,128)} %get-tuple-element.217) | copy-start | bytes 393220
  347.0 10.7 %copy-start.9 = (f32[128,256]{1,0:T(8,128)S(1)}, f32[128,256]{1,0:T(8,128)}, u32[]{:S(2)}) copy-start(f32[128,256]{1,0:T(8,128)} %get-tuple-element.218) | copy-start | bytes 393220
  347.0 11.4 %copy-start.8 = (f32[128,256]{1,0:T(8,128)S(1)}, f32[128,256]{1,0:T(8,128)}, u32[]{:S(2)}) copy-start(f32[128,256]{1,0:T(8,128)} %get-tuple-element.219) | copy-start | bytes 393220
  347.0 12.0 %copy-start.7 = (f32[128,256]{1,0:T(8,128)S(1)}, f32[128,256]{1,0:T(8,128)}, u32[]{:S(2)}) copy-start(f32[128,256]{1,0:T(8,128)} %get-tuple-element.220) | copy-start | bytes 393220
  347.0 12.6 %copy-start.6 = (f32[128,256]{1,0:T(8,128)S(1)}, f32[128,256]{1,0:T(8,128)}, u32[]{:S(2)}) copy-start(f32[128,256]{1,0:T(8,128)} %get-tuple-element.221) | copy-start | bytes 393220
  353.5 6.9 %copy-start.4 = (f32[128,1024]{1,0:T(8,128)S(1)}, f32[128,1024]{1,0:T(8,128)}, u32[]{:S(2)}) copy-start(f32[128,1024]{1,0:T(8,128)} %get-tuple-element.222) | copy-start | bytes 1572868
  354.4 6.8 %copy-start.3 = (f32[512,256]{1,0:T(8,128)S(1)}, f32[512,256]{1,0:T(8,128)}, u32[]{:S(2)}) copy-start(f32[512,256]{1,0:T(8,128)} %get-tuple-element.223) | copy-start | bytes 1572868
  354.4 7.6 %copy-start.1 = (f32[32,16]{0,1:T(8,128)S(1)}, f32[32,16]{0,1:T(8,128)}, u32[]{:S(2)}) copy-start(f32[32,16]{0,1:T(8,128)} %param.43) | copy-start | bytes 6148

commit v4 on v3

--- a/solution.py
+++ b/solution.py
@@ -11,7 +11,9 @@
 HEAD_DIM = 64
 NBUCKET = 32
 COLS = 256
-SLOTS = 4
+SLOTS = 3
+RING = 6
+LATE = 8
 epsilon = 1e-05
 masked_score = -1e30
 
@@ -483,48 +485,102 @@
     )(second_norm, resid_two, cotangent, length, gain_two, gain_three, shift_three, w_in, w_back)
 
 
-def rear_kernel(*refs):
-    d_crossed, d_resid_two, cross_key, cross_value, cross_query, resid_one = refs[:6]
-    main_key, main_value, query, own_key, own_value, own_probs, gain_one = refs[6:13]
-    hbm_weights = refs[13:21]
-    cross_probs, probs = refs[21:23]
-    (d_cross_query, d_cross_key, d_cross_value, encoded_grad, d_attended) = refs[23:28]
-    (d_query, d_key, d_value, stream_grad, grads, bias_sums, own_sums) = refs[28:35]
-    weights = refs[35:43]
-    kept, d_context, d_resid, parts, near_in, far_in = refs[43:49]
-    weight_sem, kept_sem, core_s, core_r, far_s, far_r = refs[49:]
-    c_out, c_query, w_out, w_query, w_key, w_value, c_key, c_value = weights
+def rear_kernel(units, dp_size, *refs):
+    d_crossed, cross_query, resid_one, query, own_key, own_value, own_probs, gain_one = refs[:8]
+    d_ffn, second_norm, cross_context, first_norm, mid_grads, mid_stats, window_hot = refs[8:15]
+    hbm_inner, hbm_activated, hbm_context, hbm_stream, hbm_source, hbm_resid = refs[15:21]
+    hbm_sides, hbm_weights = refs[21:25], refs[25:33]
+    cross_probs, probs = refs[33:35]
+    encoded_grad, stream_grad, small_out = refs[35:38]
+    shares, in_share, back_share = refs[38:46], refs[46], refs[47]
+    (d_cross_query, d_cross_key, d_cross_value, d_attended) = refs[48:52]
+    (d_query, d_key, d_value, bias_sums, small_in) = refs[52:57]
+    d_inner, activated = refs[57:59]
+    weights = refs[59:62]
+    kept, d_context, d_resid, parts, near_in, far_in, sides_held = refs[62:69]
+    weight_sem, kept_sem, core_s, core_r, far_s, far_r, small_s, small_r = refs[69:77]
+    held = (0, 1, 2, 0, 1, 2, 1, 2)
+    c_out, c_query, w_out, w_query, w_key, w_value, c_key, c_value = [weights[i] for i in held]
+    chunk = 1024 // dp_size
+
+    def emit(unit, total):
+        part = unit[3]
+        if unit[2] == "in":
+            in_share[:, part * COLS : (part + 1) * COLS] = total
+        elif unit[2] in ("back", "parted"):
+            back_share[part * chunk : (part + 1) * chunk, :] = total
+        else:
+            shares[part][...] = total
+
+    operands = (d_ffn, second_norm, d_inner, activated, cross_context, d_crossed, first_norm)
+    operands += (d_cross_query, d_attended, d_cross_key, d_cross_value, d_query, d_key, d_value)
+    turn, drain = reducer(units, operands, emit, refs[77:], dp_size)
+    small_copy, small_step = small_sums(small_out, small_in, small_s, small_r, dp_size)
     dp, sq, core, ypos, core_peer, y_peer = places()
     tokens, width = query.shape
     rows = tokens // 3
-    full = main_key.shape[0]
+    full = sides_held.shape[1]
+    blocks = full // rows
+    keys_held, values_held = sides_held.at[0], sides_held.at[1]
     pairs = HEADS // 2
     loads = [
-        pltpu.make_async_copy(src, dst, weight_sem.at[index])
-        for index, (src, dst) in enumerate(zip(hbm_weights, weights))
+        pltpu.make_async_copy(src, weights[held[index]], weight_sem.at[index])
+        for index, src in enumerate(hbm_weights)
     ]
+
+    def load_extra(index, src, dst):
+        return pltpu.make_async_copy(src, dst, weight_sem.at[12 + index])
+
+    early = [
+        load_extra(0, hbm_activated, activated),
+        load_extra(1, hbm_inner, d_inner),
+        load_extra(2, hbm_resid, d_resid),
+    ]
+    late = [
+        load_extra(3, hbm_context, activated.at[:, :width]),
+        load_extra(4, hbm_stream, activated.at[:, width : 2 * width]),
+        load_extra(5, hbm_source, activated.at[:rows, 2 * width : 3 * width]),
+    ]
+
+    def load_side(index):
+        return pltpu.make_async_copy(
+            hbm_sides[index], sides_held.at[index % 2], weight_sem.at[8 + index]
+        )
 
     def fetch(pair, source, base):
         slot = (pair + base) % 2
         return pltpu.make_async_copy(source.at[pair], kept.at[slot], kept_sem.at[slot])
 
+    early[0].start()
+    early[1].start()
     loads[0].start()
     fetch(0, cross_probs, 0).start()
-    for load in loads[1:]:
-        load.start()
-    greet([core_peer, y_peer])
+    load_side(0).start()
+    load_side(1).start()
+    loads[1].start()
+    loads[2].start()
+    early[2].start()
+    greet(reduce_peers(dp_size))
+    early[0].wait()
+    early[1].wait()
+    turn(0)
+    turn(1)
     loads[0].wait()
 
-    def back_to(dst, left, weight, scale=None):
+    def back_to(dst, left, weight, add=False):
         def body(cols):
-            dst[:, cols] = dot(left[...], weight[cols, :], NT).astype(dst.dtype)
+            product = dot(left[...], weight[cols, :], NT)
+            if add:
+                product = product + dst[:, cols]
+            dst[:, cols] = product.astype(dst.dtype)
 
         tiles(width // 256, 256, body)
 
     back_to(d_context, d_crossed, c_out)
+    loads[3].start()
 
     def core_copy(index):
-        view = parts.at[index].reshape(2, 2, rows, width)
+        view = parts.at[index % 2].reshape(2, 2, rows, width)
         return remote_copy(
             view.at[:, 1 - core], near_in.at[index], core_s.at[index], core_r.at[index], core_peer
         )
@@ -537,7 +593,7 @@
     def near_sum(index):
         core_copy(index).wait_recv()
         for side in range(2):
-            mine = parts[index, side * 2 + core].astype(WIDE)
+            mine = parts[index % 2, side * 2 + core].astype(WIDE)
             near_in[index, side] = (near_in[index, side].astype(WIDE) + mine).astype(LOW)
         far_copy(index).start()
 
@@ -547,7 +603,7 @@
 
     def store_part(index, cols, block):
         for part in range(full // rows):
-            parts[index, part, :, cols] = block[part * rows : (part + 1) * rows].astype(LOW)
+            parts[index % 2, part, :, cols] = block[part * rows : (part + 1) * rows].astype(LOW)
 
     def cross_pair(pair, carry):
         fetch(pair, cross_probs, 0).wait()
@@ -558,8 +614,8 @@
 
         slot = pair % 2
         cols = pl.ds(pl.multiple_of(pair * 128, 128), 128)
-        values = cross_value[:, cols]
-        key_t = flip(cross_key[:, cols]).astype(LOW)
+        values = values_held[:, cols]
+        key_t = flip(keys_held[:, cols]).astype(LOW)
         queries, d_ctx = cross_query[:, cols], d_context[:, cols]
         d_ctx_t = flip(d_ctx)
         d_query_t, d_scores = [], []
@@ -582,28 +638,46 @@
         store_part(1, cols, dot(both, split))
         return carry
 
-    lax.fori_loop(0, pairs, cross_pair, 0)
+    load_side(0).wait()
+    load_side(1).wait()
+    lax.fori_loop(0, pairs // 2, cross_pair, 0)
+    turn(2)
+    lax.fori_loop(pairs // 2, pairs, cross_pair, 0)
     fetch(0, probs, 0).start()
+    load_side(2).start()
+    load_side(3).start()
     core_copy(0).start()
     core_copy(1).start()
     loads[1].wait()
-    back_to(d_resid, d_cross_query, c_query)
+    early[2].wait()
+    back_to(d_resid, d_cross_query, c_query, True)
+    loads[6].start()
     d_gain = jnp.zeros((1, width), WIDE)
     d_shift = jnp.zeros((1, width), WIDE)
     for stream_id in range(3):
         part = slice(stream_id * rows, (stream_id + 1) * rows)
         back, gain_part, shift_part = norm_backward(
-            resid_one[part, :], gain_one[...], d_resid[part, :] + d_resid_two[part, :]
+            resid_one[part, :], gain_one[...], d_resid[part, :]
         )
         d_gain, d_shift = d_gain + gain_part, d_shift + shift_part
         d_resid[part, :] = back
         d_attended[part, :] = back.astype(LOW)
-    grads[0:1, :] = d_gain
-    grads[1:2, :] = d_shift
+    lines = [d_gain, d_shift] + [mid_grads[row : row + 1, :] for row in range(4)]
+    for row, line in enumerate(lines):
+        for piece in range(8):
+            small_out[8 * row + piece : 8 * row + piece + 1, :] = line[
+                :, 128 * piece : 128 * (piece + 1)
+            ]
+    small_out[64:72, :] = mid_stats[...]
+    small_out[72:80, :] = jnp.zeros((8, 128), WIDE)
     near_sum(0)
     near_sum(1)
+    turn(3)
     loads[2].wait()
     back_to(d_context, d_attended, w_out)
+    loads[7].start()
+    core_copy(0).wait_send()
+    core_copy(1).wait_send()
     line = lax.broadcasted_iota(jnp.int32, (rows, rows), 0)
     turned = (line + lax.broadcasted_iota(jnp.int32, (rows, rows), 1) == rows - 1).astype(LOW)
 
@@ -616,8 +690,8 @@
 
         slot = pair % 2
         cols = pl.ds(pl.multiple_of(pair * 128, 128), 128)
-        values = main_value[:, cols]
-        key_t = flip(main_key[:, cols]).astype(LOW)
+        values = values_held[:, cols]
+        key_t = flip(keys_held[:, cols]).astype(LOW)
         queries, d_ctx = query[:, cols], d_context[:, cols]
         d_ctx_t, query_t = flip(d_ctx), flip(queries)
         own_key_t, own_value_t = flip(own_key[:, cols]), flip(own_value[:, cols])
@@ -636,7 +710,7 @@
             )
             d_score = (prob * (d_prob - delta)).astype(LOW)
             d_own = (prob_own * (d_prob_own - delta[:, rows:])).astype(LOW).astype(WIDE)
-            own_sums[head] = d_own
+            bias_sums[head, blocks : blocks + 1, :] = d_own
             mixed = dot(key_t[span], d_score)
             d_query_t.append(
                 jnp.concatenate(
@@ -665,11 +739,20 @@
         store_part(3, cols, dot(both, split))
         return carry
 
-    lax.fori_loop(0, pairs, self_pair, 0)
+    load_side(2).wait()
+    load_side(3).wait()
+    lax.fori_loop(0, pairs // 2, self_pair, 0)
+    turn(4)
+    for load in late:
+        load.start()
+    lax.fori_loop(pairs // 2, pairs, self_pair, 0)
     core_copy(2).start()
     core_copy(3).start()
     d_cross_key[...] = far_sum(0)
     d_cross_value[...] = far_sum(1)
+    for load in late:
+        load.wait()
+    turn(5)
     loads[6].wait()
     loads[7].wait()
 
@@ -679,6 +762,8 @@
         encoded_grad[:, cols] = grad.astype(LOW)
 
     tiles(width // 256, 256, source_body)
+    loads[4].start()
+    loads[5].start()
     near_sum(2)
     near_sum(3)
     loads[3].wait()
@@ -687,8 +772,19 @@
         d_resid[:, cols] += dot(d_query[...], w_query[cols, :], NT)
 
     tiles(width // 256, 256, query_body)
+    turn(6)
+    table = jnp.zeros((HEADS, 128), WIDE)
+    for block in range(blocks + 1):
+        rest = bias_sums[:, block, :]
+        for _ in range(3):
+            part = rest.astype(LOW)
+            rest = rest - part.astype(WIDE)
+            table = table + dot(part, window_hot[block])
+    small_out[48:64, :] = table
+    small_copy(0).start()
     d_key[:rows, :] = far_sum(2)
     d_value[:rows, :] = far_sum(3)
+    turn(7)
     loads[4].wait()
     loads[5].wait()
 
@@ -699,112 +795,122 @@
 
     tiles(width // 256, 256, last_body)
     for index in range(4):
-        core_copy(index).wait_send()
+        if index >= 2:
+            core_copy(index).wait_send()
         far_copy(index).wait_send()
-
-
-def rear(acts, gain_one, weights, cross_probs, probs):
-    d_crossed, d_resid_two, cross_key = acts[:3]
-    tokens, width = d_crossed.shape
-    full = cross_key.shape[0]
+    last = len(units) // 2 + 4
+    for index in range(8, last):
+        turn(index)
+        if index - 8 <= dp_size.bit_length():
+            small_step(index - 8)
+    for step in range(last - 8, dp_size.bit_length() + 1):
+        small_step(step)
+    drain()
+
+
+def rear(acts, hbm_acts, sides, weights, cross_probs, probs, units, dp_size):
+    tokens, width = acts[0].shape
+    full = sides[0].shape[0]
     rows = tokens // 3
     shape = jax.ShapeDtypeStruct
     vmem = pl.BlockSpec(memory_space=pltpu.VMEM)
     hbm = pl.BlockSpec(memory_space=pl.ANY)
     sem = pltpu.SemaphoreType.DMA
     blocks = full // rows
+    chunk = width // dp_size
+    steps = dp_size.bit_length() + 1
     return pl.pallas_call(
-        rear_kernel,
+        functools.partial(rear_kernel, units, dp_size),
         out_shape=[
-            shape((tokens, width), LOW),
-            shape((rows, width), LOW),
-            shape((rows, width), LOW),
             shape((rows, width), LOW),
             shape((tokens, width), LOW),
-            shape((tokens, width), LOW),
-            shape((tokens, width), LOW),
-            shape((tokens, width), LOW),
-            shape((tokens, width), LOW),
-            shape((2, width), WIDE),
-            shape((HEADS, blocks, 2 * rows), WIDE),
-            shape((HEADS, 1, tokens - rows), WIDE),
-        ],
-        in_specs=[vmem] * 13 + [hbm] * 10,
-        out_specs=[vmem] * 12,
-        scratch_shapes=[pltpu.VMEM(w.shape, LOW) for w in weights]
+            shape((80, 128), WIDE),
+        ]
+        + [shape((chunk, COLS), WIDE)] * 8
+        + [shape((chunk, 4 * COLS), WIDE), shape((4 * chunk, COLS), WIDE)],
+        in_specs=[vmem] * len(acts) + [hbm] * (len(hbm_acts) + 14),
+        out_specs=[vmem] * 13,
+        scratch_shapes=[
+            pltpu.VMEM((tokens, width), LOW),
+            pltpu.VMEM((rows, width), LOW),
+            pltpu.VMEM((rows, width), LOW),
+            pltpu.VMEM((tokens, width), LOW),
+            pltpu.VMEM((tokens, width), LOW),
+            pltpu.VMEM((tokens, width), LOW),
+            pltpu.VMEM((tokens, width), LOW),
+            pltpu.VMEM((HEADS, blocks + 1, 2 * rows), WIDE),
+            pltpu.VMEM((steps, 80, 128), WIDE),
+            pltpu.VMEM((tokens, 4 * width), LOW),
+            pltpu.VMEM((tokens, 4 * width), LOW),
+        ]
+        + [pltpu.VMEM(w.shape, LOW) for w in weights[:3]]
         + [
             pltpu.VMEM((2, 2, full, tokens), LOW),
             pltpu.VMEM((tokens, width), LOW),
             pltpu.VMEM((tokens, width), WIDE),
-            pltpu.VMEM((4, blocks, rows, width), LOW),
+            pltpu.VMEM((2, blocks, rows, width), LOW),
             pltpu.VMEM((4, 2, rows, width), LOW),
             pltpu.VMEM((4, rows, width), LOW),
-            sem((8,)),
+            pltpu.VMEM((2, full, width), LOW),
+            sem((18,)),
             sem((2,)),
             sem((4,)),
             sem((4,)),
             sem((4,)),
             sem((4,)),
-        ],
+            sem((steps,)),
+            sem((steps,)),
+        ]
+        + reduce_buffers(len(units), dp_size),
         compiler_params=pltpu.CompilerParams(
-            collective_id=2, has_side_effects=True, vmem_limit_bytes=60 << 20
+            collective_id=2, has_side_effects=True, vmem_limit_bytes=63 << 20
         ),
-    )(*acts, gain_one, *weights, cross_probs, probs)
+    )(*acts, *hbm_acts, *sides, *weights, cross_probs, probs)
 
 
 MESH_ID = pl.DeviceIdType.MESH
 
 
-def tile_dot(x_ref, x_start, y_ref, y_start, rows):
-    left = x_ref[:, pl.ds(x_start, rows)]
-    right = y_ref[:, pl.ds(y_start, COLS)]
+def tile_dot(x_ref, x_start, y_ref, y_start, rows, tokens):
+    left = x_ref[:tokens, pl.ds(x_start, rows)]
+    right = y_ref[:tokens, pl.ds(y_start, COLS)]
     return lax.dot_general(
         left, right, (((0,), (0,)), ((), ())), preferred_element_type=jnp.float32
     )
 
 
-def reduce_kernel(units, num_in, num_out, dp_size, *refs):
-    ins, small_ref = refs[:num_in], refs[num_in]
-    outs, small_out = refs[num_in + 1 : num_in + 1 + num_out], refs[num_in + 1 + num_out]
-    sent, core_in, first_y, first_x, second, third, small_in = refs[num_in + num_out + 2 : -10]
-    sems = refs[-10:]
-    core_s, core_r, one_s, one_r, two_s, two_r, three_s, three_r, small_s, small_r = sems
-    dp, sq = lax.axis_index("dp"), lax.axis_index("seq")
-    core, ypos = sq % 2, sq // 2
+def reduce_peers(dp_size):
+    dp, sq, core, ypos, core_peer, y_peer = places()
+    xpos, zpos = dp % 2, dp // 2
+    depth = dp_size // 2
+    peers = [core_peer, y_peer, (dp + 1 - 2 * xpos, sq)]
+    return peers + [((zpos + step) % depth * 2 + xpos, sq) for step in range(1, depth)]
+
+
+def reducer(units, ins, emit, buffers, dp_size):
+    sent, core_in, first_y, first_x, second, third = buffers[:6]
+    core_s, core_r, one_s, one_r, two_s, two_r, three_s, three_r = buffers[6:14]
+    core_free, one_free, two_free = buffers[14:]
+    dp, sq, core, ypos, core_peer, y_peer = places()
     xpos, zpos = dp % 2, dp // 2
     depth = dp_size // 2
     chunk = 1024 // dp_size
-    core_peer = (dp, sq + 1 - 2 * core)
-    y_peer = (dp, sq + 2 - 4 * ypos)
     x_peer = (dp + 1 - 2 * xpos, sq)
+    count = len(units)
+    remote = remote_copy
 
     def z_peer(step):
         return ((zpos + step) % depth * 2 + xpos, sq)
 
-    barrier = pltpu.get_barrier_semaphore()
-    for peer in [core_peer, y_peer, x_peer] + [z_peer(step) for step in range(1, depth)]:
-        pl.semaphore_signal(barrier, inc=1, device_id=peer, device_id_type=MESH_ID)
-    pl.semaphore_wait(barrier, 2 + depth)
-
-    def remote(src, dst, send_sem, recv_sem, peer):
-        return pltpu.make_async_remote_copy(
-            src_ref=src,
-            dst_ref=dst,
-            send_sem=send_sem,
-            recv_sem=recv_sem,
-            device_id=peer,
-            device_id_type=MESH_ID,
-        )
-
     def half_dots(unit, half, write):
-        x_id, y_id, kind, part = units[unit]
+        x_id, y_id, kind, part, base, tokens = units[unit]
         x_ref, y_ref = ins[x_id], ins[y_id]
         rows = chunk if kind == "back" else 256
 
         def body(step, carry):
             tile, side = step // 2, step % 2
             block = side * 2 + half
-            x_start = tile * 256
+            x_start = base + tile * 256
             y_start = block * COLS
             if kind == "in":
                 y_start = block * 1024 + part * COLS
@@ -819,6 +925,7 @@
                     y_ref,
                     pl.multiple_of(y_start, COLS),
                     rows,
+                    tokens,
                 ),
             )
             return carry
@@ -827,34 +934,34 @@
 
     def core_copy(unit):
         return remote(
-            sent.at[unit % SLOTS], core_in.at[unit], core_s.at[unit], core_r.at[unit], core_peer
+            sent.at[unit % SLOTS], core_in.at[unit % RING], core_s.at[unit], core_r.at[unit], core_peer
         )
 
     def one_copy(unit):
-        half = unit // 2
+        half = unit // 2 % (RING // 2)
         if unit % 2 == 0:
             return remote(
-                core_in.at[unit, 1 - ypos], first_y.at[half], one_s.at[unit], one_r.at[unit], y_peer
+                core_in.at[unit % RING, 1 - ypos], first_y.at[half], one_s.at[unit], one_r.at[unit], y_peer
             )
-        source = core_in.at[unit].reshape(2, depth, 2, chunk, COLS)
+        source = core_in.at[unit % RING].reshape(2, depth, 2, chunk, COLS)
         return remote(
             source.at[:, :, 1 - xpos], first_x.at[half], one_s.at[unit], one_r.at[unit], x_peer
         )
 
     def two_copy(unit):
-        half = unit // 2
+        half = unit // 2 % (RING // 2)
         if unit % 2 == 0:
             source = first_y.at[half].reshape(depth, 2, chunk, COLS)
             return remote(
-                source.at[:, 1 - xpos], second.at[unit], two_s.at[unit], two_r.at[unit], x_peer
+                source.at[:, 1 - xpos], second.at[unit % LATE], two_s.at[unit], two_r.at[unit], x_peer
             )
         return remote(
-            first_x.at[half, 1 - ypos], second.at[unit], two_s.at[unit], two_r.at[unit], y_peer
+            first_x.at[half, 1 - ypos], second.at[unit % LATE], two_s.at[unit], two_r.at[unit], y_peer
         )
 
     def three_copy(unit, step):
         return remote(
-            second.at[unit, (zpos + step) % depth],
+            second.at[unit % LATE, (zpos + step) % depth],
             third.at[unit, step - 1],
             three_s.at[unit, step - 1],
             three_r.at[unit, step - 1],
@@ -870,16 +977,24 @@
             sent[slot, side, rows, :] = value.astype(jnp.bfloat16)
 
         half_dots(unit, 1 - core, write)
+        if unit >= RING:
+            pl.semaphore_wait(core_free, 1)
         core_copy(unit).start()
+
+    def allow(unit, ring, free, peer):
+        if unit + ring < count:
+            pl.semaphore_signal(free, inc=1, device_id=peer, device_id_type=MESH_ID)
 
     def core_sum(unit):
         core_copy(unit).wait_recv()
 
         def write(side, rows, value):
-            old = core_in[unit, side, rows, :].astype(jnp.float32)
-            core_in[unit, side, rows, :] = (value + old).astype(jnp.bfloat16)
+            old = core_in[unit % RING, side, rows, :].astype(jnp.float32)
+            core_in[unit % RING, side, rows, :] = (value + old).astype(jnp.bfloat16)
 
         half_dots(unit, core, write)
+        if unit >= RING:
+            pl.semaphore_wait(one_free.at[unit % 2], 1)
         one_copy(unit).start()
 
     def plus(left, right):
@@ -887,12 +1002,12 @@
 
     def one_sum(unit):
         one_copy(unit).wait_recv()
-        half = unit // 2
+        half = unit // 2 % (RING // 2)
         if unit % 2 == 0:
 
             def body(step, carry):
                 rows = pl.ds(pl.multiple_of(step * 128, 128), 128)
-                first_y[half, rows, :] = plus(first_y[half, rows, :], core_in[unit, ypos, rows, :])
+                first_y[half, rows, :] = plus(first_y[half, rows, :], core_in[unit % RING, ypos, rows, :])
                 return carry
 
             lax.fori_loop(0, 8, body, 0)
@@ -901,16 +1016,20 @@
                 side, layer = step // depth, step % depth
                 rows = pl.ds(pl.multiple_of((layer * 2 + xpos) * chunk, chunk), chunk)
                 first_x[half, side, layer] = plus(
-                    first_x[half, side, layer], core_in[unit, side, rows, :]
+                    first_x[half, side, layer], core_in[unit % RING, side, rows, :]
                 )
                 return carry
 
             lax.fori_loop(0, 2 * depth, body, 0)
+        if unit >= LATE:
+            pl.semaphore_wait(two_free.at[unit % 2], 1)
         two_copy(unit).start()
+        one_copy(unit).wait_send()
+        allow(unit, RING, core_free, core_peer)
 
     def two_sum(unit):
         two_copy(unit).wait_recv()
-        half = unit // 2
+        half = unit // 2 % (RING // 2)
 
         def body(layer, carry):
             if unit % 2 == 0:
@@ -918,10 +1037,12 @@
                 old = first_y[half, rows, :]
             else:
                 old = first_x[half, ypos, layer]
-            second[unit, layer] = plus(second[unit, layer], old)
+            second[unit % LATE, layer] = plus(second[unit % LATE, layer], old)
             return carry
 
         lax.fori_loop(0, depth, body, 0)
+        two_copy(unit).wait_send()
+        allow(unit, RING, one_free.at[unit % 2], (y_peer, x_peer)[unit % 2])
 
         def send(step, carry):
             three_copy(unit, step).start()
@@ -934,113 +1055,59 @@
             three_copy(unit, step).wait_recv()
             return total + third[unit, step - 1].astype(jnp.float32)
 
-        total = lax.fori_loop(1, depth, body, second[unit, zpos].astype(jnp.float32))
-        x_id, y_id, kind, part = units[unit]
-        if kind == "in":
-            outs[8][:, part * COLS : (part + 1) * COLS] = total
-        elif kind in ("back", "parted"):
-            outs[9][part * chunk : (part + 1) * chunk, :] = total
-        else:
-            outs[part][...] = total
-
-    bits = 0
-    while (1 << bits) < dp_size:
-        bits += 1
-    small_out[...] = small_ref[...]
-
-    def small_copy(step):
-        if step == 0:
-            peer = core_peer
-        elif step == 1:
-            peer = y_peer
-        else:
-            flip = 1 << (step - 2)
-            peer = (dp + flip - 2 * flip * (dp // flip % 2), sq)
-        return remote(small_out, small_in.at[step], small_s.at[step], small_r.at[step], peer)
-
-    def small_step(step):
-        small_copy(step).wait()
-        small_out[...] = small_out[...] + small_in[step]
-
-    count = len(units)
-    pairs = count // 2
-    small_copy(0).start()
-    for turn in range(pairs + 5):
-        for unit in (2 * turn, 2 * turn + 1):
-            if unit < count:
-                products(unit)
-        for unit in (2 * turn - 2, 2 * turn - 1):
-            if 0 <= unit < count:
-                core_sum(unit)
-        for unit in (2 * turn - 4, 2 * turn - 3):
-            if 0 <= unit < count:
-                one_sum(unit)
-        for unit in (2 * turn - 6, 2 * turn - 5):
-            if 0 <= unit < count:
-                two_sum(unit)
-        for unit in (2 * turn - 8, 2 * turn - 7):
-            if 0 <= unit < count:
-                last_sum(unit)
-        if turn < bits + 2:
-            small_step(turn)
-            if turn + 1 < bits + 2:
-                small_copy(turn + 1).start()
-    for step in range(pairs + 5, bits + 2):
-        small_step(step)
-        if step + 1 < bits + 2:
-            small_copy(step + 1).start()
-    for unit in range(count):
-        if unit >= count - SLOTS:
-            core_copy(unit).wait_send()
-        one_copy(unit).wait_send()
-        two_copy(unit).wait_send()
-
-        def drain(step, carry):
+        total = lax.fori_loop(1, depth, body, second[unit % LATE, zpos].astype(jnp.float32))
+        emit(units[unit], total)
+
+        def sent_out(step, carry):
             three_copy(unit, step).wait_send()
             return carry
 
-        lax.fori_loop(1, depth, drain, 0)
-
-
-def reduce_grads(units, operands, small, dp_size):
-    count = len(units)
+        lax.fori_loop(1, depth, sent_out, 0)
+        allow(unit, LATE, two_free.at[unit % 2], (x_peer, y_peer)[unit % 2])
+
+    def turn(index):
+        for stage, lag in ((products, 0), (core_sum, 1), (one_sum, 2), (two_sum, 3), (last_sum, 4)):
+            for unit in (2 * (index - lag), 2 * (index - lag) + 1):
+                if 0 <= unit < count:
+                    stage(unit)
+
+    def drain():
+        for unit in range(count - SLOTS, count):
+            core_copy(unit).wait_send()
+
+    return turn, drain
+
+
+def reduce_buffers(count, dp_size):
     depth, chunk = dp_size // 2, 1024 // dp_size
-    bits = dp_size.bit_length() - 1
-    low = jnp.bfloat16
-    out_shapes = [jax.ShapeDtypeStruct((chunk, COLS), jnp.float32)] * 8
-    out_shapes.append(jax.ShapeDtypeStruct((chunk, 4 * COLS), jnp.float32))
-    out_shapes.append(jax.ShapeDtypeStruct((4 * chunk, COLS), jnp.float32))
-    out_shapes.append(jax.ShapeDtypeStruct(small.shape, jnp.float32))
     sem = pltpu.SemaphoreType.DMA
-    vmem = pl.BlockSpec(memory_space=pltpu.VMEM)
-    return pl.pallas_call(
-        functools.partial(reduce_kernel, units, len(operands), 10, dp_size),
-        out_shape=out_shapes,
-        in_specs=[vmem] * (len(operands) + 1),
-        out_specs=[vmem] * 11,
-        scratch_shapes=[
-            pltpu.VMEM((SLOTS, 2, 1024, COLS), low),
-            pltpu.VMEM((count, 2, 1024, COLS), low),
-            pltpu.VMEM((count // 2, 1024, COLS), low),
-            pltpu.VMEM((count // 2, 2, depth, chunk, COLS), low),
-            pltpu.VMEM((count, depth, chunk, COLS), low),
-            pltpu.VMEM((count, depth - 1, chunk, COLS), low),
-            pltpu.VMEM((bits + 2,) + small.shape, jnp.float32),
-            sem((count,)),
-            sem((count,)),
-            sem((count,)),
-            sem((count,)),
-            sem((count,)),
-            sem((count,)),
-            sem((count, depth - 1)),
-            sem((count, depth - 1)),
-            sem((bits + 2,)),
-            sem((bits + 2,)),
-        ],
-        compiler_params=pltpu.CompilerParams(
-            collective_id=0, has_side_effects=True, vmem_limit_bytes=60 << 20
-        ),
-    )(*operands, small)
+    credit = pltpu.SemaphoreType.REGULAR
+    return [
+        pltpu.VMEM((SLOTS, 2, 1024, COLS), LOW),
+        pltpu.VMEM((RING, 2, 1024, COLS), LOW),
+        pltpu.VMEM((RING // 2, 1024, COLS), LOW),
+        pltpu.VMEM((RING // 2, 2, depth, chunk, COLS), LOW),
+        pltpu.VMEM((LATE, depth, chunk, COLS), LOW),
+        pltpu.VMEM((count, depth - 1, chunk, COLS), LOW),
+    ] + [sem((count,))] * 6 + [sem((count, depth - 1))] * 2 + [credit, credit((2,)), credit((2,))]
+
+
+def small_sums(small, small_in, small_s, small_r, dp_size):
+    dp, sq, core, ypos, core_peer, y_peer = places()
+
+    def copy(step):
+        flip = 1 << max(step - 2, 0)
+        peer = (dp + flip - 2 * flip * (dp // flip % 2), sq)
+        peer = (core_peer, y_peer, peer)[min(step, 2)]
+        return remote_copy(small, small_in.at[step], small_s.at[step], small_r.at[step], peer)
+
+    def advance(step):
+        copy(step).wait()
+        small[...] = small[...] + small_in[step]
+        if step < dp_size.bit_length():
+            copy(step + 1).start()
+
+    return copy, advance
 
 
 def per_device(
@@ -1106,68 +1173,65 @@
         w_in,
         w_back,
     )
-    rears = rear(
-        (
-            d_crossed,
-            d_resid_two,
-            cross_key,
-            cross_value,
-            cross_query,
-            resid_one,
-            main_key,
-            main_value,
-            query,
-            own_key,
-            own_value,
-            own_probs,
-        ),
-        line(gain_one),
-        (c_out, c_query, w_out, w_query, w_key, w_value, c_key, c_value),
-        cross_probs,
-        probs,
-    )
-    d_cross_query, d_cross_key, d_cross_value, encoded_grad, d_attended = rears[:5]
-    d_query_low, d_keys, d_values, stream_grad, rear_grads, bias_sums, own_sums = rears[5:]
-
     blocks = full_len // local_len
     place = jnp.arange(2 * local_len, dtype=jnp.int32)
     reach = (sq - jnp.arange(blocks, dtype=jnp.int32))[:, None] * local_len + (
         local_len - 1 - place[None, :]
     )
-    first_of = jnp.sum((bucket_table[:, None] < bucket_ids[None, :]).astype(jnp.int32), axis=0)
-    next_of = jnp.sum((bucket_table[:, None] <= bucket_ids[None, :]).astype(jnp.int32), axis=0)
+    reach = jnp.concatenate([reach, jnp.zeros((1, 2 * local_len), jnp.int32)])
+    lane_ids = jnp.arange(128, dtype=jnp.int32)
+    first_of = jnp.sum((bucket_table[:, None] < lane_ids[None, :]).astype(jnp.int32), axis=0)
+    next_of = jnp.sum((bucket_table[:, None] <= lane_ids[None, :]).astype(jnp.int32), axis=0)
     window_hot = (reach[..., None] >= first_of) & (reach[..., None] < next_of)
-    table_part = jnp.einsum(
-        "hkv,kvb->bh", bias_sums, window_hot.astype(jnp.float32), precision=exact
-    )
-    own_hot = (bucket_ids == bucket_table[0]).astype(jnp.float32)
-    table_part = table_part + own_hot[:, None] * jnp.sum(own_sums, axis=(1, 2))[None, :]
     position = sq * local_len + jnp.arange(local_len)
     count = num_streams * jnp.sum((position < lengths[0]).astype(jnp.float32))
-    stats = jnp.concatenate([jnp.sum(front_stats, axis=1), jnp.sum(ffn_stat, axis=1), count[None]])
-    tail = jnp.concatenate([table_part.reshape(-1), stats, jnp.zeros((507,), jnp.float32)])
-    small = jnp.concatenate([rear_grads, mid_grads, tail[None], jnp.zeros_like(tail)[None]])
+    mid_stats = jnp.concatenate([front_stats, ffn_stat]).reshape(4, -1, 128).sum(axis=1)
+    mid_stats = jnp.concatenate([mid_stats, jnp.full((4, 128), count / 128)])
     units = []
-    operands = [d_ffn_out, second_norm, d_inner, cross_low, d_crossed, first_norm, d_cross_query]
-    operands += [source_rows, d_cross_key, d_cross_value, context_low, d_attended]
-    operands += [flat_rows, d_query_low, d_keys, d_values]
-    if chunk % 128 == 0:
-        operands.append(activated)
-        for part in range(4):
-            units.append((16, 0, "back", part))
-    else:
-        parted = jnp.transpose(activated.reshape(-1, dp_size, 4, chunk), (2, 0, 1, 3))
-        parted = parted.reshape(4, -1, model_width)
-        for part in range(4):
-            operands.append(parted[part])
-            units.append((16 + part, 0, "parted", part))
+    tokens = num_streams * local_len
+    spread = activated
+    if chunk % 128 != 0:
+        spread = activated.reshape(-1, dp_size, 4, chunk)
+        spread = jnp.transpose(spread, (0, 2, 1, 3)).reshape(activated.shape)
     for part in range(4):
-        units.append((1, 2, "in", part))
-    units += [(3, 4, "", 7), (5, 6, "", 4), (7, 8, "", 5), (7, 9, "", 6), (10, 11, "", 3)]
-    units += [(12, 13, "", 0), (12, 14, "", 1), (12, 15, "", 2)]
-    reduced = reduce_grads(tuple(units), operands, small, dp_size)
-    shares, sums = reduced[:10], reduced[10]
-    rms = jnp.sqrt(sums[6, 512:516] / (sums[6, 516] * model_width))
+        if chunk % 128 == 0:
+            units.append((3, 0, "back", part, 0, tokens))
+        else:
+            units.append((3, 0, "parted", part, part * model_width, tokens))
+        units.append((1, 2, "in", part, 0, tokens))
+    units += [(4, 5, "", 7, 0, tokens), (6, 7, "", 4, 0, tokens), (3, 8, "", 3, 0, tokens)]
+    units += [(3, 9, "", 5, 2 * model_width, local_len), (3, 10, "", 6, 2 * model_width, local_len)]
+    units += [(3, 11 + part, "", part, model_width, tokens) for part in range(3)]
+    rears = rear(
+        (
+            d_crossed,
+            cross_query,
+            resid_one,
+            query,
+            own_key,
+            own_value,
+            own_probs,
+            line(gain_one),
+            d_ffn_out,
+            second_norm,
+            cross_low,
+            first_norm,
+            mid_grads,
+            mid_stats,
+            window_hot.astype(jnp.bfloat16),
+        ),
+        (d_inner, spread, context_low, flat_rows, source_rows, d_resid_two),
+        (cross_key, cross_value, main_key, main_value),
+        (c_out, c_query, w_out, w_query, w_key, w_value, c_key, c_value),
+        cross_probs,
+        probs,
+        tuple(units),
+        dp_size,
+    )
+    encoded_grad, stream_grad, sums = rears[:3]
+    shares = rears[3:]
+    wide_sums = sums[:48].reshape(6, model_width)
+    rms = jnp.sqrt(jnp.sum(sums[64:68], axis=1) / (jnp.sum(sums[68]) * model_width))
     return (
         layer_output.reshape(stream.shape),
         stream_grad.reshape(stream.shape),
@@ -1182,13 +1246,13 @@
         shares[7],
         shares[8],
         shares[9],
-        sums[0],
-        sums[1],
-        sums[2],
-        sums[3],
-        sums[4],
-        sums[5],
-        sums[6, :512].reshape(NBUCKET, HEADS),
+        wide_sums[0],
+        wide_sums[1],
+        wide_sums[2],
+        wide_sums[3],
+        wide_sums[4],
+        wide_sums[5],
+        jnp.transpose(sums[48:64, :NBUCKET]),
         rms,
     )
 

time: 363 us -> 321 us (0.88)
  Pallas kernels: 334 us -> 296 us
    pallas_call x2 -> x1, Pallas kernels: 247 us -> 209 us  [rear(): pl.pallas_call(functools.partial(rear_kernel, units, dp_size), out_shape=...]
    slice x4 -> x0, local copies, waits for them, and re-layouts: 5.01 us -> none  [the longest x1 1.71 us: per_device(): sums[5]]
    unnamed x43 -> x38, local copies, waits for them, and re-layouts: 9.15 us -> 10.7 us
where the time goes in v4:
time: 321 us; the launch traced here: 320 us
  Pallas kernels  296 us (92%)
  local copies, waits for them, and re-layouts  14.7 us (5%)
  other arithmetic  5.92 us (2%)
    pallas_call x1, Pallas kernels, rear(): pl.pallas_call(functools.partial(rear_kernel, units, dp_size), out_shape=...  209 us
    pallas_call x1, Pallas kernels, front(): pl.pallas_call(front_kernel, out_shape=outs, in_specs=[vmem, vmem, smem]...  59.2 us
    pallas_call x1, Pallas kernels, middle(): pl.pallas_call(middle_kernel, out_shape=[shape((tokens, width), LOW), sha...  27.6 us
    unnamed x38, local copies, waits for them, and re-layouts  10.7 us

profile of v4, /device:TPU:0, one launch (start us, length us, event | category | flops | bytes accessed | tf_op | source)
XLA Modules:
  0.0 320.3 jit_solution(8116149055249717475)
XLA Ops:
  0.7 0.0 copy-start
  1.3 0.6 fusion.1
  2.6 0.8 convert_reduce_fusion.1
  3.4 0.1 broadcast_add_fusion
  3.5 0.0 copy-done
  3.5 1.0 convolution_bitcast_fusion
  4.5 0.7 broadcast_in_dim.2.refs_3_
  5.2 1.0 and_convert_fusion.refs_14_
  6.2 59.2 %shard_map.373 = (bf16[384,1024]{1,0:T(8,128)(2,1)}, bf16[256,1024]{1,0:T(8,128)(2,1)}, bf16[256,1024]{1,0:T(8,128)(2,1)}, bf16[512,1024]{1,0:T(8,128)(2,1)}, bf...) custom-call(bf16[3,128,1024]{2,1,0:T(8,128)(2,1)} %bitcast.36, ...), custom_call_target="tpu_custom_call" | custom-call | tf_op jit(solution)/shard_map/pallas_call | solution.py:349
  65.4 0.0 copy-start.12
  65.4 27.6 %shard_map.374 = (bf16[384,1024]{1,0:T(8,128)(2,1)}, bf16[384,4096]{1,0:T(8,128)(2,1)}, bf16[384,1024]{1,0:T(8,128)(2,1)}, bf16[384,4096]{1,0:T(8,128)(2,1)}, f3...) custom-call(bf16[384,1024]{1,0:T(8,128)(2,1)} %get-tuple-element.60.refs_0_.refs_9_, ...), custom_call_target="tpu_custom_call" | custom-call | tf_op jit(solution)/shard_map/pallas_call | solution.py:463
  93.0 0.0 copy-done.12
  93.0 0.7 maximum_bitcast_fusion
  93.7 0.6 concatenate.14.refs_13_
  94.3 209.2 %shard_map.375 = (bf16[128,1024]{1,0:T(8,128)(2,1)}, bf16[384,1024]{1,0:T(8,128)(2,1)}, f32[80,128]{1,0:T(8,128)}, f32[128,256]{1,0:T(8,128)}, f32[128,256]{1,0:...) custom-call(bf16[384,1024]{1,0:T(8,128)(2,1)} %get-tuple-element.63., ...), custom_call_target="tpu_custom_call" | custom-call | tf_op jit(solution)/shard_map/pallas_call | solution.py:822
  303.5 0.0 copy-start.11
  303.6 0.0 copy-start.10
  303.6 0.0 copy-start.9
  303.6 0.0 copy-start.8
  303.6 0.0 copy-start.7
  303.6 0.0 copy-start.6
  303.6 0.0 copy-start.5
  303.6 0.0 copy-start.4
  303.6 1.4 slice_reduce_fusion.1
  305.7 0.8 slice_reduce_fusion
  306.5 0.5 divide_sqrt_fusion
  307.0 1.3 slice_bitcast_fusion
  308.3 1.3 slice_bitcast_fusion.1
  309.6 2.1 copy.58
  311.8 1.7 copy.59
  313.5 0.0 copy-done.11
  313.5 0.7 copy.60
  314.1 0.0 copy-done.10
  314.1 0.7 copy.61
  314.8 0.0 copy-done.9
  314.8 0.7 copy.62
  315.5 0.0 copy-done.8
  315.5 0.7 copy.63
  316.1 0.0 copy-done.7
  316.1 0.7 copy.64
  316.8 0.0 copy-done.6
  316.8 0.7 copy.65
  317.4 0.0 copy-done.5
  317.4 0.7 copy.66
  318.1 0.0 copy-done.4
  318.1 0.7 copy.67
  318.8 0.8 copy.68
  319.6 0.8 copy.69
  (11 shorter events, 0.1 us)
Async XLA Ops:
  0.7 2.9 copy-start
  65.4 27.6 %copy-start.12 = (f32[3,1024]{1,0:T(4,128)S(1)}, f32[3,1024]{1,0:T(4,128)}, u32[]{:S(2)}) copy-start(f32[3,1024]{1,0:T(4,128)} %get-tuple-element.74) | copy-start | bytes 36868
  303.5 9.9 %copy-start.11 = (f32[128,256]{1,0:T(8,128)S(1)}, f32[128,256]{1,0:T(8,128)}, u32[]{:S(2)}) copy-start(f32[128,256]{1,0:T(8,128)} %get-tuple-element.131) | copy-start | bytes 393220
  303.6 10.6 %copy-start.10 = (f32[128,256]{1,0:T(8,128)S(1)}, f32[128,256]{1,0:T(8,128)}, u32[]{:S(2)}) copy-start(f32[128,256]{1,0:T(8,128)} %get-tuple-element.132) | copy-start | bytes 393220
  303.6 11.2 %copy-start.9 = (f32[128,256]{1,0:T(8,128)S(1)}, f32[128,256]{1,0:T(8,128)}, u32[]{:S(2)}) copy-start(f32[128,256]{1,0:T(8,128)} %get-tuple-element.133) | copy-start | bytes 393220
  303.6 11.9 %copy-start.8 = (f32[128,256]{1,0:T(8,128)S(1)}, f32[128,256]{1,0:T(8,128)}, u32[]{:S(2)}) copy-start(f32[128,256]{1,0:T(8,128)} %get-tuple-element.134) | copy-start | bytes 393220
  303.6 12.5 %copy-start.7 = (f32[128,256]{1,0:T(8,128)S(1)}, f32[128,256]{1,0:T(8,128)}, u32[]{:S(2)}) copy-start(f32[128,256]{1,0:T(8,128)} %get-tuple-element.135) | copy-start | bytes 393220
  303.6 13.2 %copy-start.6 = (f32[128,256]{1,0:T(8,128)S(1)}, f32[128,256]{1,0:T(8,128)}, u32[]{:S(2)}) copy-start(f32[128,256]{1,0:T(8,128)} %get-tuple-element.136) | copy-start | bytes 393220
  303.6 13.8 %copy-start.5 = (f32[128,256]{1,0:T(8,128)S(1)}, f32[128,256]{1,0:T(8,128)}, u32[]{:S(2)}) copy-start(f32[128,256]{1,0:T(8,128)} %get-tuple-element.137) | copy-start | bytes 393220
  303.6 14.5 %copy-start.4 = (f32[128,256]{1,0:T(8,128)S(1)}, f32[128,256]{1,0:T(8,128)}, u32[]{:S(2)}) copy-start(f32[128,256]{1,0:T(8,128)} %get-tuple-element.138) | copy-start | bytes 393220
  309.6 9.1 %copy-start.3 = (f32[128,1024]{1,0:T(8,128)S(1)}, f32[128,1024]{1,0:T(8,128)}, u32[]{:S(2)}) copy-start(f32[128,1024]{1,0:T(8,128)} %get-tuple-element.139) | copy-start | bytes 1572868
  311.8 7.8 %copy-start.2 = (f32[512,256]{1,0:T(8,128)S(1)}, f32[512,256]{1,0:T(8,128)}, u32[]{:S(2)}) copy-start(f32[512,256]{1,0:T(8,128)} %get-tuple-element.140) | copy-start | bytes 1572868
  311.8 8.6 %copy-start.1 = (f32[32,16]{0,1:T(8,128)S(1)}, f32[32,16]{0,1:T(8,128)}, u32[]{:S(2)}) copy-start(f32[32,16]{0,1:T(8,128)} %param.43) | copy-start | bytes 6148

commit v5 on v4

--- a/solution.py
+++ b/solution.py
@@ -11,9 +11,10 @@
 HEAD_DIM = 64
 NBUCKET = 32
 COLS = 256
-SLOTS = 3
+SLOTS = 2
 RING = 6
-LATE = 8
+RING_ONE = 5
+COLORS = "yxyxzxyxyxzxyxzxyxyxzxyxzxyxyxyx"
 epsilon = 1e-05
 masked_score = -1e30
 
@@ -65,13 +66,10 @@
 
 
 def project_to(dst, left, weight, scale=None):
-    def body(cols):
-        product = dot(left[...], weight[:, cols])
-        if scale is not None:
-            product = product * scale
-        dst[:, cols] = product.astype(dst.dtype)
-
-    tiles(dst.shape[1] // 256, 256, body)
+    product = dot(left[...], weight[...])
+    if scale is not None:
+        product = product * scale
+    dst[...] = product.astype(dst.dtype)
 
 
 def norm_stats(rows):
@@ -81,9 +79,7 @@
     return centred, lax.rsqrt(spread + epsilon)
 
 
-def norm_backward(rows, gain, incoming):
-    centred, scale = norm_stats(rows)
-    unit = centred * scale
+def norm_backward(unit, scale, gain, incoming):
     scaled = incoming * gain
     first = jnp.mean(scaled, axis=-1, keepdims=True)
     second = jnp.mean(scaled * unit, axis=-1, keepdims=True)
@@ -115,12 +111,12 @@
     stream, encoded, length_ref, bias_table = refs[:4]
     gain_one, shift_one, gain_two, shift_two = refs[4:8]
     hbm_weights = refs[8:16]
-    (query, own_key, own_value, main_key, main_value, context, resid_one, first_norm) = refs[16:24]
-    (cross_query, cross_key, cross_value, cross_context, resid_two, second_norm) = refs[24:30]
-    own_probs, stats, probs_out, cross_probs_out = refs[30:34]
-    weights = refs[34:42]
-    main_all, source_all, kept, bias, masks = refs[42:47]
-    weight_sem, kept_sem, send_sem, recv_sem = refs[47:]
+    (query, own_key, own_value, main_key, main_value, context, unit_one, first_norm) = refs[16:24]
+    (cross_query, cross_key, cross_value, cross_context, unit_two, second_norm) = refs[24:30]
+    scales, own_probs, stats, probs_out, cross_probs_out = refs[30:35]
+    weights = refs[35:43]
+    main_all, source_all, kept, bias, masks, branch_out = refs[43:49]
+    weight_sem, kept_sem, send_sem, recv_sem = refs[49:]
     w_query, w_key, w_value, w_out, c_query, c_key, c_value, c_out = weights
     dp, sq, core, ypos, core_peer, y_peer = places()
     length = length_ref[0]
@@ -245,18 +241,19 @@
 
     mask = valid_rows(sq, length, rows)
     loads[3].wait()
-    project_to(resid_one, context, w_out)
+    project_to(branch_out, context, w_out)
     seen = jnp.zeros((1, stream.shape[2]), WIDE)
     branch = jnp.zeros((1, stream.shape[2]), WIDE)
     for stream_id in range(3):
         part = slice(stream_id * rows, (stream_id + 1) * rows)
-        source, attended = stream[stream_id].astype(WIDE), resid_one[part, :]
+        source, attended = stream[stream_id].astype(WIDE), branch_out[part, :]
         seen = seen + sum_squares(source, mask)
         branch = branch + sum_squares(attended, mask)
-        total = source + attended
-        resid_one[part, :] = total
-        centred, scale = norm_stats(total)
-        first_norm[part, :] = (centred * scale * gain_one[...] + shift_one[...]).astype(LOW)
+        centred, scale = norm_stats(source + attended)
+        unit = centred * scale
+        unit_one[part, :] = unit.astype(LOW)
+        scales[0, part, :] = jnp.broadcast_to(scale, (rows, 128))
+        first_norm[part, :] = (unit * gain_one[...] + shift_one[...]).astype(LOW)
     stats[0:1, :] = seen
     stats[1:2, :] = branch
     loads[4].wait()
@@ -298,16 +295,17 @@
     for pair in range(HEADS // 2 - 2, HEADS // 2):
         kept_copy(pair, cross_probs_out).wait()
     loads[7].wait()
-    project_to(resid_two, cross_context, c_out)
+    project_to(branch_out, cross_context, c_out)
     branch = jnp.zeros((1, stream.shape[2]), WIDE)
     for stream_id in range(3):
         part = slice(stream_id * rows, (stream_id + 1) * rows)
-        crossed = resid_two[part, :]
+        crossed = branch_out[part, :]
         branch = branch + sum_squares(crossed, mask)
-        total = first_norm[part, :].astype(WIDE) + crossed
-        resid_two[part, :] = total
-        centred, scale = norm_stats(total)
-        second_norm[part, :] = (centred * scale * gain_two[...] + shift_two[...]).astype(LOW)
+        centred, scale = norm_stats(first_norm[part, :].astype(WIDE) + crossed)
+        unit = centred * scale
+        unit_two[part, :] = unit.astype(LOW)
+        scales[1, part, :] = jnp.broadcast_to(scale, (rows, 128))
+        second_norm[part, :] = (unit * gain_two[...] + shift_two[...]).astype(LOW)
     stats[2:3, :] = branch
     for copy in firsts:
         copy.wait_send()
@@ -329,14 +327,15 @@
         shape((full, width), LOW),
         shape((full, width), LOW),
         shape((tokens, width), LOW),
-        shape((tokens, width), WIDE),
+        shape((tokens, width), LOW),
         shape((tokens, width), LOW),
         shape((tokens, width), LOW),
         shape((full, width), LOW),
         shape((full, width), LOW),
         shape((tokens, width), LOW),
-        shape((tokens, width), WIDE),
         shape((tokens, width), LOW),
+        shape((tokens, width), LOW),
+        shape((2, tokens, 128), WIDE),
         shape((HEADS, 1, tokens), WIDE),
         shape((3, width), WIDE),
         shape((pairs, 2, full, tokens), LOW),
@@ -350,7 +349,7 @@
         front_kernel,
         out_shape=outs,
         in_specs=[vmem, vmem, smem] + [vmem] * 5 + [hbm] * 8,
-        out_specs=[vmem] * 16 + [hbm] * 2,
+        out_specs=[vmem] * 17 + [hbm] * 2,
         scratch_shapes=[pltpu.VMEM(w.shape, LOW) for w in weights]
         + [
             pltpu.VMEM((seq, rows, width), LOW),
@@ -358,6 +357,7 @@
             pltpu.VMEM((2, 2, full, tokens), LOW),
             pltpu.VMEM((2, full, rows), WIDE),
             pltpu.VMEM((3, full, rows), WIDE),
+            pltpu.VMEM((tokens, width), WIDE),
             sem((8,)),
             sem((2,)),
             sem((6,)),
@@ -370,10 +370,10 @@
 
 
 def middle_kernel(*refs):
-    second_norm, resid_two, cotangent, length_ref, gain_two, gain_three, shift_three = refs[:7]
-    hbm_in, hbm_back = refs[7:9]
-    output, activated, d_ffn, d_inner, d_resid, d_crossed, grads, stats = refs[9:17]
-    w_in, w_back, slope, total, load_sem = refs[17:]
+    second_norm, unit_two, scales, cotangent, length_ref, gain_two, gain_three = refs[:7]
+    shift_three, hbm_in, hbm_back = refs[7:10]
+    output, activated, d_ffn, d_inner, d_resid, d_crossed, grads, stats = refs[10:18]
+    w_in, w_back, slope, total, load_sem = refs[18:]
     sq = lax.axis_index("seq")
     length = length_ref[0]
     tokens, width = second_norm.shape
@@ -419,10 +419,11 @@
         branch = branch + sum_squares(ffn, mask)
         resid = second_norm[part, :].astype(WIDE) + ffn
         centred, scale = norm_stats(resid)
-        normed = centred * scale * gain_three[...] + shift_three[...]
+        unit = centred * scale
+        normed = unit * gain_three[...] + shift_three[...]
         output[part, :] = (normed * mask).astype(LOW)
         incoming = cotangent[part, :].astype(WIDE) * mask
-        back, gain_part, shift_part = norm_backward(resid, gain_three[...], incoming)
+        back, gain_part, shift_part = norm_backward(unit, scale, gain_three[...], incoming)
         d_gain, d_shift = d_gain + gain_part, d_shift + shift_part
         total[part, :] = back
         d_ffn[part, :] = back.astype(LOW)
@@ -443,8 +444,9 @@
     d_shift = jnp.zeros((1, width), WIDE)
     for stream_id in range(3):
         part = slice(stream_id * rows, (stream_id + 1) * rows)
+        unit, scale = unit_two[part, :].astype(WIDE), scales[1, part, 0:1]
         back, gain_part, shift_part = norm_backward(
-            resid_two[part, :], gain_two[...], total[part, :]
+            unit, scale, gain_two[...], total[part, :]
         )
         d_gain, d_shift = d_gain + gain_part, d_shift + shift_part
         d_resid[part, :] = back
@@ -453,7 +455,7 @@
     grads[1:2, :] = d_shift
 
 
-def middle(second_norm, resid_two, cotangent, length, gain_two, gain_three, shift_three, w_in, w_back):
+def middle(second_norm, unit_two, scales, cotangent, length, norms, w_in, w_back):
     tokens, width = second_norm.shape
     hidden = w_in.shape[1]
     shape = jax.ShapeDtypeStruct
@@ -472,7 +474,7 @@
             shape((4, width), WIDE),
             shape((1, width), WIDE),
         ],
-        in_specs=[vmem] * 3 + [smem] + [vmem] * 3 + [hbm] * 2,
+        in_specs=[vmem] * 4 + [smem] + [vmem] * 3 + [hbm] * 2,
         out_specs=[vmem] * 8,
         scratch_shapes=[
             pltpu.VMEM(w_in.shape, LOW),
@@ -482,12 +484,13 @@
             pltpu.SemaphoreType.DMA((2, hidden // 512)),
         ],
         compiler_params=pltpu.CompilerParams(vmem_limit_bytes=60 << 20),
-    )(second_norm, resid_two, cotangent, length, gain_two, gain_three, shift_three, w_in, w_back)
+    )(second_norm, unit_two, scales, cotangent, length, *norms, w_in, w_back)
 
 
 def rear_kernel(units, dp_size, *refs):
-    d_crossed, cross_query, resid_one, query, own_key, own_value, own_probs, gain_one = refs[:8]
+    d_crossed, cross_query, unit_one, query, own_key, own_value, own_probs, gain_one = refs[:8]
     d_ffn, second_norm, cross_context, first_norm, mid_grads, mid_stats, window_hot = refs[8:15]
+    scales, refs = refs[15], refs[:15] + refs[16:]
     hbm_inner, hbm_activated, hbm_context, hbm_stream, hbm_source, hbm_resid = refs[15:21]
     hbm_sides, hbm_weights = refs[21:25], refs[25:33]
     cross_probs, probs = refs[33:35]
@@ -503,18 +506,18 @@
     c_out, c_query, w_out, w_query, w_key, w_value, c_key, c_value = [weights[i] for i in held]
     chunk = 1024 // dp_size
 
-    def emit(unit, total):
-        part = unit[3]
+    def emit(unit, item, total):
+        part, cols = unit[3], slice(item * 128, (item + 1) * 128)
         if unit[2] == "in":
-            in_share[:, part * COLS : (part + 1) * COLS] = total
+            in_share[:, part * COLS + item * 128 : part * COLS + (item + 1) * 128] = total
         elif unit[2] in ("back", "parted"):
-            back_share[part * chunk : (part + 1) * chunk, :] = total
+            back_share[part * chunk : (part + 1) * chunk, cols] = total
         else:
-            shares[part][...] = total
+            shares[part][:, cols] = total
 
     operands = (d_ffn, second_norm, d_inner, activated, cross_context, d_crossed, first_norm)
     operands += (d_cross_query, d_attended, d_cross_key, d_cross_value, d_query, d_key, d_value)
-    turn, drain = reducer(units, operands, emit, refs[77:], dp_size)
+    turn, drain = reducer(units, COLORS, operands, emit, refs[77:], dp_size)
     small_copy, small_step = small_sums(small_out, small_in, small_s, small_r, dp_size)
     dp, sq, core, ypos, core_peer, y_peer = places()
     tokens, width = query.shape
@@ -642,12 +645,15 @@
     load_side(1).wait()
     lax.fori_loop(0, pairs // 2, cross_pair, 0)
     turn(2)
+    turn(3)
     lax.fori_loop(pairs // 2, pairs, cross_pair, 0)
     fetch(0, probs, 0).start()
     load_side(2).start()
     load_side(3).start()
     core_copy(0).start()
     core_copy(1).start()
+    turn(4)
+    turn(5)
     loads[1].wait()
     early[2].wait()
     back_to(d_resid, d_cross_query, c_query, True)
@@ -656,8 +662,9 @@
     d_shift = jnp.zeros((1, width), WIDE)
     for stream_id in range(3):
         part = slice(stream_id * rows, (stream_id + 1) * rows)
+        unit, scale = unit_one[part, :].astype(WIDE), scales[0, part, 0:1]
         back, gain_part, shift_part = norm_backward(
-            resid_one[part, :], gain_one[...], d_resid[part, :]
+            unit, scale, gain_one[...], d_resid[part, :]
         )
         d_gain, d_shift = d_gain + gain_part, d_shift + shift_part
         d_resid[part, :] = back
@@ -672,7 +679,8 @@
     small_out[72:80, :] = jnp.zeros((8, 128), WIDE)
     near_sum(0)
     near_sum(1)
-    turn(3)
+    turn(6)
+    turn(7)
     loads[2].wait()
     back_to(d_context, d_attended, w_out)
     loads[7].start()
@@ -741,18 +749,26 @@
 
     load_side(2).wait()
     load_side(3).wait()
-    lax.fori_loop(0, pairs // 2, self_pair, 0)
-    turn(4)
+    quarter = pairs // 4
+    lax.fori_loop(0, quarter, self_pair, 0)
+    turn(8)
     for load in late:
         load.start()
-    lax.fori_loop(pairs // 2, pairs, self_pair, 0)
+    lax.fori_loop(quarter, 2 * quarter, self_pair, 0)
+    turn(9)
+    lax.fori_loop(2 * quarter, 3 * quarter, self_pair, 0)
+    for load in late:
+        load.wait()
+    turn(10)
+    lax.fori_loop(3 * quarter, pairs, self_pair, 0)
     core_copy(2).start()
     core_copy(3).start()
     d_cross_key[...] = far_sum(0)
     d_cross_value[...] = far_sum(1)
-    for load in late:
-        load.wait()
-    turn(5)
+    turn(11)
+    near_sum(2)
+    near_sum(3)
+    turn(12)
     loads[6].wait()
     loads[7].wait()
 
@@ -764,15 +780,13 @@
     tiles(width // 256, 256, source_body)
     loads[4].start()
     loads[5].start()
-    near_sum(2)
-    near_sum(3)
     loads[3].wait()
 
     def query_body(cols):
         d_resid[:, cols] += dot(d_query[...], w_query[cols, :], NT)
 
+    turn(13)
     tiles(width // 256, 256, query_body)
-    turn(6)
     table = jnp.zeros((HEADS, 128), WIDE)
     for block in range(blocks + 1):
         rest = bias_sums[:, block, :]
@@ -784,7 +798,8 @@
     small_copy(0).start()
     d_key[:rows, :] = far_sum(2)
     d_value[:rows, :] = far_sum(3)
-    turn(7)
+    turn(14)
+    turn(15)
     loads[4].wait()
     loads[5].wait()
 
@@ -798,12 +813,12 @@
         if index >= 2:
             core_copy(index).wait_send()
         far_copy(index).wait_send()
-    last = len(units) // 2 + 4
-    for index in range(8, last):
+    last = len(units) + 9
+    for index in range(16, last):
         turn(index)
-        if index - 8 <= dp_size.bit_length():
-            small_step(index - 8)
-    for step in range(last - 8, dp_size.bit_length() + 1):
+        if index % 2 == 0 and (index - 16) // 2 <= dp_size.bit_length():
+            small_step((index - 16) // 2)
+    for step in range((last - 15) // 2, dp_size.bit_length() + 1):
         small_step(step)
     drain()
 
@@ -861,7 +876,7 @@
             sem((steps,)),
             sem((steps,)),
         ]
-        + reduce_buffers(len(units), dp_size),
+        + reduce_buffers(COLORS, dp_size),
         compiler_params=pltpu.CompilerParams(
             collective_id=2, has_side_effects=True, vmem_limit_bytes=63 << 20
         ),
@@ -869,14 +884,6 @@
 
 
 MESH_ID = pl.DeviceIdType.MESH
-
-
-def tile_dot(x_ref, x_start, y_ref, y_start, rows, tokens):
-    left = x_ref[:tokens, pl.ds(x_start, rows)]
-    right = y_ref[:tokens, pl.ds(y_start, COLS)]
-    return lax.dot_general(
-        left, right, (((0,), (0,)), ((), ())), preferred_element_type=jnp.float32
-    )
 
 
 def reduce_peers(dp_size):
@@ -887,10 +894,11 @@
     return peers + [((zpos + step) % depth * 2 + xpos, sq) for step in range(1, depth)]
 
 
-def reducer(units, ins, emit, buffers, dp_size):
-    sent, core_in, first_y, first_x, second, third = buffers[:6]
-    core_s, core_r, one_s, one_r, two_s, two_r, three_s, three_r = buffers[6:14]
-    core_free, one_free, two_free = buffers[14:]
+def reducer(units, colors, ins, emit, buffers, dp_size):
+    sent, core_in, first_y, first_x, second_y, second_x, third = buffers[:7]
+    z_in, z_half, z_last = buffers[7:10]
+    core_s, core_r, one_s, one_r, two_s, two_r, three_s, three_r = buffers[10:18]
+    core_free, one_free, two_free = buffers[18:]
     dp, sq, core, ypos, core_peer, y_peer = places()
     xpos, zpos = dp % 2, dp // 2
     depth = dp_size // 2
@@ -898,6 +906,13 @@
     x_peer = (dp + 1 - 2 * xpos, sq)
     count = len(units)
     remote = remote_copy
+    nth = [colors[:item].count(colors[item]) for item in range(2 * count)]
+    order = [item - colors[:item].count("z") for item in range(2 * count)]
+    firsts = {"y": first_y, "x": first_x}
+    seconds = {"y": second_y, "x": second_x}
+    color_id = {"y": 0, "x": RING_ONE}
+    first_peer = {"y": y_peer, "x": x_peer}
+    second_peer = {"y": x_peer, "x": y_peer}
 
     def z_peer(step):
         return ((zpos + step) % depth * 2 + xpos, sq)
@@ -905,171 +920,258 @@
     def half_dots(unit, half, write):
         x_id, y_id, kind, part, base, tokens = units[unit]
         x_ref, y_ref = ins[x_id], ins[y_id]
-        rows = chunk if kind == "back" else 256
-
-        def body(step, carry):
-            tile, side = step // 2, step % 2
-            block = side * 2 + half
-            x_start = base + tile * 256
-            y_start = block * COLS
+        if kind == "back":
+            starts = [device * 4 * chunk + part * chunk for device in range(dp_size)]
+            left = jnp.concatenate([x_ref[:tokens, s : s + chunk] for s in starts], axis=1)
+        else:
+            left = x_ref[:tokens, base : base + 1024]
+        for side in range(2):
+            start = (side * 2 + half) * COLS
             if kind == "in":
-                y_start = block * 1024 + part * COLS
-            if kind == "back":
-                x_start = tile * (4 * chunk) + part * chunk
-            write(
-                side,
-                pl.ds(pl.multiple_of(tile * rows, rows), rows),
-                tile_dot(
-                    x_ref,
-                    pl.multiple_of(x_start, 128),
-                    y_ref,
-                    pl.multiple_of(y_start, COLS),
-                    rows,
-                    tokens,
-                ),
+                start = (side * 2 + half) * 1024 + part * COLS
+            right = y_ref[:tokens, pl.ds(pl.multiple_of(start, COLS), COLS)]
+            value = lax.dot_general(
+                left, right, (((0,), (0,)), ((), ())), preferred_element_type=WIDE
             )
-            return carry
-
-        lax.fori_loop(0, 2 * (1024 // rows), body, 0)
+            write(0, side, value[:, :128])
+            write(1, side, value[:, 128:])
+
+    def landed(item):
+        return core_in.at[item // 2 % RING, item % 2]
 
     def core_copy(unit):
         return remote(
-            sent.at[unit % SLOTS], core_in.at[unit % RING], core_s.at[unit], core_r.at[unit], core_peer
+            sent.at[unit % SLOTS],
+            core_in.at[unit % RING],
+            core_s.at[unit],
+            core_r.at[unit],
+            core_peer,
         )
 
-    def one_copy(unit):
-        half = unit // 2 % (RING // 2)
-        if unit % 2 == 0:
-            return remote(
-                core_in.at[unit % RING, 1 - ypos], first_y.at[half], one_s.at[unit], one_r.at[unit], y_peer
-            )
-        source = core_in.at[unit % RING].reshape(2, depth, 2, chunk, COLS)
+    def one_copy(item):
+        color, source = colors[item], landed(item)
+        if color == "y":
+            source = source.at[1 - ypos]
+        else:
+            source = source.reshape(2, depth, 2, chunk, 128).at[:, :, 1 - xpos]
         return remote(
-            source.at[:, :, 1 - xpos], first_x.at[half], one_s.at[unit], one_r.at[unit], x_peer
+            source,
+            firsts[color].at[nth[item] % RING_ONE],
+            one_s.at[item],
+            one_r.at[item],
+            first_peer[color],
         )
 
-    def two_copy(unit):
-        half = unit // 2 % (RING // 2)
-        if unit % 2 == 0:
-            source = first_y.at[half].reshape(depth, 2, chunk, COLS)
-            return remote(
-                source.at[:, 1 - xpos], second.at[unit % LATE], two_s.at[unit], two_r.at[unit], x_peer
-            )
+    def two_copy(item):
+        color = colors[item]
+        source = firsts[color].at[nth[item] % RING_ONE]
+        if color == "y":
+            source = source.reshape(depth, 2, chunk, 128).at[:, 1 - xpos]
+        else:
+            source = source.at[1 - ypos]
         return remote(
-            first_x.at[half, 1 - ypos], second.at[unit % LATE], two_s.at[unit], two_r.at[unit], y_peer
+            source,
+            seconds[color].at[nth[item] % RING_ONE],
+            two_s.at[item],
+            two_r.at[item],
+            second_peer[color],
         )
 
-    def three_copy(unit, step):
+    def three_copy(item, step):
+        color = colors[item]
         return remote(
-            second.at[unit % LATE, (zpos + step) % depth],
-            third.at[unit, step - 1],
-            three_s.at[unit, step - 1],
-            three_r.at[unit, step - 1],
+            seconds[color].at[nth[item] % RING_ONE, (zpos + step) % depth],
+            third.at[order[item], step - 1],
+            three_s.at[item, step - 1],
+            three_r.at[item, step - 1],
             z_peer(step),
         )
+
+    def z_copy(item, step):
+        source = landed(item).reshape(2, depth, 2 * chunk, 128)
+        return remote(
+            source.at[:, (zpos + step) % depth],
+            z_in.at[nth[item], step - 1],
+            three_s.at[item, step - 1],
+            three_r.at[item, step - 1],
+            z_peer(step),
+        )
+
+    def zy_copy(item):
+        return remote(
+            z_in.at[nth[item], 0, 1 - ypos],
+            z_half.at[nth[item]],
+            one_s.at[item],
+            one_r.at[item],
+            y_peer,
+        )
+
+    def zx_copy(item):
+        source = z_half.at[nth[item]].reshape(2, chunk, 128)
+        return remote(
+            source.at[1 - xpos], z_last.at[nth[item]], two_s.at[item], two_r.at[item], x_peer
+        )
+
+    def take(free, slot):
+        pl.semaphore_wait(free.at[slot], 1)
+
+    def allow(free, slot, peer):
+        pl.semaphore_signal(free.at[slot], inc=1, device_id=peer, device_id_type=MESH_ID)
+
+    def steps(action):
+        def body(step, carry):
+            action(step)
+            return carry
+
+        lax.fori_loop(1, depth, body, 0)
+
+    def plus(left, right):
+        return (left.astype(WIDE) + right.astype(WIDE)).astype(LOW)
 
     def products(unit):
         slot = unit % SLOTS
         if unit >= SLOTS:
             core_copy(unit - SLOTS).wait_send()
 
-        def write(side, rows, value):
-            sent[slot, side, rows, :] = value.astype(jnp.bfloat16)
+        def write(item, side, value):
+            sent[slot, item, side] = value.astype(LOW)
 
         half_dots(unit, 1 - core, write)
         if unit >= RING:
-            pl.semaphore_wait(core_free, 1)
+            for item in range(2):
+                take(core_free, unit % RING * 2 + item)
         core_copy(unit).start()
-
-    def allow(unit, ring, free, peer):
-        if unit + ring < count:
-            pl.semaphore_signal(free, inc=1, device_id=peer, device_id_type=MESH_ID)
 
     def core_sum(unit):
         core_copy(unit).wait_recv()
-
-        def write(side, rows, value):
-            old = core_in[unit % RING, side, rows, :].astype(jnp.float32)
-            core_in[unit % RING, side, rows, :] = (value + old).astype(jnp.bfloat16)
+        slot = unit % RING
+
+        def write(item, side, value):
+            old = core_in[slot, item, side].astype(WIDE)
+            core_in[slot, item, side] = (value + old).astype(LOW)
 
         half_dots(unit, core, write)
-        if unit >= RING:
-            pl.semaphore_wait(one_free.at[unit % 2], 1)
-        one_copy(unit).start()
-
-    def plus(left, right):
-        return (left.astype(jnp.float32) + right.astype(jnp.float32)).astype(jnp.bfloat16)
-
-    def one_sum(unit):
-        one_copy(unit).wait_recv()
-        half = unit // 2 % (RING // 2)
-        if unit % 2 == 0:
+        for item in (2 * unit, 2 * unit + 1):
+            color = colors[item]
+            if color == "z":
+                steps(lambda step: z_copy(item, step).start())
+                continue
+            if nth[item] >= RING_ONE:
+                take(one_free, color_id[color] + nth[item] % RING_ONE)
+            one_copy(item).start()
+
+    def core_done(item):
+        if item // 2 + RING < count:
+            allow(core_free, item // 2 % RING * 2 + item % 2, core_peer)
+
+    def one_sum(item):
+        color = colors[item]
+        if color == "z":
+            return
+        one_copy(item).wait_recv()
+        slot, base, own = nth[item] % RING_ONE, item // 2 % RING, item % 2
+        if color == "y":
 
             def body(step, carry):
-                rows = pl.ds(pl.multiple_of(step * 128, 128), 128)
-                first_y[half, rows, :] = plus(first_y[half, rows, :], core_in[unit % RING, ypos, rows, :])
-                return carry
-
-            lax.fori_loop(0, 8, body, 0)
-        else:
-            def body(step, carry):
-                side, layer = step // depth, step % depth
-                rows = pl.ds(pl.multiple_of((layer * 2 + xpos) * chunk, chunk), chunk)
-                first_x[half, side, layer] = plus(
-                    first_x[half, side, layer], core_in[unit % RING, side, rows, :]
+                rows = pl.ds(pl.multiple_of(step * 256, 256), 256)
+                first_y[slot, rows, :] = plus(
+                    first_y[slot, rows, :], core_in[base, own, ypos, rows, :]
                 )
                 return carry
 
-            lax.fori_loop(0, 2 * depth, body, 0)
-        if unit >= LATE:
-            pl.semaphore_wait(two_free.at[unit % 2], 1)
-        two_copy(unit).start()
-        one_copy(unit).wait_send()
-        allow(unit, RING, core_free, core_peer)
-
-    def two_sum(unit):
-        two_copy(unit).wait_recv()
-        half = unit // 2 % (RING // 2)
+            lax.fori_loop(0, 4, body, 0)
+        else:
+
+            def body(layer, carry):
+                rows = pl.ds(pl.multiple_of((layer * 2 + xpos) * chunk, chunk), chunk)
+                for side in range(2):
+                    first_x[slot, side, layer] = plus(
+                        first_x[slot, side, layer], core_in[base, own, side, rows, :]
+                    )
+                return carry
+
+            lax.fori_loop(0, depth, body, 0)
+        if nth[item] >= RING_ONE:
+            take(two_free, color_id[color] + nth[item] % RING_ONE)
+        two_copy(item).start()
+        one_copy(item).wait_send()
+        core_done(item)
+
+    def z_sum(item):
+        base, own = item // 2 % RING, item % 2
+        rows = pl.ds(pl.multiple_of(zpos * 2 * chunk, 2 * chunk), 2 * chunk)
+        steps(lambda step: z_copy(item, step).wait_recv())
+        for side in range(2):
+
+            def body(step, total):
+                return total + z_in[nth[item], step - 1, side].astype(WIDE)
+
+            mine = core_in[base, own, side, rows, :].astype(WIDE)
+            z_in[nth[item], 0, side] = lax.fori_loop(1, depth, body, mine).astype(LOW)
+        zy_copy(item).start()
+        steps(lambda step: z_copy(item, step).wait_send())
+        core_done(item)
+
+    def two_sum(item):
+        color = colors[item]
+        if color == "z":
+            z_sum(item)
+            return
+        two_copy(item).wait_recv()
+        slot = nth[item] % RING_ONE
+        second = seconds[color]
 
         def body(layer, carry):
-            if unit % 2 == 0:
+            if color == "y":
                 rows = pl.ds(pl.multiple_of((layer * 2 + xpos) * chunk, chunk), chunk)
-                old = first_y[half, rows, :]
+                old = first_y[slot, rows, :]
             else:
-                old = first_x[half, ypos, layer]
-            second[unit % LATE, layer] = plus(second[unit % LATE, layer], old)
+                old = first_x[slot, ypos, layer]
+            second[slot, layer] = plus(second[slot, layer], old)
             return carry
 
         lax.fori_loop(0, depth, body, 0)
-        two_copy(unit).wait_send()
-        allow(unit, RING, one_free.at[unit % 2], (y_peer, x_peer)[unit % 2])
-
-        def send(step, carry):
-            three_copy(unit, step).start()
-            return carry
-
-        lax.fori_loop(1, depth, send, 0)
-
-    def last_sum(unit):
+        steps(lambda step: three_copy(item, step).start())
+        two_copy(item).wait_send()
+        if nth[item] + RING_ONE < colors.count(color):
+            allow(one_free, color_id[color] + slot, first_peer[color])
+
+    def last_sum(item):
+        color = colors[item]
+        if color == "z":
+            zy_copy(item).wait_recv()
+            z_half[nth[item]] = plus(z_half[nth[item]], z_in[nth[item], 0, ypos])
+            zx_copy(item).start()
+            zy_copy(item).wait_send()
+            return
+        slot = nth[item] % RING_ONE
+
         def body(step, total):
-            three_copy(unit, step).wait_recv()
-            return total + third[unit, step - 1].astype(jnp.float32)
-
-        total = lax.fori_loop(1, depth, body, second[unit % LATE, zpos].astype(jnp.float32))
-        emit(units[unit], total)
-
-        def sent_out(step, carry):
-            three_copy(unit, step).wait_send()
-            return carry
-
-        lax.fori_loop(1, depth, sent_out, 0)
-        allow(unit, LATE, two_free.at[unit % 2], (x_peer, y_peer)[unit % 2])
+            three_copy(item, step).wait_recv()
+            return total + third[order[item], step - 1].astype(WIDE)
+
+        total = lax.fori_loop(1, depth, body, seconds[color][slot, zpos].astype(WIDE))
+        emit(units[item // 2], item % 2, total)
+        steps(lambda step: three_copy(item, step).wait_send())
+        if nth[item] + RING_ONE < colors.count(color):
+            allow(two_free, color_id[color] + slot, second_peer[color])
+
+    def z_end(item):
+        if colors[item] == "z":
+            zx_copy(item).wait_recv()
+            rows = pl.ds(pl.multiple_of(xpos * chunk, chunk), chunk)
+            mine = z_half[nth[item], rows, :].astype(WIDE)
+            emit(units[item // 2], item % 2, mine + z_last[nth[item]].astype(WIDE))
+            zx_copy(item).wait_send()
 
     def turn(index):
-        for stage, lag in ((products, 0), (core_sum, 1), (one_sum, 2), (two_sum, 3), (last_sum, 4)):
-            for unit in (2 * (index - lag), 2 * (index - lag) + 1):
-                if 0 <= unit < count:
-                    stage(unit)
+        for stage, lag in ((products, 0), (core_sum, 1)):
+            if 0 <= index - lag < count:
+                stage(index - lag)
+        for stage, lag in ((one_sum, 3), (two_sum, 5), (last_sum, 7), (z_end, 9)):
+            for item in (2 * (index - lag), 2 * (index - lag) + 1):
+                if 0 <= item < 2 * count:
+                    stage(item)
 
     def drain():
         for unit in range(count - SLOTS, count):
@@ -1078,18 +1180,29 @@
     return turn, drain
 
 
-def reduce_buffers(count, dp_size):
+def reduce_buffers(colors, dp_size):
     depth, chunk = dp_size // 2, 1024 // dp_size
+    count, slow = len(colors), max(colors.count("z"), 1)
     sem = pltpu.SemaphoreType.DMA
     credit = pltpu.SemaphoreType.REGULAR
-    return [
-        pltpu.VMEM((SLOTS, 2, 1024, COLS), LOW),
-        pltpu.VMEM((RING, 2, 1024, COLS), LOW),
-        pltpu.VMEM((RING // 2, 1024, COLS), LOW),
-        pltpu.VMEM((RING // 2, 2, depth, chunk, COLS), LOW),
-        pltpu.VMEM((LATE, depth, chunk, COLS), LOW),
-        pltpu.VMEM((count, depth - 1, chunk, COLS), LOW),
-    ] + [sem((count,))] * 6 + [sem((count, depth - 1))] * 2 + [credit, credit((2,)), credit((2,))]
+    return (
+        [
+            pltpu.VMEM((SLOTS, 2, 2, 1024, 128), LOW),
+            pltpu.VMEM((RING, 2, 2, 1024, 128), LOW),
+            pltpu.VMEM((RING_ONE, 1024, 128), LOW),
+            pltpu.VMEM((RING_ONE, 2, depth, chunk, 128), LOW),
+            pltpu.VMEM((RING_ONE, depth, chunk, 128), LOW),
+            pltpu.VMEM((RING_ONE, depth, chunk, 128), LOW),
+            pltpu.VMEM((count - colors.count("z"), depth - 1, chunk, 128), LOW),
+            pltpu.VMEM((slow, depth - 1, 2, 2 * chunk, 128), LOW),
+            pltpu.VMEM((slow, 2 * chunk, 128), LOW),
+            pltpu.VMEM((slow, chunk, 128), LOW),
+        ]
+        + [sem((count // 2,))] * 2
+        + [sem((count,))] * 4
+        + [sem((count, depth - 1))] * 2
+        + [credit((2 * RING,)), credit((2 * RING_ONE,)), credit((2 * RING_ONE,))]
+    )
 
 
 def small_sums(small, small_in, small_s, small_r, dp_size):
@@ -1159,17 +1272,16 @@
         (line(gain_one), line(shift_one), line(gain_two), line(shift_two)),
         (w_query, w_key, w_value, w_out, c_query, c_key, c_value, c_out),
     )
-    query, own_key, own_value, main_key, main_value, context_low, resid_one, first_norm = fronts[:8]
-    cross_query, cross_key, cross_value, cross_low, resid_two, second_norm = fronts[8:14]
-    own_probs, front_stats, probs, cross_probs = fronts[14:]
+    query, own_key, own_value, main_key, main_value, context_low, unit_one, first_norm = fronts[:8]
+    cross_query, cross_key, cross_value, cross_low, unit_two, second_norm = fronts[8:14]
+    scales, own_probs, front_stats, probs, cross_probs = fronts[14:]
     layer_output, activated, d_ffn_out, d_inner, d_resid_two, d_crossed, mid_grads, ffn_stat = middle(
         second_norm,
-        resid_two,
+        unit_two,
+        scales,
         flat_cotangent,
         lengths,
-        line(gain_two),
-        line(gain_three),
-        line(shift_three),
+        (line(gain_two), line(gain_three), line(shift_three)),
         w_in,
         w_back,
     )
@@ -1206,7 +1318,7 @@
         (
             d_crossed,
             cross_query,
-            resid_one,
+            unit_one,
             query,
             own_key,
             own_value,
@@ -1219,6 +1331,7 @@
             mid_grads,
             mid_stats,
             window_hot.astype(jnp.bfloat16),
+            scales,
         ),
         (d_inner, spread, context_low, flat_rows, source_rows, d_resid_two),
         (cross_key, cross_value, main_key, main_value),

time: 321 us -> 284 us (0.88); the launches traced: 320 us -> 280 us
  Pallas kernels: 296 us -> 255 us
    pallas_call x1, Pallas kernels: 209 us -> 173 us  [rear(): pl.pallas_call(functools.partial(rear_kernel, units, dp_size), out_shape=...]
    pallas_call x1, Pallas kernels: 59.2 us -> 54.7 us  [front(): pl.pallas_call(front_kernel, out_shape=outs, in_specs=[vmem, vmem, smem]...]
where the time goes in v5:
time: 284 us; the launch traced here: 280 us
  Pallas kernels  255 us (90%)
  local copies, waits for them, and re-layouts  14.6 us (5%)
  other arithmetic  5.92 us (2%)
  between operations  3.22 us (1%)
    pallas_call x1, Pallas kernels, rear(): pl.pallas_call(functools.partial(rear_kernel, units, dp_size), out_shape=...  173 us
    pallas_call x1, Pallas kernels, front(): pl.pallas_call(front_kernel, out_shape=outs, in_specs=[vmem, vmem, smem]...  54.7 us
    pallas_call x1, Pallas kernels, middle(): pl.pallas_call(middle_kernel, out_shape=[shape((tokens, width), LOW), sha...  27.4 us
    unnamed x38, local copies, waits for them, and re-layouts  10.7 us

profile of v5, /device:TPU:0, one launch (start us, length us, event | category | flops | bytes accessed | tf_op | source)
XLA Modules:
  0.0 279.9 jit_solution(9400977606840301666)
XLA Ops:
  0.7 0.0 copy-start
  1.3 0.6 fusion.1
  2.6 0.8 convert_reduce_fusion.1
  3.4 0.1 broadcast_add_fusion
  3.5 0.0 copy-done
  3.5 1.0 convolution_bitcast_fusion
  4.5 0.7 broadcast_in_dim.2.refs_3_
  5.2 1.0 and_convert_fusion.refs_14_
  6.2 54.7 %shard_map.373 = (bf16[384,1024]{1,0:T(8,128)(2,1)}, bf16[256,1024]{1,0:T(8,128)(2,1)}, bf16[256,1024]{1,0:T(8,128)(2,1)}, bf16[512,1024]{1,0:T(8,128)(2,1)}, bf...) custom-call(bf16[3,128,1024]{2,1,0:T(8,128)(2,1)} %bitcast.36, ...), custom_call_target="tpu_custom_call" | custom-call | tf_op jit(solution)/shard_map/pallas_call | solution.py:348
  60.8 0.0 copy-start.12
  60.9 27.4 %shard_map.374 = (bf16[384,1024]{1,0:T(8,128)(2,1)}, bf16[384,4096]{1,0:T(8,128)(2,1)}, bf16[384,1024]{1,0:T(8,128)(2,1)}, bf16[384,4096]{1,0:T(8,128)(2,1)}, f3...) custom-call(bf16[384,1024]{1,0:T(8,128)(2,1)} %get-tuple-element.61.refs_0_.refs_9_, ...), custom_call_target="tpu_custom_call" | custom-call | tf_op jit(solution)/shard_map/pallas_call | solution.py:465
  88.3 0.0 copy-done.12
  88.3 0.7 maximum_bitcast_fusion
  89.0 0.6 concatenate.14.refs_13_
  89.6 173.1 %shard_map.375 = (bf16[128,1024]{1,0:T(8,128)(2,1)}, bf16[384,1024]{1,0:T(8,128)(2,1)}, f32[80,128]{1,0:T(8,128)}, f32[128,256]{1,0:T(8,128)}, f32[128,256]{1,0:...) custom-call(bf16[384,1024]{1,0:T(8,128)(2,1)} %get-tuple-element.65., ...), custom_call_target="tpu_custom_call" | custom-call | tf_op jit(solution)/shard_map/pallas_call | solution.py:837
  262.7 0.0 copy-start.11
  262.7 0.0 copy-start.10
  262.7 0.0 copy-start.9
  262.7 0.0 copy-start.8
  262.7 0.0 copy-start.7
  262.7 0.0 copy-start.6
  262.7 0.0 copy-start.5
  262.7 0.0 copy-start.4
  262.8 1.4 slice_reduce_fusion.1
  264.8 0.8 slice_reduce_fusion
  265.6 0.5 divide_sqrt_fusion
  266.1 1.3 slice_bitcast_fusion
  267.4 1.3 slice_bitcast_fusion.1
  268.7 2.1 copy.58
  270.9 1.7 copy.59
  272.6 0.0 copy-done.11
  272.6 0.7 copy.60
  273.3 0.0 copy-done.10
  273.3 0.7 copy.61
  273.9 0.7 copy.62
  274.6 0.7 copy.63
  275.2 0.0 copy-done.7
  275.2 0.7 copy.64
  275.9 0.0 copy-done.6
  275.9 0.7 copy.65
  276.6 0.0 copy-done.5
  276.6 0.7 copy.66
  277.2 0.0 copy-done.4
  277.2 0.7 copy.67
  277.9 0.0 copy-done.3
  277.9 0.8 copy.68
  278.7 0.0 copy-done.2
  278.7 0.8 copy.69
  (11 shorter events, 0.1 us)
Async XLA Ops:
  0.7 2.9 %copy-start = (f32[32,16]{0,1:T(8,128)S(1)}, f32[32,16]{0,1:T(8,128)}, u32[]{:S(2)}) copy-start(f32[32,16]{0,1:T(8,128)} %param.43) | copy-start | bytes 6148
  60.8 27.4 %copy-start.12 = (f32[3,1024]{1,0:T(4,128)S(1)}, f32[3,1024]{1,0:T(4,128)}, u32[]{:S(2)}) copy-start(f32[3,1024]{1,0:T(4,128)} %get-tuple-element.76) | copy-start | bytes 36868
  262.7 9.9 %copy-start.11 = (f32[128,256]{1,0:T(8,128)S(1)}, f32[128,256]{1,0:T(8,128)}, u32[]{:S(2)}) copy-start(f32[128,256]{1,0:T(8,128)} %get-tuple-element.133) | copy-start | bytes 393220
  262.7 10.6 %copy-start.10 = (f32[128,256]{1,0:T(8,128)S(1)}, f32[128,256]{1,0:T(8,128)}, u32[]{:S(2)}) copy-start(f32[128,256]{1,0:T(8,128)} %get-tuple-element.134) | copy-start | bytes 393220
  262.7 11.2 %copy-start.9 = (f32[128,256]{1,0:T(8,128)S(1)}, f32[128,256]{1,0:T(8,128)}, u32[]{:S(2)}) copy-start(f32[128,256]{1,0:T(8,128)} %get-tuple-element.135) | copy-start | bytes 393220
  262.7 11.9 %copy-start.8 = (f32[128,256]{1,0:T(8,128)S(1)}, f32[128,256]{1,0:T(8,128)}, u32[]{:S(2)}) copy-start(f32[128,256]{1,0:T(8,128)} %get-tuple-element.136) | copy-start | bytes 393220
  262.7 12.5 %copy-start.7 = (f32[128,256]{1,0:T(8,128)S(1)}, f32[128,256]{1,0:T(8,128)}, u32[]{:S(2)}) copy-start(f32[128,256]{1,0:T(8,128)} %get-tuple-element.137) | copy-start | bytes 393220
  262.7 13.2 %copy-start.6 = (f32[128,256]{1,0:T(8,128)S(1)}, f32[128,256]{1,0:T(8,128)}, u32[]{:S(2)}) copy-start(f32[128,256]{1,0:T(8,128)} %get-tuple-element.138) | copy-start | bytes 393220
  262.7 13.8 %copy-start.5 = (f32[128,256]{1,0:T(8,128)S(1)}, f32[128,256]{1,0:T(8,128)}, u32[]{:S(2)}) copy-start(f32[128,256]{1,0:T(8,128)} %get-tuple-element.139) | copy-start | bytes 393220
  262.7 14.5 %copy-start.4 = (f32[128,256]{1,0:T(8,128)S(1)}, f32[128,256]{1,0:T(8,128)}, u32[]{:S(2)}) copy-start(f32[128,256]{1,0:T(8,128)} %get-tuple-element.140) | copy-start | bytes 393220
  268.7 9.1 %copy-start.3 = (f32[128,1024]{1,0:T(8,128)S(1)}, f32[128,1024]{1,0:T(8,128)}, u32[]{:S(2)}) copy-start(f32[128,1024]{1,0:T(8,128)} %get-tuple-element.141) | copy-start | bytes 1572868
  270.9 7.8 %copy-start.2 = (f32[512,256]{1,0:T(8,128)S(1)}, f32[512,256]{1,0:T(8,128)}, u32[]{:S(2)}) copy-start(f32[512,256]{1,0:T(8,128)} %get-tuple-element.142) | copy-start | bytes 1572868
  270.9 8.6 %copy-start.1 = (f32[32,16]{0,1:T(8,128)S(1)}, f32[32,16]{0,1:T(8,128)}, u32[]{:S(2)}) copy-start(f32[32,16]{0,1:T(8,128)} %param.43) | copy-start | bytes 6148

commit v6 on v5

--- a/solution.py
+++ b/solution.py
@@ -108,15 +108,21 @@
 
 
 def front_kernel(*refs):
-    stream, encoded, length_ref, bias_table = refs[:4]
-    gain_one, shift_one, gain_two, shift_two = refs[4:8]
-    hbm_weights = refs[8:16]
-    (query, own_key, own_value, main_key, main_value, context, unit_one, first_norm) = refs[16:24]
-    (cross_query, cross_key, cross_value, cross_context, unit_two, second_norm) = refs[24:30]
-    scales, own_probs, stats, probs_out, cross_probs_out = refs[30:35]
-    weights = refs[35:43]
-    main_all, source_all, kept, bias, masks, branch_out = refs[43:49]
-    weight_sem, kept_sem, send_sem, recv_sem = refs[49:]
+    stream, encoded, length_ref, bucket_row, position_bias = refs[:5]
+    gain_one, shift_one, gain_two, shift_two = refs[5:9]
+    hbm_weights = refs[9:17]
+    outs, probs_out, cross_probs_out = refs[17:34], refs[34], refs[35]
+    held, refs = refs[36:53], refs[53:]
+    (query, own_key, own_value, main_key, main_value, context, unit_one, first_norm) = held[:8]
+    (cross_query, cross_key, cross_value, cross_context, unit_two, second_norm) = held[8:14]
+    scales, own_probs, stats = held[14:]
+    weights = refs[:8]
+    main_all, source_all, kept, bias, masks, branch_out, bias_table = refs[8:15]
+    weight_sem, kept_sem, send_sem, recv_sem, out_sem = refs[15:]
+    stores = [
+        pltpu.make_async_copy(src, dst, out_sem.at[index])
+        for index, (src, dst) in enumerate(zip(held, outs))
+    ]
     w_query, w_key, w_value, w_out, c_query, c_key, c_value, c_out = weights
     dp, sq, core, ypos, core_peer, y_peer = places()
     length = length_ref[0]
@@ -144,9 +150,21 @@
                     peer,
                 )
             )
-            firsts[-1].start()
+    firsts[0].start()
+    firsts[1].start()
     main_all[sq] = stream[0]
     source_all[sq] = encoded[...]
+    bucket = lax.broadcasted_iota(jnp.int32, (NBUCKET, full), 0)
+    table_hot = (bucket == bucket_row[...]).astype(WIDE).astype(LOW)
+    by_distance = jnp.zeros((HEADS, full), WIDE)
+    rest = position_bias[...]
+    for _ in range(3):
+        part = rest.astype(LOW)
+        rest = rest - part.astype(WIDE)
+        by_distance = by_distance + dot(part, table_hot, (((0,), (0,)), ((), ())))
+    bias_table[...] = jnp.zeros_like(bias_table)
+    for head in range(HEADS):
+        bias_table[head, :, full:] = by_distance[head : head + 1]
 
     def passed_on(index):
         other = gathered[index].at[sq + 2 - 4 * ypos]
@@ -156,27 +174,31 @@
     flat = stream.reshape(3 * rows, stream.shape[2])
     loads[0].wait()
     project_to(query, flat, w_query, 0.125)
-    firsts[0].wait_recv()
-    passed_on(0).start()
+    stores[0].start()
     predicting = flat.at[rows:, :]
     loads[1].wait()
     project_to(own_key, predicting, w_key)
     loads[2].wait()
     project_to(own_value, predicting, w_value)
-    firsts[1].wait_recv()
-    passed_on(0).wait_recv()
-    firsts[2].wait_recv()
-    passed_on(1).start()
-    wide_main = main_all.reshape(full, main_all.shape[2])
-    project_to(main_key, wide_main, w_key)
-    project_to(main_value, wide_main, w_value)
-
     key_row = lax.broadcasted_iota(jnp.int32, (full, rows), 0)
     distance = sq * rows + lax.broadcasted_iota(jnp.int32, (full, rows), 1) - key_row
     in_range = key_row < length
     masks[0] = jnp.where((distance >= 0) & in_range, 0.0, masked_score)
     masks[1] = jnp.where((distance > 0) & in_range, 0.0, masked_score)
     masks[2] = jnp.where(in_range, 0.0, masked_score)
+    firsts[0].wait_recv()
+    passed_on(0).start()
+    firsts[2].start()
+    firsts[3].start()
+    stores[1].start()
+    stores[2].start()
+    firsts[1].wait_recv()
+    passed_on(0).wait_recv()
+    wide_main = main_all.reshape(full, main_all.shape[2])
+    project_to(main_key, wide_main, w_key)
+    project_to(main_value, wide_main, w_value)
+    stores[3].start()
+    stores[4].start()
 
     def kept_copy(pair, out):
         slot = pair % 2
@@ -238,10 +260,14 @@
     lax.fori_loop(0, HEADS // 2, self_pair, 0)
     for pair in range(HEADS // 2 - 2, HEADS // 2):
         kept_copy(pair, probs_out).wait()
+    stores[5].start()
+    stores[15].start()
 
     mask = valid_rows(sq, length, rows)
     loads[3].wait()
     project_to(branch_out, context, w_out)
+    firsts[2].wait_recv()
+    passed_on(1).start()
     seen = jnp.zeros((1, stream.shape[2]), WIDE)
     branch = jnp.zeros((1, stream.shape[2]), WIDE)
     for stream_id in range(3):
@@ -258,6 +284,8 @@
     stats[1:2, :] = branch
     loads[4].wait()
     project_to(cross_query, first_norm, c_query, 0.125)
+    for index in (6, 7, 8):
+        stores[index].start()
     firsts[3].wait_recv()
     passed_on(1).wait_recv()
     wide_source = source_all.reshape(full, source_all.shape[2])
@@ -265,6 +293,8 @@
     project_to(cross_key, wide_source, c_key)
     loads[6].wait()
     project_to(cross_value, wide_source, c_value)
+    stores[9].start()
+    stores[10].start()
 
     def cross_pair(pair, carry):
         @pl.when(pair >= 2)
@@ -294,6 +324,7 @@
     lax.fori_loop(0, HEADS // 2, cross_pair, 0)
     for pair in range(HEADS // 2 - 2, HEADS // 2):
         kept_copy(pair, cross_probs_out).wait()
+    stores[11].start()
     loads[7].wait()
     project_to(branch_out, cross_context, c_out)
     branch = jnp.zeros((1, stream.shape[2]), WIDE)
@@ -307,13 +338,17 @@
         scales[1, part, :] = jnp.broadcast_to(scale, (rows, 128))
         second_norm[part, :] = (unit * gain_two[...] + shift_two[...]).astype(LOW)
     stats[2:3, :] = branch
+    for index in (12, 13, 14, 16):
+        stores[index].start()
+    for store in stores:
+        store.wait()
     for copy in firsts:
         copy.wait_send()
     for index in range(2):
         passed_on(index).wait_send()
 
 
-def front(stream, encoded, length, bias_table, norms, weights):
+def front(stream, encoded, length, bucket_row, position_bias, norms, weights):
     streams, rows, width = stream.shape
     seq = lax.axis_size("seq")
     full, tokens = seq * rows, streams * rows
@@ -348,9 +383,10 @@
     return pl.pallas_call(
         front_kernel,
         out_shape=outs,
-        in_specs=[vmem, vmem, smem] + [vmem] * 5 + [hbm] * 8,
-        out_specs=[vmem] * 17 + [hbm] * 2,
-        scratch_shapes=[pltpu.VMEM(w.shape, LOW) for w in weights]
+        in_specs=[vmem, vmem, smem] + [vmem] * 6 + [hbm] * 8,
+        out_specs=[hbm] * 19,
+        scratch_shapes=[pltpu.VMEM(out.shape, out.dtype) for out in outs[:17]]
+        + [pltpu.VMEM(w.shape, LOW) for w in weights]
         + [
             pltpu.VMEM((seq, rows, width), LOW),
             pltpu.VMEM((seq, rows, width), LOW),
@@ -358,29 +394,35 @@
             pltpu.VMEM((2, full, rows), WIDE),
             pltpu.VMEM((3, full, rows), WIDE),
             pltpu.VMEM((tokens, width), WIDE),
+            pltpu.VMEM((HEADS, 1, 2 * full), WIDE),
             sem((8,)),
             sem((2,)),
             sem((6,)),
             sem((6,)),
+            sem((17,)),
         ],
         compiler_params=pltpu.CompilerParams(
             collective_id=1, has_side_effects=True, vmem_limit_bytes=60 << 20
         ),
-    )(stream, encoded, length, bias_table, *norms, *weights)
+    )(stream, encoded, length, bucket_row, position_bias, *norms, *weights)
 
 
 def middle_kernel(*refs):
-    second_norm, unit_two, scales, cotangent, length_ref, gain_two, gain_three = refs[:7]
-    shift_three, hbm_in, hbm_back = refs[7:10]
-    output, activated, d_ffn, d_inner, d_resid, d_crossed, grads, stats = refs[10:18]
-    w_in, w_back, slope, total, load_sem = refs[18:]
+    second_norm, cotangent, length_ref, gain_three, shift_three, hbm_in, hbm_back = refs[:7]
+    outs, grads, stats = refs[7:12], refs[12], refs[13]
+    output, activated, d_ffn, slope, total = refs[14:19]
+    w_in, w_back, load_sem, out_sem = refs[19:]
     sq = lax.axis_index("seq")
     length = length_ref[0]
     tokens, width = second_norm.shape
     rows = tokens // 3
     hidden = w_in.shape[1]
-    size = 512
+    size = 1024
     steps = hidden // size
+    stores = [
+        pltpu.make_async_copy(src, dst, out_sem.at[index])
+        for index, (src, dst) in enumerate(zip(refs[14:19], outs))
+    ]
 
     def load_in(step):
         cols = pl.ds(pl.multiple_of(step * size, size), size)
@@ -409,6 +451,8 @@
         return carry
 
     lax.fori_loop(0, steps, forward, 0)
+    stores[1].start()
+    stores[3].start()
     mask = valid_rows(sq, length, rows)
     branch = jnp.zeros((1, width), WIDE)
     d_gain = jnp.zeros((1, width), WIDE)
@@ -428,71 +472,54 @@
         total[part, :] = back
         d_ffn[part, :] = back.astype(LOW)
     stats[...] = branch
-    grads[2:3, :] = d_gain
-    grads[3:4, :] = d_shift
-
-    def backward(step, carry):
-        cols = pl.ds(pl.multiple_of(step * size, size), size)
-        d_act = dot(d_ffn[...], w_back[cols, :], NT)
-        d_in = (d_act * slope[:, cols].astype(WIDE)).astype(LOW)
-        d_inner[:, cols] = d_in
-        total[...] += dot(d_in, w_in[:, cols], NT)
-        return carry
-
-    lax.fori_loop(0, steps, backward, 0)
-    d_gain = jnp.zeros((1, width), WIDE)
-    d_shift = jnp.zeros((1, width), WIDE)
-    for stream_id in range(3):
-        part = slice(stream_id * rows, (stream_id + 1) * rows)
-        unit, scale = unit_two[part, :].astype(WIDE), scales[1, part, 0:1]
-        back, gain_part, shift_part = norm_backward(
-            unit, scale, gain_two[...], total[part, :]
-        )
-        d_gain, d_shift = d_gain + gain_part, d_shift + shift_part
-        d_resid[part, :] = back
-        d_crossed[part, :] = back.astype(LOW)
     grads[0:1, :] = d_gain
     grads[1:2, :] = d_shift
-
-
-def middle(second_norm, unit_two, scales, cotangent, length, norms, w_in, w_back):
+    for index in (0, 2, 4):
+        stores[index].start()
+    for store in stores:
+        store.wait()
+
+
+def middle(second_norm, cotangent, length, norms, w_in, w_back):
     tokens, width = second_norm.shape
     hidden = w_in.shape[1]
     shape = jax.ShapeDtypeStruct
     vmem = pl.BlockSpec(memory_space=pltpu.VMEM)
     smem = pl.BlockSpec(memory_space=pltpu.SMEM)
     hbm = pl.BlockSpec(memory_space=pl.ANY)
+    outs = [
+        shape((tokens, width), LOW),
+        shape((tokens, hidden), LOW),
+        shape((tokens, width), LOW),
+        shape((tokens, hidden), LOW),
+        shape((tokens, width), WIDE),
+    ]
     return pl.pallas_call(
         middle_kernel,
-        out_shape=[
-            shape((tokens, width), LOW),
-            shape((tokens, hidden), LOW),
-            shape((tokens, width), LOW),
-            shape((tokens, hidden), LOW),
-            shape((tokens, width), WIDE),
-            shape((tokens, width), LOW),
-            shape((4, width), WIDE),
-            shape((1, width), WIDE),
-        ],
-        in_specs=[vmem] * 4 + [smem] + [vmem] * 3 + [hbm] * 2,
-        out_specs=[vmem] * 8,
-        scratch_shapes=[
+        out_shape=outs + [shape((2, width), WIDE), shape((1, width), WIDE)],
+        in_specs=[vmem] * 2 + [smem] + [vmem] * 2 + [hbm] * 2,
+        out_specs=[hbm] * 5 + [vmem] * 2,
+        scratch_shapes=[pltpu.VMEM(out.shape, out.dtype) for out in outs]
+        + [
             pltpu.VMEM(w_in.shape, LOW),
             pltpu.VMEM(w_back.shape, LOW),
-            pltpu.VMEM((tokens, hidden), LOW),
-            pltpu.VMEM((tokens, width), WIDE),
-            pltpu.SemaphoreType.DMA((2, hidden // 512)),
+            pltpu.SemaphoreType.DMA((2, hidden // 1024)),
+            pltpu.SemaphoreType.DMA((5,)),
         ],
         compiler_params=pltpu.CompilerParams(vmem_limit_bytes=60 << 20),
-    )(second_norm, unit_two, scales, cotangent, length, *norms, w_in, w_back)
+    )(second_norm, cotangent, length, *norms, w_in, w_back)
 
 
 def rear_kernel(units, dp_size, *refs):
-    d_crossed, cross_query, unit_one, query, own_key, own_value, own_probs, gain_one = refs[:8]
-    d_ffn, second_norm, cross_context, first_norm, mid_grads, mid_stats, window_hot = refs[8:15]
-    scales, refs = refs[15], refs[:15] + refs[16:]
-    hbm_inner, hbm_activated, hbm_context, hbm_stream, hbm_source, hbm_resid = refs[15:21]
+    cross_query, unit_one, query, own_key, own_value, own_probs, gain_one = refs[:7]
+    refs = (None,) + refs
+    d_ffn, second_norm, cross_context, first_norm, mid_grads, ffn_stat, front_stats = refs[8:15]
+    scales, gain_two, bucket_row, length_ref = refs[15:19]
+    refs = refs[:15] + refs[19:]
+    hbm_slope, hbm_activated, hbm_context, hbm_stream, hbm_source, hbm_resid = refs[15:21]
+    hbm_unit, refs = refs[21], refs[:21] + refs[22:]
     hbm_sides, hbm_weights = refs[21:25], refs[25:33]
+    hbm_ffn, refs = refs[33:35], refs[:33] + refs[35:]
     cross_probs, probs = refs[33:35]
     encoded_grad, stream_grad, small_out = refs[35:38]
     shares, in_share, back_share = refs[38:46], refs[46], refs[47]
@@ -501,6 +528,7 @@
     d_inner, activated = refs[57:59]
     weights = refs[59:62]
     kept, d_context, d_resid, parts, near_in, far_in, sides_held = refs[62:69]
+    d_crossed, ffn_sem, refs = refs[69], refs[70], refs[:69] + refs[71:]
     weight_sem, kept_sem, core_s, core_r, far_s, far_r, small_s, small_r = refs[69:77]
     held = (0, 1, 2, 0, 1, 2, 1, 2)
     c_out, c_query, w_out, w_query, w_key, w_value, c_key, c_value = [weights[i] for i in held]
@@ -536,8 +564,9 @@
 
     early = [
         load_extra(0, hbm_activated, activated),
-        load_extra(1, hbm_inner, d_inner),
+        load_extra(1, hbm_slope, d_inner),
         load_extra(2, hbm_resid, d_resid),
+        load_extra(6, hbm_unit, d_context),
     ]
     late = [
         load_extra(3, hbm_context, activated.at[:, :width]),
@@ -554,20 +583,56 @@
         slot = (pair + base) % 2
         return pltpu.make_async_copy(source.at[pair], kept.at[slot], kept_sem.at[slot])
 
+    def keep_lines(base, lines):
+        for row, line in enumerate(lines):
+            for piece in range(8):
+                at = 8 * (base + row) + piece
+                small_out[at : at + 1, :] = line[:, 128 * piece : 128 * (piece + 1)]
+
+    def ffn_load(index):
+        span = pl.ds(index // 2 * width, width)
+        source = hbm_ffn[0].at[span] if index % 2 == 0 else hbm_ffn[1].at[:, span]
+        return pltpu.make_async_copy(source, weights[index % 3], ffn_sem.at[index])
+
     early[0].start()
     early[1].start()
-    loads[0].start()
+    for index in range(3):
+        ffn_load(index).start()
+    early[2].start()
+    early[3].start()
     fetch(0, cross_probs, 0).start()
     load_side(0).start()
     load_side(1).start()
-    loads[1].start()
-    loads[2].start()
-    early[2].start()
     greet(reduce_peers(dp_size))
     early[0].wait()
+    turn(0)
     early[1].wait()
-    turn(0)
-    turn(1)
+    early[2].wait()
+    ffn_steps = hbm_ffn[0].shape[0] // width
+    for step in range(ffn_steps):
+        span = slice(step * width, (step + 1) * width)
+        ffn_load(2 * step).wait()
+        d_act = dot(d_ffn[...], weights[2 * step % 3][...], NT)
+        d_inner[:, span] = (d_act * d_inner[:, span].astype(WIDE)).astype(LOW)
+        ffn_load(2 * step + 1).wait()
+        d_resid[...] += dot(d_inner[:, span], weights[(2 * step + 1) % 3][...], NT)
+        for index in (2 * step + 3, 2 * step + 4):
+            if index < 2 * ffn_steps:
+                ffn_load(index).start()
+        turn(1 + step)
+    for index in range(3):
+        loads[index].start()
+    early[3].wait()
+    d_gain_two = jnp.zeros((1, width), WIDE)
+    d_shift_two = jnp.zeros((1, width), WIDE)
+    for stream_id in range(3):
+        part = slice(stream_id * rows, (stream_id + 1) * rows)
+        unit, scale = d_context[part, :].astype(WIDE), scales[1, part, 0:1]
+        back, gain_part, shift_part = norm_backward(unit, scale, gain_two[...], d_resid[part, :])
+        d_gain_two, d_shift_two = d_gain_two + gain_part, d_shift_two + shift_part
+        d_resid[part, :] = back
+        d_crossed[part, :] = back.astype(LOW)
+    keep_lines(2, [d_gain_two, d_shift_two])
     loads[0].wait()
 
     def back_to(dst, left, weight, add=False):
@@ -644,18 +709,15 @@
     load_side(0).wait()
     load_side(1).wait()
     lax.fori_loop(0, pairs // 2, cross_pair, 0)
-    turn(2)
-    turn(3)
+    turn(5)
     lax.fori_loop(pairs // 2, pairs, cross_pair, 0)
     fetch(0, probs, 0).start()
     load_side(2).start()
     load_side(3).start()
     core_copy(0).start()
     core_copy(1).start()
-    turn(4)
-    turn(5)
+    turn(6)
     loads[1].wait()
-    early[2].wait()
     back_to(d_resid, d_cross_query, c_query, True)
     loads[6].start()
     d_gain = jnp.zeros((1, width), WIDE)
@@ -669,17 +731,19 @@
         d_gain, d_shift = d_gain + gain_part, d_shift + shift_part
         d_resid[part, :] = back
         d_attended[part, :] = back.astype(LOW)
-    lines = [d_gain, d_shift] + [mid_grads[row : row + 1, :] for row in range(4)]
-    for row, line in enumerate(lines):
-        for piece in range(8):
-            small_out[8 * row + piece : 8 * row + piece + 1, :] = line[
-                :, 128 * piece : 128 * (piece + 1)
-            ]
-    small_out[64:72, :] = mid_stats[...]
-    small_out[72:80, :] = jnp.zeros((8, 128), WIDE)
+    keep_lines(0, [d_gain, d_shift])
+    keep_lines(4, [mid_grads[row : row + 1, :] for row in range(2)])
+    for row, line in enumerate([front_stats[row : row + 1, :] for row in range(3)] + [ffn_stat[...]]):
+        folded = line[:, :128]
+        for piece in range(1, 8):
+            folded = folded + line[:, 128 * piece : 128 * (piece + 1)]
+        small_out[64 + row : 65 + row, :] = folded
+    mask = valid_rows(sq, length_ref[0], rows)
+    count = jnp.sum(jnp.broadcast_to(mask, (rows, 128)), axis=0, keepdims=True)
+    small_out[68:69, :] = count * (3.0 / 128.0)
+    small_out[69:80, :] = jnp.zeros((11, 128), WIDE)
     near_sum(0)
     near_sum(1)
-    turn(6)
     turn(7)
     loads[2].wait()
     back_to(d_context, d_attended, w_out)
@@ -787,13 +851,23 @@
 
     turn(13)
     tiles(width // 256, 256, query_body)
+    bucket = lax.broadcasted_iota(jnp.int32, (128, full), 0)
+    ones = jnp.ones((8, full), LOW)
+    below = (bucket_row[...] < bucket).astype(WIDE).astype(LOW)
+    upto = (bucket_row[...] <= bucket).astype(WIDE).astype(LOW)
+    first, after = dot(ones, below, NT)[0:1], dot(ones, upto, NT)[0:1]
+    lane = lax.broadcasted_iota(jnp.int32, (2 * rows, 128), 0)
     table = jnp.zeros((HEADS, 128), WIDE)
     for block in range(blocks + 1):
+        reach = ((sq - block) * rows + rows - 1 - lane).astype(WIDE)
+        if block == blocks:
+            reach = jnp.zeros((2 * rows, 128), WIDE)
+        window_hot = ((reach >= first) & (reach < after)).astype(WIDE).astype(LOW)
         rest = bias_sums[:, block, :]
         for _ in range(3):
             part = rest.astype(LOW)
             rest = rest - part.astype(WIDE)
-            table = table + dot(part, window_hot[block])
+            table = table + dot(part, window_hot)
     small_out[48:64, :] = table
     small_copy(0).start()
     d_key[:rows, :] = far_sum(2)
@@ -823,12 +897,13 @@
     drain()
 
 
-def rear(acts, hbm_acts, sides, weights, cross_probs, probs, units, dp_size):
+def rear(acts, hbm_acts, sides, weights, ffn_weights, cross_probs, probs, units, dp_size):
     tokens, width = acts[0].shape
     full = sides[0].shape[0]
     rows = tokens // 3
     shape = jax.ShapeDtypeStruct
     vmem = pl.BlockSpec(memory_space=pltpu.VMEM)
+    smem = pl.BlockSpec(memory_space=pltpu.SMEM)
     hbm = pl.BlockSpec(memory_space=pl.ANY)
     sem = pltpu.SemaphoreType.DMA
     blocks = full // rows
@@ -843,7 +918,7 @@
         ]
         + [shape((chunk, COLS), WIDE)] * 8
         + [shape((chunk, 4 * COLS), WIDE), shape((4 * chunk, COLS), WIDE)],
-        in_specs=[vmem] * len(acts) + [hbm] * (len(hbm_acts) + 14),
+        in_specs=[vmem] * (len(acts) - 1) + [smem] + [hbm] * (len(hbm_acts) + 16),
         out_specs=[vmem] * 13,
         scratch_shapes=[
             pltpu.VMEM((tokens, width), LOW),
@@ -867,7 +942,9 @@
             pltpu.VMEM((4, 2, rows, width), LOW),
             pltpu.VMEM((4, rows, width), LOW),
             pltpu.VMEM((2, full, width), LOW),
-            sem((18,)),
+            pltpu.VMEM((tokens, width), LOW),
+            sem((8,)),
+            sem((19,)),
             sem((2,)),
             sem((4,)),
             sem((4,)),
@@ -880,7 +957,43 @@
         compiler_params=pltpu.CompilerParams(
             collective_id=2, has_side_effects=True, vmem_limit_bytes=63 << 20
         ),
-    )(*acts, *hbm_acts, *sides, *weights, cross_probs, probs)
+    )(*acts, *hbm_acts, *sides, *weights, *ffn_weights, cross_probs, probs)
+
+
+def finish_kernel(num, *refs):
+    ins, sums = refs[:num], refs[num]
+    outs, lines, table, rms, sems = refs[num + 1 : 2 * num + 1], refs[-9:-3], *refs[-3:]
+    copies = [
+        pltpu.make_async_copy(src, dst, sems.at[index])
+        for index, (src, dst) in enumerate(zip(ins, outs))
+    ]
+    for copy in copies:
+        copy.start()
+    for row, line in enumerate(lines):
+        line[...] = sums[8 * row : 8 * row + 8, :]
+    wide = jnp.concatenate([sums[48:64, :], jnp.zeros((112, 128), WIDE)], axis=0)
+    table[...] = jnp.transpose(wide)[:NBUCKET, :HEADS]
+    totals = jnp.sum(sums[64:72, :], axis=1, keepdims=True)
+    rms[...] = jnp.broadcast_to(jnp.sqrt(totals / (totals[4:5] * 1024.0)), (8, 128))
+    for copy in copies:
+        copy.wait()
+
+
+def finish(arrays, sums):
+    shape = jax.ShapeDtypeStruct
+    vmem = pl.BlockSpec(memory_space=pltpu.VMEM)
+    hbm = pl.BlockSpec(memory_space=pl.ANY)
+    num = len(arrays)
+    return pl.pallas_call(
+        functools.partial(finish_kernel, num),
+        out_shape=[shape(array.shape, array.dtype) for array in arrays]
+        + [shape((8, 128), WIDE)] * 6
+        + [shape((NBUCKET, HEADS), WIDE), shape((8, 128), WIDE)],
+        in_specs=[hbm] * num + [vmem],
+        out_specs=[hbm] * num + [vmem] * 8,
+        scratch_shapes=[pltpu.SemaphoreType.DMA((num,))],
+        compiler_params=pltpu.CompilerParams(vmem_limit_bytes=8 << 20),
+    )(*arrays, sums)
 
 
 MESH_ID = pl.DeviceIdType.MESH
@@ -1249,14 +1362,9 @@
 ):
     num_rows, num_streams, local_len, model_width = stream.shape
     full_len = local_len * lax.axis_size("seq")
-    sq = lax.axis_index("seq")
     dp_size = lax.axis_size("dp")
     chunk = model_width // dp_size
-    bucket_ids = jnp.arange(NBUCKET, dtype=jnp.int32)
-    exact = lax.Precision.HIGHEST
-    table_hot = (bucket_table[:, None] == bucket_ids[None, :]).astype(jnp.float32)
-    by_distance = jnp.einsum("db,bh->hd", table_hot, position_bias, precision=exact)
-    bias_table = jnp.concatenate([jnp.zeros_like(by_distance), by_distance], axis=1)[:, None, :]
+    bucket_row = bucket_table.reshape(1, full_len)
     flat_rows = stream.reshape(-1, model_width)
     source_rows = encoded.reshape(-1, model_width)
     flat_cotangent = cotangent.reshape(-1, model_width)
@@ -1268,37 +1376,22 @@
         stream.reshape(num_streams, local_len, model_width),
         source_rows,
         lengths,
-        bias_table,
+        bucket_row,
+        position_bias,
         (line(gain_one), line(shift_one), line(gain_two), line(shift_two)),
         (w_query, w_key, w_value, w_out, c_query, c_key, c_value, c_out),
     )
     query, own_key, own_value, main_key, main_value, context_low, unit_one, first_norm = fronts[:8]
     cross_query, cross_key, cross_value, cross_low, unit_two, second_norm = fronts[8:14]
     scales, own_probs, front_stats, probs, cross_probs = fronts[14:]
-    layer_output, activated, d_ffn_out, d_inner, d_resid_two, d_crossed, mid_grads, ffn_stat = middle(
+    layer_output, activated, d_ffn_out, slope, d_resid_three, mid_grads, ffn_stat = middle(
         second_norm,
-        unit_two,
-        scales,
         flat_cotangent,
         lengths,
-        (line(gain_two), line(gain_three), line(shift_three)),
+        (line(gain_three), line(shift_three)),
         w_in,
         w_back,
     )
-    blocks = full_len // local_len
-    place = jnp.arange(2 * local_len, dtype=jnp.int32)
-    reach = (sq - jnp.arange(blocks, dtype=jnp.int32))[:, None] * local_len + (
-        local_len - 1 - place[None, :]
-    )
-    reach = jnp.concatenate([reach, jnp.zeros((1, 2 * local_len), jnp.int32)])
-    lane_ids = jnp.arange(128, dtype=jnp.int32)
-    first_of = jnp.sum((bucket_table[:, None] < lane_ids[None, :]).astype(jnp.int32), axis=0)
-    next_of = jnp.sum((bucket_table[:, None] <= lane_ids[None, :]).astype(jnp.int32), axis=0)
-    window_hot = (reach[..., None] >= first_of) & (reach[..., None] < next_of)
-    position = sq * local_len + jnp.arange(local_len)
-    count = num_streams * jnp.sum((position < lengths[0]).astype(jnp.float32))
-    mid_stats = jnp.concatenate([front_stats, ffn_stat]).reshape(4, -1, 128).sum(axis=1)
-    mid_stats = jnp.concatenate([mid_stats, jnp.full((4, 128), count / 128)])
     units = []
     tokens = num_streams * local_len
     spread = activated
@@ -1310,13 +1403,13 @@
             units.append((3, 0, "back", part, 0, tokens))
         else:
             units.append((3, 0, "parted", part, part * model_width, tokens))
+    for part in range(4):
         units.append((1, 2, "in", part, 0, tokens))
     units += [(4, 5, "", 7, 0, tokens), (6, 7, "", 4, 0, tokens), (3, 8, "", 3, 0, tokens)]
     units += [(3, 9, "", 5, 2 * model_width, local_len), (3, 10, "", 6, 2 * model_width, local_len)]
     units += [(3, 11 + part, "", part, model_width, tokens) for part in range(3)]
     rears = rear(
         (
-            d_crossed,
             cross_query,
             unit_one,
             query,
@@ -1329,22 +1422,26 @@
             cross_low,
             first_norm,
             mid_grads,
-            mid_stats,
-            window_hot.astype(jnp.bfloat16),
+            ffn_stat,
+            front_stats,
             scales,
+            line(gain_two),
+            bucket_row,
+            lengths,
         ),
-        (d_inner, spread, context_low, flat_rows, source_rows, d_resid_two),
+        (slope, spread, context_low, flat_rows, source_rows, d_resid_three, unit_two),
         (cross_key, cross_value, main_key, main_value),
         (c_out, c_query, w_out, w_query, w_key, w_value, c_key, c_value),
+        (w_back, w_in),
         cross_probs,
         probs,
         tuple(units),
         dp_size,
     )
-    encoded_grad, stream_grad, sums = rears[:3]
-    shares = rears[3:]
-    wide_sums = sums[:48].reshape(6, model_width)
-    rms = jnp.sqrt(jnp.sum(sums[64:68], axis=1) / (jnp.sum(sums[68]) * model_width))
+    ends = finish(list(rears[:2]) + list(rears[3:]), rears[2])
+    encoded_grad, stream_grad = ends[:2]
+    shares, lines, table_grad = ends[2:12], ends[12:18], ends[18]
+    rms = ends[19][:4, 0]
     return (
         layer_output.reshape(stream.shape),
         stream_grad.reshape(stream.shape),
@@ -1359,13 +1456,13 @@
         shares[7],
         shares[8],
         shares[9],
-        wide_sums[0],
-        wide_sums[1],
-        wide_sums[2],
-        wide_sums[3],
-        wide_sums[4],
-        wide_sums[5],
-        jnp.transpose(sums[48:64, :NBUCKET]),
+        lines[0].reshape(model_width),
+        lines[1].reshape(model_width),
+        lines[2].reshape(model_width),
+        lines[3].reshape(model_width),
+        lines[4].reshape(model_width),
+        lines[5].reshape(model_width),
+        table_grad,
         rms,
     )
 

time: 284 us -> 260 us (0.915)
  Pallas kernels: 255 us -> 240 us
  other arithmetic: 5.92 us -> 0 us
    pallas_call x1 -> x2, Pallas kernels: 27.4 us -> 19.6 us  [the longest x1 17.2 us: middle(): pl.pallas_call(middle_kernel, out_shape=outs + [shape((2, width), WIDE),...]
    pallas_call x1, Pallas kernels: 54.7 us -> 47.2 us  [front(): pl.pallas_call(front_kernel, out_shape=outs, in_specs=[vmem, vmem, smem]...]
    reduce_sum x5 -> x0, other arithmetic: 3.64 us -> none  [the longest x1 1.4 us: per_device(): jnp.sum(sums[68]) * model_width]
    unnamed x38 -> x28, local copies, waits for them, and re-layouts: 10.7 us -> 14.2 us
where the time goes in v6:
time: 260 us; the launch traced here: 256 us
  Pallas kernels  240 us (92%)
  local copies, waits for them, and re-layouts  14.8 us (6%)
    pallas_call x1, Pallas kernels, rear(): pl.pallas_call(functools.partial(rear_kernel, units, dp_size), out_shape=...  173 us
    pallas_call x1, Pallas kernels, front(): pl.pallas_call(front_kernel, out_shape=outs, in_specs=[vmem, vmem, smem]...  47.2 us
    pallas_call x1, Pallas kernels, middle(): pl.pallas_call(middle_kernel, out_shape=outs + [shape((2, width), WIDE),...  17.2 us
    unnamed x28, local copies, waits for them, and re-layouts  14.2 us

profile of v6, /device:TPU:0, one launch (start us, length us, event | category | flops | bytes accessed | tf_op | source)
XLA Modules:
  0.0 256.3 jit_solution(8899751808197443372)
XLA Ops:
  1.3 1.4 copy.45.refs_4_
  2.7 47.2 %shard_map.373 = (bf16[384,1024]{1,0:T(8,128)(2,1)}, bf16[256,1024]{1,0:T(8,128)(2,1)}, bf16[256,1024]{1,0:T(8,128)(2,1)}, bf16[512,1024]{1,0:T(8,128)(2,1)}, bf...) custom-call(bf16[3,128,1024]{2,1,0:T(8,128)(2,1)} %bitcast.20, ...), custom_call_target="tpu_custom_call" | custom-call | tf_op jit(solution)/shard_map/pallas_call | solution.py:383
  49.9 17.2 %shard_map.374 = (bf16[384,1024]{1,0:T(8,128)(2,1)}, bf16[384,4096]{1,0:T(8,128)(2,1)}, bf16[384,1024]{1,0:T(8,128)(2,1)}, bf16[384,4096]{1,0:T(8,128)(2,1)}, f3...) custom-call(bf16[384,1024]{1,0:T(8,128)(2,1)} %get-tuple-element.80.refs_0_.refs_8_, ...), custom_call_target="tpu_custom_call" | custom-call | tf_op jit(solution)/shard_map/pallas_call | solution.py:497
  67.1 173.1 %shard_map.375 = (bf16[128,1024]{1,0:T(8,128)(2,1)}, bf16[384,1024]{1,0:T(8,128)(2,1)}, f32[80,128]{1,0:T(8,128)}, f32[128,256]{1,0:T(8,128)}, f32[128,256]{1,0:...) custom-call(bf16[384,1024]{1,0:T(8,128)(2,1)} %get-tuple-element.82., ...), custom_call_target="tpu_custom_call" | custom-call | tf_op jit(solution)/shard_map/pallas_call | solution.py:912
  240.1 0.0 copy-start
  240.1 1.1 copy-done
  241.3 0.0 copy-start.1
  241.3 1.0 copy-done.1
  242.3 0.0 copy-start.2
  242.3 1.0 copy-done.2
  243.4 0.0 copy-start.3
  243.4 0.9 copy-done.3
  244.3 0.0 copy-start.4
  244.3 0.9 copy-done.4
  245.2 0.0 copy-start.5
  245.2 0.9 copy-done.5
  246.1 0.0 copy-start.6
  246.1 0.9 copy-done.6
  247.0 0.0 copy-start.7
  247.0 0.9 copy-done.7
  247.9 0.0 copy-start.8
  247.9 0.9 copy-done.8
  248.8 0.0 copy-start.9
  248.8 0.9 copy-done.9
  249.7 0.0 copy-start.10
  249.7 0.9 copy-done.10
  250.6 0.0 copy-start.11
  250.6 0.9 copy-done.11
  251.5 0.0 copy-start.12
  251.5 0.8 copy-done.12
  252.3 2.4 shard_map.376
  254.7 0.7 copy.46
  255.4 0.6 slice_reduce_fusion
Async XLA Ops:
  240.1 1.1 copy-start
  241.3 1.0 copy-start.1
  242.3 1.0 copy-start.2
  243.4 0.9 copy-start.3
  244.3 0.9 copy-start.4
  245.2 0.9 copy-start.5
  246.1 0.9 copy-start.6
  247.0 0.9 copy-start.7
  247.9 0.9 copy-start.8
  248.8 0.9 copy-start.9
  249.7 0.9 copy-start.10
  250.6 0.9 copy-start.11
  251.5 0.8 copy-start.12

commit v7 on v6

--- a/solution.py
+++ b/solution.py
@@ -161,7 +161,7 @@
     for _ in range(3):
         part = rest.astype(LOW)
         rest = rest - part.astype(WIDE)
-        by_distance = by_distance + dot(part, table_hot, (((0,), (0,)), ((), ())))
+        by_distance = by_distance + dot(part, table_hot)
     bias_table[...] = jnp.zeros_like(bias_table)
     for head in range(HEADS):
         bias_table[head, :, full:] = by_distance[head : head + 1]
@@ -606,6 +606,7 @@
     greet(reduce_peers(dp_size))
     early[0].wait()
     turn(0)
+    turn(1)
     early[1].wait()
     early[2].wait()
     ffn_steps = hbm_ffn[0].shape[0] // width
@@ -619,7 +620,8 @@
         for index in (2 * step + 3, 2 * step + 4):
             if index < 2 * ffn_steps:
                 ffn_load(index).start()
-        turn(1 + step)
+        if step != 2:
+            turn((2, 3, None, 4)[step])
     for index in range(3):
         loads[index].start()
     early[3].wait()
@@ -971,8 +973,7 @@
         copy.start()
     for row, line in enumerate(lines):
         line[...] = sums[8 * row : 8 * row + 8, :]
-    wide = jnp.concatenate([sums[48:64, :], jnp.zeros((112, 128), WIDE)], axis=0)
-    table[...] = jnp.transpose(wide)[:NBUCKET, :HEADS]
+    table[...] = sums[48:64, :NBUCKET]
     totals = jnp.sum(sums[64:72, :], axis=1, keepdims=True)
     rms[...] = jnp.broadcast_to(jnp.sqrt(totals / (totals[4:5] * 1024.0)), (8, 128))
     for copy in copies:
@@ -988,11 +989,11 @@
         functools.partial(finish_kernel, num),
         out_shape=[shape(array.shape, array.dtype) for array in arrays]
         + [shape((8, 128), WIDE)] * 6
-        + [shape((NBUCKET, HEADS), WIDE), shape((8, 128), WIDE)],
+        + [shape((HEADS, NBUCKET), WIDE), shape((8, 128), WIDE)],
         in_specs=[hbm] * num + [vmem],
         out_specs=[hbm] * num + [vmem] * 8,
         scratch_shapes=[pltpu.SemaphoreType.DMA((num,))],
-        compiler_params=pltpu.CompilerParams(vmem_limit_bytes=8 << 20),
+        compiler_params=pltpu.CompilerParams(vmem_limit_bytes=60 << 20),
     )(*arrays, sums)
 
 
@@ -1377,7 +1378,7 @@
         source_rows,
         lengths,
         bucket_row,
-        position_bias,
+        jnp.transpose(position_bias),
         (line(gain_one), line(shift_one), line(gain_two), line(shift_two)),
         (w_query, w_key, w_value, w_out, c_query, c_key, c_value, c_out),
     )
@@ -1462,7 +1463,7 @@
         lines[3].reshape(model_width),
         lines[4].reshape(model_width),
         lines[5].reshape(model_width),
-        table_grad,
+        jnp.transpose(table_grad),
         rms,
     )
 

time: 260 us -> 340 us (1.31)
  Pallas kernels: 240 us -> 334 us
  local copies, waits for them, and re-layouts: 14.8 us -> 1.31 us
    pallas_call x1, Pallas kernels: 2.37 us -> 98 us  [finish(): pl.pallas_call(functools.partial(finish_kernel, num), out_shape=[shape(ar...]
    unnamed x28 -> x0, local copies, waits for them, and re-layouts: 14.2 us -> none
where the time goes in v7:
time: 340 us; the launch traced here: 337 us
  Pallas kernels  334 us (98%)
    pallas_call x1, Pallas kernels, rear(): pl.pallas_call(functools.partial(rear_kernel, units, dp_size), out_shape=...  171 us
    pallas_call x1, Pallas kernels, finish(): pl.pallas_call(functools.partial(finish_kernel, num), out_shape=[shape(ar...  98 us
    pallas_call x1, Pallas kernels, front(): pl.pallas_call(front_kernel, out_shape=outs, in_specs=[vmem, vmem, smem]...  47.2 us
    pallas_call x1, Pallas kernels, middle(): pl.pallas_call(middle_kernel, out_shape=outs + [shape((2, width), WIDE),...  17.2 us

profile of v7, /device:TPU:0, one launch (start us, length us, event | category | flops | bytes accessed | tf_op | source)
XLA Modules:
  0.0 336.8 jit_solution(278972115076431258)
XLA Ops:
  1.3 47.2 %shard_map.373 = (bf16[384,1024]{1,0:T(8,128)(2,1)}, bf16[256,1024]{1,0:T(8,128)(2,1)}, bf16[256,1024]{1,0:T(8,128)(2,1)}, bf16[512,1024]{1,0:T(8,128)(2,1)}, bf...) custom-call(bf16[3,128,1024]{2,1,0:T(8,128)(2,1)} %bitcast.22, ...), custom_call_target="tpu_custom_call" | custom-call | tf_op jit(solution)/shard_map/pallas_call | solution.py:383
  48.5 17.2 %shard_map.374 = (bf16[384,1024]{1,0:T(8,128)(2,1)}, bf16[384,4096]{1,0:T(8,128)(2,1)}, bf16[384,1024]{1,0:T(8,128)(2,1)}, bf16[384,4096]{1,0:T(8,128)(2,1)}, f3...) custom-call(bf16[384,1024]{1,0:T(8,128)(2,1)} %get-tuple-element.80.refs_0_.refs_8_, ...), custom_call_target="tpu_custom_call" | custom-call | tf_op jit(solution)/shard_map/pallas_call | solution.py:497
  65.7 171.4 %shard_map.375 = (bf16[128,1024]{1,0:T(8,128)(2,1)}, bf16[384,1024]{1,0:T(8,128)(2,1)}, f32[80,128]{1,0:T(8,128)}, f32[128,256]{1,0:T(8,128)}, f32[128,256]{1,0:...) custom-call(bf16[384,1024]{1,0:T(8,128)(2,1)} %get-tuple-element.82., ...), custom_call_target="tpu_custom_call" | custom-call | tf_op jit(solution)/shard_map/pallas_call | solution.py:914
  237.1 98.0 %shard_map.376 = (bf16[128,1024]{1,0:T(8,128)(2,1)}, bf16[384,1024]{1,0:T(8,128)(2,1)}, f32[128,256]{1,0:T(8,128)}, f32[128,256]{1,0:T(8,128)}, f32[128,256]{1,0...) custom-call(bf16[128,1024]{1,0:T(8,128)(2,1)} %get-tuple-element.106, ...), custom_call_target="tpu_custom_call" | custom-call | tf_op jit(solution)/shard_map/pallas_call | solution.py:988
  335.1 1.3 slice_reduce_fusion

commit v8 on v7

--- a/solution.py
+++ b/solution.py
@@ -964,20 +964,25 @@
 
 def finish_kernel(num, *refs):
     ins, sums = refs[:num], refs[num]
-    outs, lines, table, rms, sems = refs[num + 1 : 2 * num + 1], refs[-9:-3], *refs[-3:]
-    copies = [
-        pltpu.make_async_copy(src, dst, sems.at[index])
-        for index, (src, dst) in enumerate(zip(ins, outs))
-    ]
-    for copy in copies:
-        copy.start()
+    outs, lines = refs[num + 1 : 2 * num + 1], refs[2 * num + 1 : 2 * num + 7]
+    table, rms = refs[2 * num + 7 : 2 * num + 9]
+    held, (in_sem, out_sem) = refs[2 * num + 9 : -2], refs[-2:]
+    loads, stores = [], []
+    for index, (src, mid, dst) in enumerate(zip(ins, held, outs)):
+        loads.append(pltpu.make_async_copy(src, mid, in_sem.at[index]))
+        stores.append(pltpu.make_async_copy(mid, dst, out_sem.at[index]))
+    for load in loads:
+        load.start()
     for row, line in enumerate(lines):
         line[...] = sums[8 * row : 8 * row + 8, :]
     table[...] = sums[48:64, :NBUCKET]
     totals = jnp.sum(sums[64:72, :], axis=1, keepdims=True)
     rms[...] = jnp.broadcast_to(jnp.sqrt(totals / (totals[4:5] * 1024.0)), (8, 128))
-    for copy in copies:
-        copy.wait()
+    for load, store in zip(loads, stores):
+        load.wait()
+        store.start()
+    for store in stores:
+        store.wait()
 
 
 def finish(arrays, sums):
@@ -992,7 +997,8 @@
         + [shape((HEADS, NBUCKET), WIDE), shape((8, 128), WIDE)],
         in_specs=[hbm] * num + [vmem],
         out_specs=[hbm] * num + [vmem] * 8,
-        scratch_shapes=[pltpu.SemaphoreType.DMA((num,))],
+        scratch_shapes=[pltpu.VMEM(array.shape, array.dtype) for array in arrays]
+        + [pltpu.SemaphoreType.DMA((num,))] * 2,
         compiler_params=pltpu.CompilerParams(vmem_limit_bytes=60 << 20),
     )(*arrays, sums)
 

time: 340 us -> 247 us (0.73)
  Pallas kernels: 334 us -> 240 us
    pallas_call x1, Pallas kernels: 98 us -> 4.45 us  [finish(): pl.pallas_call(functools.partial(finish_kernel, num), out_shape=[shape(ar...]
where the time goes in v8:
time: 247 us; the launch traced here: 243 us
  Pallas kernels  240 us (97%)
    pallas_call x1, Pallas kernels, rear(): pl.pallas_call(functools.partial(rear_kernel, units, dp_size), out_shape=...  171 us
    pallas_call x1, Pallas kernels, front(): pl.pallas_call(front_kernel, out_shape=outs, in_specs=[vmem, vmem, smem]...  47.2 us
    pallas_call x1, Pallas kernels, middle(): pl.pallas_call(middle_kernel, out_shape=outs + [shape((2, width), WIDE),...  17.2 us

profile of v8, /device:TPU:0, one launch (start us, length us, event | category | flops | bytes accessed | tf_op | source)
XLA Modules:
  0.0 243.3 jit_solution(11436961332384087852)
XLA Ops:
  1.3 47.2 %shard_map.373 = (bf16[384,1024]{1,0:T(8,128)(2,1)}, bf16[256,1024]{1,0:T(8,128)(2,1)}, bf16[256,1024]{1,0:T(8,128)(2,1)}, bf16[512,1024]{1,0:T(8,128)(2,1)}, bf...) custom-call(bf16[3,128,1024]{2,1,0:T(8,128)(2,1)} %bitcast.22, ...), custom_call_target="tpu_custom_call" | custom-call | tf_op jit(solution)/shard_map/pallas_call | solution.py:383
  48.5 17.2 %shard_map.374 = (bf16[384,1024]{1,0:T(8,128)(2,1)}, bf16[384,4096]{1,0:T(8,128)(2,1)}, bf16[384,1024]{1,0:T(8,128)(2,1)}, bf16[384,4096]{1,0:T(8,128)(2,1)}, f3...) custom-call(bf16[384,1024]{1,0:T(8,128)(2,1)} %get-tuple-element.80.refs_0_.refs_8_, ...), custom_call_target="tpu_custom_call" | custom-call | tf_op jit(solution)/shard_map/pallas_call | solution.py:497
  65.7 171.4 %shard_map.375 = (bf16[128,1024]{1,0:T(8,128)(2,1)}, bf16[384,1024]{1,0:T(8,128)(2,1)}, f32[80,128]{1,0:T(8,128)}, f32[128,256]{1,0:T(8,128)}, f32[128,256]{1,0:...) custom-call(bf16[384,1024]{1,0:T(8,128)(2,1)} %get-tuple-element.82., ...), custom_call_target="tpu_custom_call" | custom-call | tf_op jit(solution)/shard_map/pallas_call | solution.py:914
  237.1 4.5 %shard_map.376 = (bf16[128,1024]{1,0:T(8,128)(2,1)}, bf16[384,1024]{1,0:T(8,128)(2,1)}, f32[128,256]{1,0:T(8,128)}, f32[128,256]{1,0:T(8,128)}, f32[128,256]{1,0...) custom-call(bf16[128,1024]{1,0:T(8,128)(2,1)} %get-tuple-element.106, ...), custom_call_target="tpu_custom_call" | custom-call | tf_op jit(solution)/shard_map/pallas_call | solution.py:993
  241.6 1.3 slice_reduce_fusion

commit v9 on v8

--- a/solution.py
+++ b/solution.py
@@ -12,6 +12,7 @@
 NBUCKET = 32
 COLS = 256
 SLOTS = 2
+LATER = (0, 1, 2, 3, 4, 9, 10)
 RING = 6
 RING_ONE = 5
 COLORS = "yxyxzxyxyxzxyxzxyxyxzxyxzxyxyxyx"
@@ -511,6 +512,12 @@
 
 
 def rear_kernel(units, dp_size, *refs):
+    refs, act_held, act_sem = list(refs[: -len(LATER) - 1]), refs[-len(LATER) - 1 : -1], refs[-1]
+    act_loads = []
+    for index, (place, held_ref) in enumerate(zip(LATER, act_held)):
+        act_loads.append(pltpu.make_async_copy(refs[place], held_ref, act_sem.at[index]))
+        refs[place] = held_ref
+    refs = tuple(refs)
     cross_query, unit_one, query, own_key, own_value, own_probs, gain_one = refs[:7]
     refs = (None,) + refs
     d_ffn, second_norm, cross_context, first_norm, mid_grads, ffn_stat, front_stats = refs[8:15]
@@ -603,6 +610,8 @@
     fetch(0, cross_probs, 0).start()
     load_side(0).start()
     load_side(1).start()
+    for load in act_loads:
+        load.start()
     greet(reduce_peers(dp_size))
     early[0].wait()
     turn(0)
@@ -710,6 +719,8 @@
 
     load_side(0).wait()
     load_side(1).wait()
+    for load in act_loads:
+        load.wait()
     lax.fori_loop(0, pairs // 2, cross_pair, 0)
     turn(5)
     lax.fori_loop(pairs // 2, pairs, cross_pair, 0)
@@ -920,7 +931,7 @@
         ]
         + [shape((chunk, COLS), WIDE)] * 8
         + [shape((chunk, 4 * COLS), WIDE), shape((4 * chunk, COLS), WIDE)],
-        in_specs=[vmem] * (len(acts) - 1) + [smem] + [hbm] * (len(hbm_acts) + 16),
+        in_specs=[hbm if place in LATER else vmem for place in range(len(acts) - 1)] + [smem] + [hbm] * (len(hbm_acts) + 16),
         out_specs=[vmem] * 13,
         scratch_shapes=[
             pltpu.VMEM((tokens, width), LOW),
@@ -955,7 +966,9 @@
             sem((steps,)),
             sem((steps,)),
         ]
-        + reduce_buffers(COLORS, dp_size),
+        + reduce_buffers(COLORS, dp_size)
+        + [pltpu.VMEM(acts[place].shape, LOW) for place in LATER]
+        + [sem((len(LATER),))],
         compiler_params=pltpu.CompilerParams(
             collective_id=2, has_side_effects=True, vmem_limit_bytes=63 << 20
         ),
@@ -1285,7 +1298,7 @@
             zx_copy(item).wait_send()
 
     def turn(index):
-        for stage, lag in ((products, 0), (core_sum, 1)):
+        for stage, lag in ((core_sum, 1), (products, 0)):
             if 0 <= index - lag < count:
                 stage(index - lag)
         for stage, lag in ((one_sum, 3), (two_sum, 5), (last_sum, 7), (z_end, 9)):

time: 247 us -> 246 us (level)
  no operation moved by 1% of the time
where the time goes in v9:
time: 246 us; the launch traced here: 243 us
  Pallas kernels  239 us (97%)
    pallas_call x1, Pallas kernels, rear(): pl.pallas_call(functools.partial(rear_kernel, units, dp_size), out_shape=...  171 us
    pallas_call x1, Pallas kernels, front(): pl.pallas_call(front_kernel, out_shape=outs, in_specs=[vmem, vmem, smem]...  47.2 us
    pallas_call x1, Pallas kernels, middle(): pl.pallas_call(middle_kernel, out_shape=outs + [shape((2, width), WIDE),...  17.2 us

profile of v9, /device:TPU:0, one launch (start us, length us, event | category | flops | bytes accessed | tf_op | source)
XLA Modules:
  0.0 242.5 jit_solution(13926859193377026789)
XLA Ops:
  1.3 47.2 %shard_map.373 = (bf16[384,1024]{1,0:T(8,128)(2,1)}, bf16[256,1024]{1,0:T(8,128)(2,1)}, bf16[256,1024]{1,0:T(8,128)(2,1)}, bf16[512,1024]{1,0:T(8,128)(2,1)}, bf...) custom-call(bf16[3,128,1024]{2,1,0:T(8,128)(2,1)} %bitcast.22, ...), custom_call_target="tpu_custom_call" | custom-call | tf_op jit(solution)/shard_map/pallas_call | solution.py:384
  48.5 17.2 %shard_map.374 = (bf16[384,1024]{1,0:T(8,128)(2,1)}, bf16[384,4096]{1,0:T(8,128)(2,1)}, bf16[384,1024]{1,0:T(8,128)(2,1)}, bf16[384,4096]{1,0:T(8,128)(2,1)}, f3...) custom-call(bf16[384,1024]{1,0:T(8,128)(2,1)} %get-tuple-element.80.refs_0_.refs_8_, ...), custom_call_target="tpu_custom_call" | custom-call | tf_op jit(solution)/shard_map/pallas_call | solution.py:498
  65.7 170.6 %shard_map.375 = (bf16[128,1024]{1,0:T(8,128)(2,1)}, bf16[384,1024]{1,0:T(8,128)(2,1)}, f32[80,128]{1,0:T(8,128)}, f32[128,256]{1,0:T(8,128)}, f32[128,256]{1,0:...) custom-call(bf16[384,1024]{1,0:T(8,128)(2,1)} %get-tuple-element.82., ...), custom_call_target="tpu_custom_call" | custom-call | tf_op jit(solution)/shard_map/pallas_call | solution.py:925
  236.3 4.5 %shard_map.376 = (bf16[128,1024]{1,0:T(8,128)(2,1)}, bf16[384,1024]{1,0:T(8,128)(2,1)}, f32[128,256]{1,0:T(8,128)}, f32[128,256]{1,0:T(8,128)}, f32[128,256]{1,0...) custom-call(bf16[128,1024]{1,0:T(8,128)(2,1)} %get-tuple-element.106, ...), custom_call_target="tpu_custom_call" | custom-call | tf_op jit(solution)/shard_map/pallas_call | solution.py:1006
  240.8 1.3 slice_reduce_fusion
